TPU v7x, 32 devices: a whole 2x2x4 slice. The times are simulated.
32 devices in a mesh: grp: 8 (over y, x, core), blk: 4 (over z).
Axes of the slice: x: 2, y: 2, z: 4, core: 2. Of those that a mesh axis runs over, the one named last changes fastest.
Arguments:
- dual_populace: float32 [19, 64, 64, 128], P(None, 'grp', 'blk'), may hold values from -6 to 6
- forward_motion_vector: float32 [3, 64, 64, 128], P(None, 'grp', 'blk'), may hold values from -0.4 to 0.4
- forward_heat_level: float32 [64, 64, 128], P('grp', 'blk'), may hold values from 0.5 to 1.5
- objective_heat_gradient: float32 [64, 64, 128], P('grp', 'blk'), may hold values from -6 to 6
- liquid_indicator: int32 [64, 64, 128], P('grp', 'blk'), may hold values 0 or 1
- filter_span_group: int32 [64, 64, 128], P('grp', 'blk'), may hold values from 0 to 3
Outputs:
- adjoint_out: float32 [19, 64, 64, 128], P(None, 'grp', 'blk')
- filtered: float32 [64, 64, 128], P('grp', 'blk')
All inputs are finite; a program needn't handle non-finite values. No bound on the sum of `liquid_indicator` on one device may be relied on, other than what follows from the above.
Results may differ from a plain program's by a relative error of at most 0.000031.
Values sent between devices are 32-bit elements; how exact they have to be, the bound alone decides.
No kernel may reach another device: no remote copies, remote signals or barrier semaphores. Data moves between devices by JAX's collectives and lax.ppermute only.
A program may use at most 64 MiB of HBM per device.

v0:
```python
import jax
import jax.numpy as jnp
from jax import lax
from jax.sharding import PartitionSpec as P

STEPS = 3
SWEEPS = 8


VELOCITIES = (
    (0, 0, 0),
    (1, 0, 0),
    (-1, 0, 0),
    (0, 1, 0),
    (0, -1, 0),
    (0, 0, 1),
    (0, 0, -1),
    (1, 1, 0),
    (-1, -1, 0),
    (1, -1, 0),
    (-1, 1, 0),
    (1, 0, 1),
    (-1, 0, -1),
    (1, 0, -1),
    (-1, 0, 1),
    (0, 1, 1),
    (0, -1, -1),
    (0, 1, -1),
    (0, -1, 1),
)
WEIGHTS = (1.0 / 3.0,) + (1.0 / 18.0,) * 6 + (1.0 / 36.0,) * 12


def padded_2(x, sides, width):
    for axis, dim in sides:
        size, length = (lax.axis_size(axis), x.shape[dim])
        up = [(i, (i + 1) % size) for i in range(size - 1)]
        down = [(j, i) for i, j in up]
        last = lax.slice_in_dim(x, length - width, length, axis=dim)
        leading = lax.slice_in_dim(x, 0, width, axis=dim)
        before = lax.ppermute(last, axis, up)
        after = lax.ppermute(leading, axis, down)
        x = jnp.concatenate([before, x, after], axis=dim)
    return x


def collide(pulled, omega, vel_x, vel_y, vel_z, objective_heat_gradient):
    equilib = jnp.zeros_like(omega)
    average = jnp.zeros_like(omega)
    for population in range(19):
        cx, cy, cz = VELOCITIES[population]
        along = cx * vel_x + cy * vel_y + cz * vel_z
        equilib = equilib + WEIGHTS[population] * (1.0 + 3.0 * along) * pulled[population]
        average = average + WEIGHTS[population] * pulled[population]
    posts = [
        pulled[population]
        - omega * (pulled[population] - equilib)
        + WEIGHTS[population] * objective_heat_gradient
        for population in range(19)
    ]
    return (jnp.stack(posts), equilib - average)


def pull_from(extended):
    width_x, width_y, width_z = (extended.shape[1] - 2, extended.shape[2] - 2, extended.shape[3])
    padded = jnp.pad(extended, ((0, 0), (0, 0), (0, 0), (1, 1)))
    pieces = []
    for population in range(19):
        cx, cy, cz = VELOCITIES[population]
        pieces.append(
            padded[
                population,
                1 + cx : 1 + cx + width_x,
                1 + cy : 1 + cy + width_y,
                1 + cz : 1 + cz + width_z,
            ]
        )
    return jnp.stack(pieces)


def on_device(
    dual_populace,
    forward_motion_vector,
    forward_heat_level,
    objective_heat_gradient,
    liquid_indicator,
    filter_span_group,
):
    fluid = liquid_indicator.astype(jnp.float32)
    moving = forward_motion_vector * fluid[None]
    omega = 0.9 + 0.7 * fluid
    state = dual_populace
    gradient_map = jnp.zeros_like(forward_heat_level)
    for number in range(STEPS):
        extended = padded_2(state, (("grp", 1), ("blk", 2)), 1)
        pulled = pull_from(extended)
        state, correction_increment = collide(
            pulled, omega, moving[0], moving[1], moving[2], objective_heat_gradient
        )
        gradient_map = gradient_map + forward_heat_level * correction_increment
    radius_sq = 0.25 * jnp.power(4.0, filter_span_group.astype(jnp.float32))
    smooth = gradient_map
    denom = 1.0 + 6.0 * radius_sq
    for number in range(SWEEPS):
        rimmed = padded_2(smooth, (("grp", 0), ("blk", 1)), 1)
        padded = jnp.pad(rimmed, ((0, 0), (0, 0), (1, 1)))
        beside = padded[2:, 1:-1, 1:-1] + padded[:-2, 1:-1, 1:-1]
        beside = beside + padded[1:-1, 2:, 1:-1] + padded[1:-1, :-2, 1:-1]
        beside = beside + padded[1:-1, 1:-1, 2:] + padded[1:-1, 1:-1, :-2]
        smooth = (gradient_map + radius_sq * beside) / denom
    return (state, smooth)


def solution(mesh):
    in_specs = (
        P(None, "grp", "blk", None),
        P(None, "grp", "blk", None),
        P("grp", "blk", None),
        P("grp", "blk", None),
        P("grp", "blk", None),
        P("grp", "blk", None),
    )
    out_specs = (P(None, "grp", "blk", None), P("grp", "blk", None))
    return jax.shard_map(
        on_device, mesh=mesh, in_specs=in_specs, out_specs=out_specs, check_vma=False
    )
```

profile of v0, /device:TPU:12, one launch (start us, length us, event | category | flops | bytes accessed | tf_op | source)
XLA Modules:
  0.0 198.2 jit_solution(16904007648260212466)
XLA Ops:
  3.6 4.5 %collective-permute-start = (f32[19,1,16,128]{3,2,1,0:T(8,128)S(1)}, f32[19,1,16,128]{3,2,1,0:T(8,128)S(1)}, u32[]{:S(2)}, u32[]{:S(2)}) collective-permute-start(f32[19,1,16,128]{3,2,1,0:T(8,128)S(1)} %get-tuple-element.61), channel_id=1, source_target_pairs={{4,0},{8,4},{12,8},{16,12},{20,16},{24,20},{28,24},{5,1},{9,5},{13... | collective-permute-start | bytes 466952 | tf_op jit(solution)/shard_map/ppermute | solution.py:42
  11.0 3.5 %collective-permute-start.3 = (f32[19,10,1,128]{3,2,1,0:T(1,128)S(1)}, f32[19,10,1,128]{3,2,1,0:T(1,128)S(1)}, u32[]{:S(2)}, u32[]{:S(2)}) collective-permute-start(f32[19,10,1,128]{3,2,1,0:T(1,128)S(1)} %get-tuple-element.55), channel_id=1, source_target_pairs={{0,1},{1,2},{2,3},{4,5},{5,6},{6,7},{8,9},{9,10},{10,11},{12,13},{... | collective-permute-start | bytes 291848 | tf_op jit(solution)/shard_map/ppermute | solution.py:41
  27.1 4.5 %collective-permute-start.4 = (f32[19,1,16,128]{3,2,1,0:T(8,128)S(1)}, f32[19,1,16,128]{3,2,1,0:T(8,128)S(1)}, u32[]{:S(2)}, u32[]{:S(2)}) collective-permute-start(f32[19,1,16,128]{3,2,1,0:T(8,128)S(1)} %get-tuple-element.60), channel_id=1, source_target_pairs={{4,0},{8,4},{12,8},{16,12},{20,16},{24,20},{28,24},{5,1},{9,5},{13... | collective-permute-start | bytes 466952 | tf_op jit(solution)/shard_map/ppermute | solution.py:42
  41.1 3.5 %collective-permute-done.6 = f32[19,10,1,128]{3,2,1,0:T(1,128)S(1)} collective-permute-done((f32[19,10,1,128]{3,2,1,0:T(1,128)S(1)}, f32[19,10,1,128]{3,2,1,0:T(1,128)S(1)}, u32[]{:S(2)}, u32[]{:S(2)}) %collective-permute-start.6) | collective-permute-done | bytes 97312 | tf_op jit(solution)/shard_map/ppermute | solution.py:42
  44.6 4.3 %select_maximum_fusion.4 = f32[19,10,18,130]{3,2,1,0:T(8,128)S(1)} fusion(f32[19,10,1,128]{3,2,1,0:T(1,128)S(1)} %collective-permute-done.6, f32[19,10,1,128]{3,2,1,0:T(1,128)S(1)} %collective-permute-done.7, f32[19,1,16,128]{3,2,1,0:T(8,128)S(1)} %collective-permute-done.4, f32[19,8,16,128]{3,2,1,0:T(8,128)S(1)} %constant_dynamic-update-slice_fusion.3, ...), kind=kLoop, calls=%fused_computation.6 | loop fusion | flops 5335200 | bytes 3529440 | tf_op jit(solution)/shard_map/concatenate | solution.py:43
  52.0 4.5 %collective-permute-start.8 = (f32[19,1,16,128]{3,2,1,0:T(8,128)S(1)}, f32[19,1,16,128]{3,2,1,0:T(8,128)S(1)}, u32[]{:S(2)}, u32[]{:S(2)}) collective-permute-start(f32[19,1,16,128]{3,2,1,0:T(8,128)S(1)} %get-tuple-element.58), channel_id=1, source_target_pairs={{4,0},{8,4},{12,8},{16,12},{20,16},{24,20},{28,24},{5,1},{9,5},{13... | collective-permute-start | bytes 466952 | tf_op jit(solution)/shard_map/ppermute | solution.py:42
  61.4 4.1 %collective-permute-start.10 = (f32[19,10,1,128]{3,2,1,0:T(1,128)S(1)}, f32[19,10,1,128]{3,2,1,0:T(1,128)S(1)}, u32[]{:S(2)}, u32[]{:S(2)}) collective-permute-start(f32[19,10,1,128]{3,2,1,0:T(1,128)S(1)} %get-tuple-element.52), channel_id=1, source_target_pairs={{1,0},{2,1},{3,2},{5,4},{6,5},{7,6},{9,8},{10,9},{11,10},{13,12},{... | collective-permute-start | bytes 291848 | tf_op jit(solution)/shard_map/ppermute | solution.py:42
  68.0 4.3 %select_maximum_fusion = f32[19,10,18,130]{3,2,1,0:T(8,128)S(1)} fusion(f32[19,10,1,128]{3,2,1,0:T(1,128)S(1)} %collective-permute-done.10, f32[19,10,1,128]{3,2,1,0:T(1,128)S(1)} %collective-permute-done.11, f32[19,1,16,128]{3,2,1,0:T(8,128)S(1)} %collective-permute-done.8, f32[19,8,16,128]{3,2,1,0:T(8,128)S(1)} %constant_dynamic-update-slice_fusion.22, ...), kind=kLoop, calls=%fused_computation.2 | loop fusion | flops 5335200 | bytes 3529440 | tf_op jit(solution)/shard_map/concatenate | solution.py:43
  75.0 4.5 %collective-permute-start.12 = (f32[1,16,128]{2,1,0:T(8,128)S(1)}, f32[1,16,128]{2,1,0:T(8,128)S(1)}, u32[]{:S(2)}, u32[]{:S(2)}) collective-permute-start(f32[1,16,128]{2,1,0:T(8,128)S(1)} %get-tuple-element.94), channel_id=1, source_target_pairs={{4,0},{8,4},{12,8},{16,12},{20,16},{24,20},{28,24},{5,1},{9,5},{13... | collective-permute-start | bytes 24584 | tf_op jit(solution)/shard_map/ppermute | solution.py:42
  82.8 3.9 %collective-permute-start.14 = (f32[10,1,128]{2,1,0:T(1,128)S(1)}, f32[10,1,128]{2,1,0:T(1,128)S(1)}, u32[]{:S(2)}, u32[]{:S(2)}) collective-permute-start(f32[10,1,128]{2,1,0:T(1,128)S(1)} %get-tuple-element.78), channel_id=1, source_target_pairs={{1,0},{2,1},{3,2},{5,4},{6,5},{7,6},{9,8},{10,9},{11,10},{13,12},{... | collective-permute-start | bytes 15368 | tf_op jit(solution)/shard_map/ppermute | solution.py:42
  90.6 4.7 %collective-permute-start.16 = (f32[1,16,128]{2,1,0:T(8,128)S(1)}, f32[1,16,128]{2,1,0:T(8,128)S(1)}, u32[]{:S(2)}, u32[]{:S(2)}) collective-permute-start(f32[1,16,128]{2,1,0:T(8,128)S(1)} %get-tuple-element.92), channel_id=1, source_target_pairs={{4,0},{8,4},{12,8},{16,12},{20,16},{24,20},{28,24},{5,1},{9,5},{13... | collective-permute-start | bytes 24584 | tf_op jit(solution)/shard_map/ppermute | solution.py:42
  98.4 3.9 %collective-permute-start.18 = (f32[10,1,128]{2,1,0:T(1,128)S(1)}, f32[10,1,128]{2,1,0:T(1,128)S(1)}, u32[]{:S(2)}, u32[]{:S(2)}) collective-permute-start(f32[10,1,128]{2,1,0:T(1,128)S(1)} %get-tuple-element.76), channel_id=1, source_target_pairs={{1,0},{2,1},{3,2},{5,4},{6,5},{7,6},{9,8},{10,9},{11,10},{13,12},{... | collective-permute-start | bytes 15368 | tf_op jit(solution)/shard_map/ppermute | solution.py:42
  106.1 4.5 %collective-permute-start.20 = (f32[1,16,128]{2,1,0:T(8,128)S(1)}, f32[1,16,128]{2,1,0:T(8,128)S(1)}, u32[]{:S(2)}, u32[]{:S(2)}) collective-permute-start(f32[1,16,128]{2,1,0:T(8,128)S(1)} %get-tuple-element.90), channel_id=1, source_target_pairs={{4,0},{8,4},{12,8},{16,12},{20,16},{24,20},{28,24},{5,1},{9,5},{13... | collective-permute-start | bytes 24584 | tf_op jit(solution)/shard_map/ppermute | solution.py:42
  114.0 3.9 %collective-permute-start.22 = (f32[10,1,128]{2,1,0:T(1,128)S(1)}, f32[10,1,128]{2,1,0:T(1,128)S(1)}, u32[]{:S(2)}, u32[]{:S(2)}) collective-permute-start(f32[10,1,128]{2,1,0:T(1,128)S(1)} %get-tuple-element.74), channel_id=1, source_target_pairs={{1,0},{2,1},{3,2},{5,4},{6,5},{7,6},{9,8},{10,9},{11,10},{13,12},{... | collective-permute-start | bytes 15368 | tf_op jit(solution)/shard_map/ppermute | solution.py:42
  121.7 4.5 %collective-permute-start.24 = (f32[1,16,128]{2,1,0:T(8,128)S(1)}, f32[1,16,128]{2,1,0:T(8,128)S(1)}, u32[]{:S(2)}, u32[]{:S(2)}) collective-permute-start(f32[1,16,128]{2,1,0:T(8,128)S(1)} %get-tuple-element.88), channel_id=1, source_target_pairs={{4,0},{8,4},{12,8},{16,12},{20,16},{24,20},{28,24},{5,1},{9,5},{13... | collective-permute-start | bytes 24584 | tf_op jit(solution)/shard_map/ppermute | solution.py:42
  129.5 3.9 %collective-permute-start.26 = (f32[10,1,128]{2,1,0:T(1,128)S(1)}, f32[10,1,128]{2,1,0:T(1,128)S(1)}, u32[]{:S(2)}, u32[]{:S(2)}) collective-permute-start(f32[10,1,128]{2,1,0:T(1,128)S(1)} %get-tuple-element.72), channel_id=1, source_target_pairs={{1,0},{2,1},{3,2},{5,4},{6,5},{7,6},{9,8},{10,9},{11,10},{13,12},{... | collective-permute-start | bytes 15368 | tf_op jit(solution)/shard_map/ppermute | solution.py:42
  137.3 4.5 %collective-permute-start.28 = (f32[1,16,128]{2,1,0:T(8,128)S(1)}, f32[1,16,128]{2,1,0:T(8,128)S(1)}, u32[]{:S(2)}, u32[]{:S(2)}) collective-permute-start(f32[1,16,128]{2,1,0:T(8,128)S(1)} %get-tuple-element.86), channel_id=1, source_target_pairs={{4,0},{8,4},{12,8},{16,12},{20,16},{24,20},{28,24},{5,1},{9,5},{13... | collective-permute-start | bytes 24584 | tf_op jit(solution)/shard_map/ppermute | solution.py:42
  145.1 3.9 %collective-permute-start.30 = (f32[10,1,128]{2,1,0:T(1,128)S(1)}, f32[10,1,128]{2,1,0:T(1,128)S(1)}, u32[]{:S(2)}, u32[]{:S(2)}) collective-permute-start(f32[10,1,128]{2,1,0:T(1,128)S(1)} %get-tuple-element.70), channel_id=1, source_target_pairs={{1,0},{2,1},{3,2},{5,4},{6,5},{7,6},{9,8},{10,9},{11,10},{13,12},{... | collective-permute-start | bytes 15368 | tf_op jit(solution)/shard_map/ppermute | solution.py:42
  152.8 4.5 %collective-permute-start.32 = (f32[1,16,128]{2,1,0:T(8,128)S(1)}, f32[1,16,128]{2,1,0:T(8,128)S(1)}, u32[]{:S(2)}, u32[]{:S(2)}) collective-permute-start(f32[1,16,128]{2,1,0:T(8,128)S(1)} %get-tuple-element.84), channel_id=1, source_target_pairs={{4,0},{8,4},{12,8},{16,12},{20,16},{24,20},{28,24},{5,1},{9,5},{13... | collective-permute-start | bytes 24584 | tf_op jit(solution)/shard_map/ppermute | solution.py:42
  160.7 3.9 %collective-permute-start.34 = (f32[10,1,128]{2,1,0:T(1,128)S(1)}, f32[10,1,128]{2,1,0:T(1,128)S(1)}, u32[]{:S(2)}, u32[]{:S(2)}) collective-permute-start(f32[10,1,128]{2,1,0:T(1,128)S(1)} %get-tuple-element.68), channel_id=1, source_target_pairs={{1,0},{2,1},{3,2},{5,4},{6,5},{7,6},{9,8},{10,9},{11,10},{13,12},{... | collective-permute-start | bytes 15368 | tf_op jit(solution)/shard_map/ppermute | solution.py:42
  168.4 4.5 %collective-permute-start.36 = (f32[1,16,128]{2,1,0:T(8,128)S(1)}, f32[1,16,128]{2,1,0:T(8,128)S(1)}, u32[]{:S(2)}, u32[]{:S(2)}) collective-permute-start(f32[1,16,128]{2,1,0:T(8,128)S(1)} %get-tuple-element.82), channel_id=1, source_target_pairs={{4,0},{8,4},{12,8},{16,12},{20,16},{24,20},{28,24},{5,1},{9,5},{13... | collective-permute-start | bytes 24584 | tf_op jit(solution)/shard_map/ppermute | solution.py:42
  176.2 3.9 %collective-permute-start.38 = (f32[10,1,128]{2,1,0:T(1,128)S(1)}, f32[10,1,128]{2,1,0:T(1,128)S(1)}, u32[]{:S(2)}, u32[]{:S(2)}) collective-permute-start(f32[10,1,128]{2,1,0:T(1,128)S(1)} %get-tuple-element.66), channel_id=1, source_target_pairs={{1,0},{2,1},{3,2},{5,4},{6,5},{7,6},{9,8},{10,9},{11,10},{13,12},{... | collective-permute-start | bytes 15368 | tf_op jit(solution)/shard_map/ppermute | solution.py:42
  184.0 4.5 %collective-permute-start.40 = (f32[1,16,128]{2,1,0:T(8,128)S(1)}, f32[1,16,128]{2,1,0:T(8,128)S(1)}, u32[]{:S(2)}, u32[]{:S(2)}) collective-permute-start(f32[1,16,128]{2,1,0:T(8,128)S(1)} %get-tuple-element.80), channel_id=1, source_target_pairs={{4,0},{8,4},{12,8},{16,12},{20,16},{24,20},{28,24},{5,1},{9,5},{13... | collective-permute-start | bytes 24584 | tf_op jit(solution)/shard_map/ppermute | solution.py:42
  191.8 3.9 %collective-permute-start.42 = (f32[10,1,128]{2,1,0:T(1,128)S(1)}, f32[10,1,128]{2,1,0:T(1,128)S(1)}, u32[]{:S(2)}, u32[]{:S(2)}) collective-permute-start(f32[10,1,128]{2,1,0:T(1,128)S(1)} %get-tuple-element.64), channel_id=1, source_target_pairs={{1,0},{2,1},{3,2},{5,4},{6,5},{7,6},{9,8},{10,9},{11,10},{13,12},{... | collective-permute-start | bytes 15368 | tf_op jit(solution)/shard_map/ppermute | solution.py:42
  (182 shorter events, 95.3 us)
Async XLA Ops:
  1.7 7.4 %collective-permute-start.1 = (f32[19,1,16,128]{3,2,1,0:T(8,128)S(1)}, f32[19,1,16,128]{3,2,1,0:T(8,128)S(1)}, u32[]{:S(2)}, u32[]{:S(2)}) collective-permute-start(f32[19,1,16,128]{3,2,1,0:T(8,128)S(1)} %get-tuple-element.62), channel_id=1, source_target_pairs={{0,4},{4,8},{8,12},{12,16},{16,20},{20,24},{24,28},{1,5},{5,9},{9,... | collective-permute-start | bytes 466952 | tf_op jit(solution)/shard_map/ppermute | solution.py:41
  3.6 7.3 %collective-permute-start = (f32[19,1,16,128]{3,2,1,0:T(8,128)S(1)}, f32[19,1,16,128]{3,2,1,0:T(8,128)S(1)}, u32[]{:S(2)}, u32[]{:S(2)}) collective-permute-start(f32[19,1,16,128]{3,2,1,0:T(8,128)S(1)} %get-tuple-element.61), channel_id=1, source_target_pairs={{4,0},{8,4},{12,8},{16,12},{20,16},{24,20},{28,24},{5,1},{9,5},{13... | collective-permute-start | bytes 466952 | tf_op jit(solution)/shard_map/ppermute | solution.py:42
  11.0 7.4 %collective-permute-start.3 = (f32[19,10,1,128]{3,2,1,0:T(1,128)S(1)}, f32[19,10,1,128]{3,2,1,0:T(1,128)S(1)}, u32[]{:S(2)}, u32[]{:S(2)}) collective-permute-start(f32[19,10,1,128]{3,2,1,0:T(1,128)S(1)} %get-tuple-element.55), channel_id=1, source_target_pairs={{0,1},{1,2},{2,3},{4,5},{5,6},{6,7},{8,9},{9,10},{10,11},{12,13},{... | collective-permute-start | bytes 291848 | tf_op jit(solution)/shard_map/ppermute | solution.py:41
  14.5 7.2 %collective-permute-start.2 = (f32[19,10,1,128]{3,2,1,0:T(1,128)S(1)}, f32[19,10,1,128]{3,2,1,0:T(1,128)S(1)}, u32[]{:S(2)}, u32[]{:S(2)}) collective-permute-start(f32[19,10,1,128]{3,2,1,0:T(1,128)S(1)} %get-tuple-element.56), channel_id=1, source_target_pairs={{1,0},{2,1},{3,2},{5,4},{6,5},{7,6},{9,8},{10,9},{11,10},{13,12},{... | collective-permute-start | bytes 291848 | tf_op jit(solution)/shard_map/ppermute | solution.py:42
  25.2 7.9 %collective-permute-start.5 = (f32[19,1,16,128]{3,2,1,0:T(8,128)S(1)}, f32[19,1,16,128]{3,2,1,0:T(8,128)S(1)}, u32[]{:S(2)}, u32[]{:S(2)}) collective-permute-start(f32[19,1,16,128]{3,2,1,0:T(8,128)S(1)} %get-tuple-element.59), channel_id=1, source_target_pairs={{0,4},{4,8},{8,12},{12,16},{16,20},{20,24},{24,28},{1,5},{5,9},{9,... | collective-permute-start | bytes 466952 | tf_op jit(solution)/shard_map/ppermute | solution.py:41
  27.1 7.3 %collective-permute-start.4 = (f32[19,1,16,128]{3,2,1,0:T(8,128)S(1)}, f32[19,1,16,128]{3,2,1,0:T(8,128)S(1)}, u32[]{:S(2)}, u32[]{:S(2)}) collective-permute-start(f32[19,1,16,128]{3,2,1,0:T(8,128)S(1)} %get-tuple-element.60), channel_id=1, source_target_pairs={{4,0},{8,4},{12,8},{16,12},{20,16},{24,20},{28,24},{5,1},{9,5},{13... | collective-permute-start | bytes 466952 | tf_op jit(solution)/shard_map/ppermute | solution.py:42
  34.6 6.5 %collective-permute-start.7 = (f32[19,10,1,128]{3,2,1,0:T(1,128)S(1)}, f32[19,10,1,128]{3,2,1,0:T(1,128)S(1)}, u32[]{:S(2)}, u32[]{:S(2)}) collective-permute-start(f32[19,10,1,128]{3,2,1,0:T(1,128)S(1)} %get-tuple-element.53), channel_id=1, source_target_pairs={{0,1},{1,2},{2,3},{4,5},{5,6},{6,7},{8,9},{9,10},{10,11},{12,13},{... | collective-permute-start | bytes 291848 | tf_op jit(solution)/shard_map/ppermute | solution.py:41
  38.1 6.5 %collective-permute-start.6 = (f32[19,10,1,128]{3,2,1,0:T(1,128)S(1)}, f32[19,10,1,128]{3,2,1,0:T(1,128)S(1)}, u32[]{:S(2)}, u32[]{:S(2)}) collective-permute-start(f32[19,10,1,128]{3,2,1,0:T(1,128)S(1)} %get-tuple-element.54), channel_id=1, source_target_pairs={{1,0},{2,1},{3,2},{5,4},{6,5},{7,6},{9,8},{10,9},{11,10},{13,12},{... | collective-permute-start | bytes 291848 | tf_op jit(solution)/shard_map/ppermute | solution.py:42
  50.1 7.7 %collective-permute-start.9 = (f32[19,1,16,128]{3,2,1,0:T(8,128)S(1)}, f32[19,1,16,128]{3,2,1,0:T(8,128)S(1)}, u32[]{:S(2)}, u32[]{:S(2)}) collective-permute-start(f32[19,1,16,128]{3,2,1,0:T(8,128)S(1)} %get-tuple-element.57), channel_id=1, source_target_pairs={{0,4},{4,8},{8,12},{12,16},{16,20},{20,24},{24,28},{1,5},{5,9},{9,... | collective-permute-start | bytes 466952 | tf_op jit(solution)/shard_map/ppermute | solution.py:41
  52.0 7.3 %collective-permute-start.8 = (f32[19,1,16,128]{3,2,1,0:T(8,128)S(1)}, f32[19,1,16,128]{3,2,1,0:T(8,128)S(1)}, u32[]{:S(2)}, u32[]{:S(2)}) collective-permute-start(f32[19,1,16,128]{3,2,1,0:T(8,128)S(1)} %get-tuple-element.58), channel_id=1, source_target_pairs={{4,0},{8,4},{12,8},{16,12},{20,16},{24,20},{28,24},{5,1},{9,5},{13... | collective-permute-start | bytes 466952 | tf_op jit(solution)/shard_map/ppermute | solution.py:42
  59.4 6.5 %collective-permute-start.11 = (f32[19,10,1,128]{3,2,1,0:T(1,128)S(1)}, f32[19,10,1,128]{3,2,1,0:T(1,128)S(1)}, u32[]{:S(2)}, u32[]{:S(2)}) collective-permute-start(f32[19,10,1,128]{3,2,1,0:T(1,128)S(1)} %get-tuple-element.51), channel_id=1, source_target_pairs={{0,1},{1,2},{2,3},{4,5},{5,6},{6,7},{8,9},{9,10},{10,11},{12,13},{... | collective-permute-start | bytes 291848 | tf_op jit(solution)/shard_map/ppermute | solution.py:41
  61.4 6.6 %collective-permute-start.10 = (f32[19,10,1,128]{3,2,1,0:T(1,128)S(1)}, f32[19,10,1,128]{3,2,1,0:T(1,128)S(1)}, u32[]{:S(2)}, u32[]{:S(2)}) collective-permute-start(f32[19,10,1,128]{3,2,1,0:T(1,128)S(1)} %get-tuple-element.52), channel_id=1, source_target_pairs={{1,0},{2,1},{3,2},{5,4},{6,5},{7,6},{9,8},{10,9},{11,10},{13,12},{... | collective-permute-start | bytes 291848 | tf_op jit(solution)/shard_map/ppermute | solution.py:42
  73.1 6.6 %collective-permute-start.13 = (f32[1,16,128]{2,1,0:T(8,128)S(1)}, f32[1,16,128]{2,1,0:T(8,128)S(1)}, u32[]{:S(2)}, u32[]{:S(2)}) collective-permute-start(f32[1,16,128]{2,1,0:T(8,128)S(1)} %get-tuple-element.93), channel_id=1, source_target_pairs={{0,4},{4,8},{8,12},{12,16},{16,20},{20,24},{24,28},{1,5},{5,9},{9,... | collective-permute-start | bytes 24584 | tf_op jit(solution)/shard_map/ppermute | solution.py:41
  88.6 6.8 %collective-permute-start.17 = (f32[1,16,128]{2,1,0:T(8,128)S(1)}, f32[1,16,128]{2,1,0:T(8,128)S(1)}, u32[]{:S(2)}, u32[]{:S(2)}) collective-permute-start(f32[1,16,128]{2,1,0:T(8,128)S(1)} %get-tuple-element.91), channel_id=1, source_target_pairs={{0,4},{4,8},{8,12},{12,16},{16,20},{20,24},{24,28},{1,5},{5,9},{9,... | collective-permute-start | bytes 24584 | tf_op jit(solution)/shard_map/ppermute | solution.py:41
  96.5 5.9 %collective-permute-start.19 = (f32[10,1,128]{2,1,0:T(1,128)S(1)}, f32[10,1,128]{2,1,0:T(1,128)S(1)}, u32[]{:S(2)}, u32[]{:S(2)}) collective-permute-start(f32[10,1,128]{2,1,0:T(1,128)S(1)} %get-tuple-element.75), channel_id=1, source_target_pairs={{0,1},{1,2},{2,3},{4,5},{5,6},{6,7},{8,9},{9,10},{10,11},{12,13},{... | collective-permute-start | bytes 15368 | tf_op jit(solution)/shard_map/ppermute | solution.py:41
  104.2 6.5 %collective-permute-start.21 = (f32[1,16,128]{2,1,0:T(8,128)S(1)}, f32[1,16,128]{2,1,0:T(8,128)S(1)}, u32[]{:S(2)}, u32[]{:S(2)}) collective-permute-start(f32[1,16,128]{2,1,0:T(8,128)S(1)} %get-tuple-element.89), channel_id=1, source_target_pairs={{0,4},{4,8},{8,12},{12,16},{16,20},{20,24},{24,28},{1,5},{5,9},{9,... | collective-permute-start | bytes 24584 | tf_op jit(solution)/shard_map/ppermute | solution.py:41
  119.8 6.5 %collective-permute-start.25 = (f32[1,16,128]{2,1,0:T(8,128)S(1)}, f32[1,16,128]{2,1,0:T(8,128)S(1)}, u32[]{:S(2)}, u32[]{:S(2)}) collective-permute-start(f32[1,16,128]{2,1,0:T(8,128)S(1)} %get-tuple-element.87), channel_id=1, source_target_pairs={{0,4},{4,8},{8,12},{12,16},{16,20},{20,24},{24,28},{1,5},{5,9},{9,... | collective-permute-start | bytes 24584 | tf_op jit(solution)/shard_map/ppermute | solution.py:41
  135.3 6.6 %collective-permute-start.29 = (f32[1,16,128]{2,1,0:T(8,128)S(1)}, f32[1,16,128]{2,1,0:T(8,128)S(1)}, u32[]{:S(2)}, u32[]{:S(2)}) collective-permute-start(f32[1,16,128]{2,1,0:T(8,128)S(1)} %get-tuple-element.85), channel_id=1, source_target_pairs={{0,4},{4,8},{8,12},{12,16},{16,20},{20,24},{24,28},{1,5},{5,9},{9,... | collective-permute-start | bytes 24584 | tf_op jit(solution)/shard_map/ppermute | solution.py:41
  143.2 5.9 %collective-permute-start.31 = (f32[10,1,128]{2,1,0:T(1,128)S(1)}, f32[10,1,128]{2,1,0:T(1,128)S(1)}, u32[]{:S(2)}, u32[]{:S(2)}) collective-permute-start(f32[10,1,128]{2,1,0:T(1,128)S(1)} %get-tuple-element.69), channel_id=1, source_target_pairs={{0,1},{1,2},{2,3},{4,5},{5,6},{6,7},{8,9},{9,10},{10,11},{12,13},{... | collective-permute-start | bytes 15368 | tf_op jit(solution)/shard_map/ppermute | solution.py:41
  150.9 6.5 %collective-permute-start.33 = (f32[1,16,128]{2,1,0:T(8,128)S(1)}, f32[1,16,128]{2,1,0:T(8,128)S(1)}, u32[]{:S(2)}, u32[]{:S(2)}) collective-permute-start(f32[1,16,128]{2,1,0:T(8,128)S(1)} %get-tuple-element.83), channel_id=1, source_target_pairs={{0,4},{4,8},{8,12},{12,16},{16,20},{20,24},{24,28},{1,5},{5,9},{9,... | collective-permute-start | bytes 24584 | tf_op jit(solution)/shard_map/ppermute | solution.py:41
  158.7 6.0 %collective-permute-start.35 = (f32[10,1,128]{2,1,0:T(1,128)S(1)}, f32[10,1,128]{2,1,0:T(1,128)S(1)}, u32[]{:S(2)}, u32[]{:S(2)}) collective-permute-start(f32[10,1,128]{2,1,0:T(1,128)S(1)} %get-tuple-element.67), channel_id=1, source_target_pairs={{0,1},{1,2},{2,3},{4,5},{5,6},{6,7},{8,9},{9,10},{10,11},{12,13},{... | collective-permute-start | bytes 15368 | tf_op jit(solution)/shard_map/ppermute | solution.py:41
  166.5 6.6 %collective-permute-start.37 = (f32[1,16,128]{2,1,0:T(8,128)S(1)}, f32[1,16,128]{2,1,0:T(8,128)S(1)}, u32[]{:S(2)}, u32[]{:S(2)}) collective-permute-start(f32[1,16,128]{2,1,0:T(8,128)S(1)} %get-tuple-element.81), channel_id=1, source_target_pairs={{0,4},{4,8},{8,12},{12,16},{16,20},{20,24},{24,28},{1,5},{5,9},{9,... | collective-permute-start | bytes 24584 | tf_op jit(solution)/shard_map/ppermute | solution.py:41
  182.0 6.5 %collective-permute-start.41 = (f32[1,16,128]{2,1,0:T(8,128)S(1)}, f32[1,16,128]{2,1,0:T(8,128)S(1)}, u32[]{:S(2)}, u32[]{:S(2)}) collective-permute-start(f32[1,16,128]{2,1,0:T(8,128)S(1)} %get-tuple-element.79), channel_id=1, source_target_pairs={{0,4},{4,8},{8,12},{12,16},{16,20},{20,24},{24,28},{1,5},{5,9},{9,... | collective-permute-start | bytes 24584 | tf_op jit(solution)/shard_map/ppermute | solution.py:41
  189.9 6.0 %collective-permute-start.43 = (f32[10,1,128]{2,1,0:T(1,128)S(1)}, f32[10,1,128]{2,1,0:T(1,128)S(1)}, u32[]{:S(2)}, u32[]{:S(2)}) collective-permute-start(f32[10,1,128]{2,1,0:T(1,128)S(1)} %get-tuple-element.63), channel_id=1, source_target_pairs={{0,1},{1,2},{2,3},{4,5},{5,6},{6,7},{8,9},{9,10},{10,11},{12,13},{... | collective-permute-start | bytes 15368 | tf_op jit(solution)/shard_map/ppermute | solution.py:41
  (27 other events, 171.9 us)
where the time goes:
time: 202 us; the launch traced here: 198 us
  starting transfers between devices  136 us (67%)
  waiting for transfers between devices  39.5 us (20%)
  other arithmetic  18.6 us (9%)
  local copies, waits for them, and re-layouts  2.71 us (1%)
    ppermute x22, starting transfers between devices, padded_2(): after = lax.ppermute(leading, axis, down)  90.2 us
    ppermute x22, starting transfers between devices, padded_2(): before = lax.ppermute(last, axis, up)  45.4 us
    ppermute x22, waiting for transfers between devices, padded_2(): after = lax.ppermute(leading, axis, down)  34 us
    concatenate x21, other arithmetic, padded_2(): x = jnp.concatenate([before, x, after], axis=dim)  12.4 us
    ppermute x22, waiting for transfers between devices, padded_2(): before = lax.ppermute(last, axis, up)  5.48 us
  transfers between devices with their start and end apart: 44, of which 28 were waited for; matrix products, arithmetic and copies ran while one was open for 2% of the time, Pallas kernels for 0%

commit v1 on v0

v1 whole, which is shorter than its diff:
```python
import functools

import jax
import jax.numpy as jnp
from jax import lax
from jax.experimental import pallas as pl
from jax.experimental.pallas import tpu as pltpu
from jax.sharding import PartitionSpec as P

SWEEPS = 8
REACH = 8

VELOCITIES = (
    (0, 0, 0),
    (1, 0, 0),
    (-1, 0, 0),
    (0, 1, 0),
    (0, -1, 0),
    (0, 0, 1),
    (0, 0, -1),
    (1, 1, 0),
    (-1, -1, 0),
    (1, -1, 0),
    (-1, 1, 0),
    (1, 0, 1),
    (-1, 0, -1),
    (1, 0, -1),
    (-1, 0, 1),
    (0, 1, 1),
    (0, -1, -1),
    (0, 1, -1),
    (0, -1, 1),
)
POPS = 19
SHARE = 1.0 / 36.0
MULTIPLE = (12.0,) + (2.0,) * 6 + (1.0,) * 12
RIGHT = tuple(i for i in range(POPS) if VELOCITIES[i][0] == 1)
LEFT = tuple(i for i in range(POPS) if VELOCITIES[i][0] == -1)
LEVEL = tuple(i for i in range(POPS) if VELOCITIES[i][0] == 0)
PAD = 8
FIRST = 5
EDGES = 19


def rim_entries(sign):
    entries = [(0, i, 1) for i in range(POPS)]
    entries += [(0, i, 2) for i in range(POPS) if VELOCITIES[i][1] != -sign]
    entries += [(0, i, 3) for i in range(POPS) if VELOCITIES[i][1] == sign]
    for distance in (1, 2):
        entries += [(1, i, distance) for i in range(3)]
        entries += [(2, 0, distance), (3, 0, distance)]
    return entries


def lane_pull(v, cz):
    if cz == 0:
        return v
    lanes = v.shape[-1]
    lane = lax.broadcasted_iota(jnp.int32, v.shape, 1)
    if cz == 1:
        return jnp.where(lane != lanes - 1, pltpu.roll(v, lanes - 1, 1), 0.0)
    return jnp.where(lane != 0, pltpu.roll(v, 1, 1), 0.0)


def total(terms):
    terms = [t for t in terms if t is not None]
    return functools.reduce(lambda a, b: a + b, terms) if terms else None


def scaled(v, factor):
    return None if v is None else factor * v


def negated(v):
    return None if v is None else -v


def moments(p):
    s, d = {}, {}
    for i in range(1, POPS, 2):
        a, b = p[i], p[i + 1]
        s[i] = total([a, b])
        d[i] = a - b if a is not None and b is not None else (a if b is None else negated(b))
    average = total(
        [scaled(p[0], 12.0), scaled(total([s[1], s[3], s[5]]), 2.0)] + [s[i] for i in (7, 9, 11, 13, 15, 17)]
    )
    along_x = total([scaled(d[1], 2.0), d[7], d[9], d[11], d[13]])
    along_y = total([scaled(d[3], 2.0), d[7], negated(d[9]), d[15], d[17]])
    along_z = total([scaled(d[5], 2.0), d[11], negated(d[13]), d[15], negated(d[17])])
    return average, (along_x, along_y, along_z)


def relaxed(p, u):
    average, along = moments(p)
    shift = total([u[k] * along[k] for k in range(3) if along[k] is not None])
    return shift, SHARE * average + shift


def pulled_from(read, pops):
    p = [None] * POPS
    for i in pops:
        p[i] = lane_pull(read(i), VELOCITIES[i][2])
    return p


def posts_of(p, keep, equilib, rate, source, pops):
    base = rate * equilib
    terms = {m: base + (source if m == 1.0 else m * source) for m in (12.0, 2.0, 1.0)}
    return {i: keep * p[i] + terms[MULTIPLE[i]] for i in pops}


def extend(x_size, y_size, dual, vel, grad, fluid, above, below, state, coef):
    pitch = y_size + 2 * PAD
    planes = x_size + 2
    lanes = dual.shape[-1]
    flat = state.reshape(state.shape[0] * pitch, lanes)

    def copy_own(i, _):
        for x in range(x_size):
            state[i * planes + x + 1, pl.ds(PAD, y_size), :] = dual[i * x_size + x]
        return 0

    lax.fori_loop(0, POPS, copy_own, 0)
    rows = {}
    for sign, ref in ((1, above), (-1, below)):
        for k, (kind, i, distance) in enumerate(rim_entries(sign)):
            at = PAD + (y_size - 1 + distance if sign == 1 else -distance)
            value = ref[pl.ds(k * x_size, x_size), :]
            if kind == 0:
                flat[pl.ds((i * planes + 1) * pitch + at, x_size, stride=pitch), :] = value
            else:
                rows[(kind, i, at)] = value
    coef_flat = coef.reshape(coef.shape[0] * pitch, lanes)

    def coefficients(there, ux, uy, uz, g):
        inside = there > 0.5
        wet = jnp.where(inside, there - 1.0, 0.0)
        keep = jnp.where(inside, 0.1 - 0.7 * wet, 0.0)
        rate = jnp.where(inside, 0.9 + 0.7 * wet, 0.0)
        scale = (3.0 * SHARE) * wet
        return keep, rate, scale * ux, scale * uy, scale * uz, SHARE * g

    def own_coefficients(x, _):
        there = fluid[x].astype(jnp.float32) + 1.0
        values = coefficients(there, vel[x], vel[x_size + x], vel[2 * x_size + x], grad[x])
        for n, value in enumerate(values):
            coef[n * x_size + x, pl.ds(PAD, y_size), :] = value
        return 0

    lax.fori_loop(0, x_size, own_coefficients, 0)
    for at in sorted({key[2] for key in rows}):
        values = coefficients(rows[(2, 0, at)], *(rows[(1, n, at)] for n in range(3)), rows[(3, 0, at)])
        for n, value in enumerate(values):
            coef_flat[pl.ds(n * x_size * pitch + at, x_size, stride=pitch), :] = value


def rim_kernel(x_size, y_size, dual, vel, grad, fluid, low, high):
    lanes = dual.shape[-1]
    flat = [ref.reshape(ref.shape[0] * y_size, lanes) for ref in (dual, vel, fluid, grad)]
    for sign, out in ((1, low), (-1, high)):
        for k, (kind, i, distance) in enumerate(rim_entries(sign)):
            row = distance - 1 if sign == 1 else y_size - distance
            value = flat[kind][pl.ds(i * x_size * y_size + row, x_size, stride=y_size), :]
            if kind == 2:
                value = value.astype(jnp.float32) + 1.0
            out[pl.ds(k * x_size, x_size), :] = value


def edge_kernel(x_size, y_size, dual, vel, grad, fluid, above, below, to_left, to_right, state, coef, near, far):
    extend(x_size, y_size, dual, vel, grad, fluid, above, below, state, coef)
    planes = x_size + 2
    window = y_size + 8
    groups = window // 8
    for out, plane, inward, pops in ((to_left, 0, 1, RIGHT), (to_right, x_size - 1, -1, LEFT)):
        known = pops + LEVEL

        def coefs(x, at):
            return [coef[n * x_size + x, pl.ds(at, 8), :] for n in range(6)]

        def read_state(x, at):
            def read(i):
                cx, cy, _ = VELOCITIES[i]
                return state[i * planes + x + 1 + cx, pl.ds(at + cy, 8), :]

            return read

        for j in range(groups):
            at = FIRST + 8 * j
            keep, rate, *u, source = coefs(plane, at)
            for n, i in enumerate(pops):
                out[pl.ds(n * window + 8 * j, 8), :] = state[i * planes + plane + 1, pl.ds(at, 8), :]
            for n, value in enumerate((rate, *u)):
                out[pl.ds((15 + n) * window + 8 * j, 8), :] = value
            p = pulled_from(read_state(plane, at), known)
            _, equilib = relaxed(p, u)
            posts = posts_of(p, keep, equilib, rate, source, known)
            for n, i in enumerate(pops):
                out[pl.ds((5 + n) * window + 8 * j, 8), :] = posts[i]
            for n, i in enumerate(LEVEL):
                near[n, pl.ds(at, 8), :] = posts[i]
            keep, rate, *u, source = coefs(plane + inward, at)
            p = pulled_from(read_state(plane + inward, at), range(POPS))
            _, equilib = relaxed(p, u)
            posts = posts_of(p, keep, equilib, rate, source, pops)
            for n, i in enumerate(pops):
                far[n, pl.ds(at, 8), :] = posts[i]
        for j in range(groups):
            at = FIRST + 8 * j
            keep, rate, *u, source = coefs(plane, at)

            def read(i):
                ref, n = (far, pops.index(i)) if i in pops else (near, LEVEL.index(i))
                return ref[n, pl.ds(at + VELOCITIES[i][1], 8), :]

            p = pulled_from(read, known)
            _, equilib = relaxed(p, u)
            posts = posts_of(p, keep, equilib, rate, source, pops)
            for n, i in enumerate(pops):
                out[pl.ds((10 + n) * window + 8 * j, 8), :] = posts[i]


def steps_kernel(
    x_size, y_size, dual, vel, grad, fluid, above, below, heat, span, from_right, from_left,
    adjoint, sens, state, later, coef, shifts, extra,
):
    extend(x_size, y_size, dual, vel, grad, fluid, above, below, state, coef)
    planes = x_size + 2
    window = y_size + 8
    groups = window // 8
    sides = ((from_right, x_size - 1, x_size + 1, RIGHT, LEFT), (from_left, 0, 0, LEFT, RIGHT))

    for ref, _, halo, pops, _ in sides:
        for n, i in enumerate(pops):
            for j in range(groups):
                state[i * planes + halo, pl.ds(FIRST + 8 * j, 8), :] = ref[pl.ds(n * window + 8 * j, 8), :]

    def read_from(source, x, at):
        def read(i):
            cx, cy, _ = VELOCITIES[i]
            return source[i * planes + x + 1 + cx, pl.ds(at + cy, 8), :]

        return read

    def step(number, source, target):
        def plane(x, _):
            for j in range(groups):
                at = FIRST + 8 * j
                keep, rate, *u, drive = [coef[n * x_size + x, pl.ds(at, 8), :] for n in range(6)]
                p = pulled_from(read_from(source, x, at), range(POPS))
                shift, equilib = relaxed(p, u)
                shifts[(number - 1) * x_size + x, pl.ds(at, 8), :] = shift
                posts = posts_of(p, keep, equilib, rate, drive, range(POPS))
                for i in range(POPS):
                    target[i * planes + x + 1, pl.ds(at, 8), :] = posts[i]
            return 0

        lax.fori_loop(0, x_size, plane, 0)
        for side, (ref, edge, halo, pops, back) in enumerate(sides):
            for j in range(groups):
                at = FIRST + 8 * j
                rate, *u = [ref[pl.ds((15 + n) * window + 8 * j, 8), :] for n in range(4)]

                def read(i):
                    cy = VELOCITIES[i][1]
                    if i in back:
                        return source[i * planes + edge + 1, pl.ds(at + cy, 8), :]
                    return extra[side, pl.ds(at + cy, 8), :]

                p = pulled_from(read, back if number == 1 else back + LEVEL)
                added = rate * relaxed(p, u)[1]
                if number == 1:
                    extra[side, pl.ds(at, 8), :] = added
                for n, i in enumerate(pops):
                    target[i * planes + halo, pl.ds(at, 8), :] = (
                        ref[pl.ds((5 * number + n) * window + 8 * j, 8), :] + added
                    )

    step(1, state, later)
    step(2, later, state)

    def last(x, _):
        for j in range(y_size // 8):
            at = PAD + 8 * j
            keep, rate, *u, drive = [coef[n * x_size + x, pl.ds(at, 8), :] for n in range(6)]
            p = pulled_from(read_from(state, x, at), range(POPS))
            shift, equilib = relaxed(p, u)
            posts = posts_of(p, keep, equilib, rate, drive, range(POPS))
            for i in range(POPS):
                adjoint[i * x_size + x, pl.ds(8 * j, 8), :] = posts[i]
            shift = shifts[x, pl.ds(at, 8), :] + shifts[x_size + x, pl.ds(at, 8), :] + shift
            sens[x, pl.ds(8 * j, 8), :] = heat[x, pl.ds(8 * j, 8), :] * shift
        sens[x_size + x] = span[x].astype(jnp.float32) + 1.0
        return 0

    lax.fori_loop(0, x_size, last, 0)


def band_kernel(x_size, y_size, own, left, right, low, high):
    for kind in range(2):
        for n, ref in enumerate((left, own, right)):
            for x in range(x_size):
                k = kind * 3 * x_size + n * x_size + x
                low[k] = ref[kind * x_size + x, pl.ds(0, REACH), :]
                high[k] = ref[kind * x_size + x, pl.ds(y_size - REACH, REACH), :]


def filter_kernel(x_size, y_size, own, left, right, above, below, filtered, first, second, given, beta):
    wide = 3 * x_size
    rows = y_size + 2 * REACH

    def prepare(n, ref):
        def plane(x, _):
            k = n * x_size + x
            parts = (
                (0, REACH, below[k], below[wide + k]),
                (REACH, y_size, ref[x], ref[x_size + x]),
                (REACH + y_size, REACH, above[k], above[wide + k]),
            )
            for start, count, s, there in parts:
                r2 = jnp.where(there < 1.5, 0.25, jnp.where(there < 2.5, 1.0, jnp.where(there < 3.5, 4.0, 16.0)))
                inverse = 1.0 / (1.0 + 6.0 * r2)
                first[k, pl.ds(PAD + start, count), :] = s
                given[k, pl.ds(start, count), :] = s * inverse
                beta[k, pl.ds(start, count), :] = jnp.where(there > 0.5, r2 * inverse, 0.0)
            return 0

        lax.fori_loop(0, x_size, plane, 0)

    for n, ref in enumerate((left, own, right)):
        prepare(n, ref)
    source, target = first, second
    for number in range(1, SWEEPS + 1):
        final = number == SWEEPS
        margin = SWEEPS - number

        def plane(x, _, source=source, target=target, final=final):
            for j in range(1, 1 + y_size // 8) if final else range(rows // 8):
                at = PAD + 8 * j
                middle = source[x, pl.ds(at, 8), :]
                beside = source[x + 1, pl.ds(at, 8), :] + source[x - 1, pl.ds(at, 8), :]
                beside = beside + source[x, pl.ds(at + 1, 8), :] + source[x, pl.ds(at - 1, 8), :]
                beside = beside + lane_pull(middle, 1) + lane_pull(middle, -1)
                value = given[x, pl.ds(8 * j, 8), :] + beta[x, pl.ds(8 * j, 8), :] * beside
                if final:
                    filtered[x - x_size, pl.ds(8 * j - REACH, 8), :] = value
                else:
                    target[x, pl.ds(at, 8), :] = value
            return 0

        lax.fori_loop(x_size - margin, 2 * x_size + margin, plane, 0)
        source, target = target, source


def call(kernel, outs, scratch, args, name):
    return pl.pallas_call(
        kernel,
        out_shape=[jax.ShapeDtypeStruct(shape, jnp.float32) for shape in outs],
        in_specs=[pl.BlockSpec(memory_space=pltpu.VMEM)] * len(args),
        out_specs=[pl.BlockSpec(memory_space=pltpu.VMEM)] * len(outs),
        scratch_shapes=[pltpu.VMEM(shape, jnp.float32) for shape in scratch],
        compiler_params=pltpu.CompilerParams(vmem_limit_bytes=32 * 1024 * 1024),
        name=name,
    )(*args)


def both_ways(axis, to_previous, to_next):
    size = lax.axis_size(axis)
    on = [(i, i + 1) for i in range(size - 1)]
    back = [(i + 1, i) for i in range(size - 1)]
    return lax.ppermute(to_previous, axis, back), lax.ppermute(to_next, axis, on)


def on_device(dual_populace, forward_motion_vector, forward_heat_level, objective_heat_gradient, liquid_indicator,
              filter_span_group):
    _, x_size, y_size, lanes = dual_populace.shape
    planes, pitch, window = x_size + 2, y_size + 2 * PAD, y_size + 8
    dual = dual_populace.reshape(POPS * x_size, y_size, lanes)
    vel = forward_motion_vector.reshape(3 * x_size, y_size, lanes)
    fields = (dual, vel, objective_heat_gradient, liquid_indicator)
    rim = (len(rim_entries(1)) * x_size, lanes)
    edge = (EDGES * window, lanes)
    state = (POPS * planes, pitch, lanes)
    coef = (6 * x_size, pitch, lanes)

    low, high = call(
        functools.partial(rim_kernel, x_size, y_size), [rim, rim], [], fields, "rim_rows"
    )
    above, below = both_ways("blk", low, high)
    to_left, to_right = call(
        functools.partial(edge_kernel, x_size, y_size),
        [edge, edge],
        [state, coef, (len(LEVEL), pitch, lanes), (len(RIGHT), pitch, lanes)],
        (*fields, above, below),
        "edge_planes",
    )
    from_right, from_left = both_ways("grp", to_left, to_right)
    adjoint, sens = call(
        functools.partial(steps_kernel, x_size, y_size),
        [(POPS * x_size, y_size, lanes), (2 * x_size, y_size, lanes)],
        [state, state, coef, (2 * x_size, pitch, lanes), (2, pitch, lanes)],
        (*fields, above, below, forward_heat_level, filter_span_group, from_right, from_left),
        "three_steps",
    )
    right, left = both_ways("grp", sens, sens)
    band = (6 * x_size, REACH, lanes)
    low, high = call(
        functools.partial(band_kernel, x_size, y_size), [band, band], [], (sens, left, right), "band_rows"
    )
    above, below = both_ways("blk", low, high)
    wide = 3 * x_size
    rows = y_size + 2 * REACH
    (filtered,) = call(
        functools.partial(filter_kernel, x_size, y_size),
        [(x_size, y_size, lanes)],
        [(wide, rows + 2 * PAD, lanes)] * 2 + [(wide, rows, lanes)] * 2,
        (sens, left, right, above, below),
        "eight_sweeps",
    )
    return adjoint.reshape(dual_populace.shape), filtered


def solution(mesh):
    in_specs = (
        P(None, "grp", "blk", None),
        P(None, "grp", "blk", None),
        P("grp", "blk", None),
        P("grp", "blk", None),
        P("grp", "blk", None),
        P("grp", "blk", None),
    )
    out_specs = (P(None, "grp", "blk", None), P("grp", "blk", None))
    return jax.shard_map(
        on_device, mesh=mesh, in_specs=in_specs, out_specs=out_specs, check_vma=False
    )
```

time: 202 us -> 61.3 us (0.30); the launches traced: 198 us -> 60.4 us
  starting transfers between devices: 136 us -> 20.5 us
  waiting for transfers between devices: 39.5 us -> 19 us
  other arithmetic: 18.6 us -> 0 us
  Pallas kernels: 0 us -> 16.3 us
    ppermute x44 -> x8, starting transfers between devices: 136 us -> 20.5 us  [the longest x4 12.2 us: both_ways(): lax.ppermute(to_next, axis, on)]
    ppermute x44 -> x8, waiting for transfers between devices: 39.5 us -> 19 us  [the longest x4 13.4 us: both_ways(): lax.ppermute(to_next, axis, on)]
    pallas_call x0 -> x5, Pallas kernels: none -> 16.3 us  [call(): pl.pallas_call(kernel, out_shape=[jax.ShapeDtypeStruct(shape, jnp.float32...]
    concatenate x21 -> x0, other arithmetic: 12.4 us -> none  [padded_2(): x = jnp.concatenate([before, x, after], axis=dim)]
    unnamed x54 -> x0, other arithmetic: 2.97 us -> none
    unnamed x16 -> x12, local copies, waits for them, and re-layouts: 1.47 us -> 3.9 us
  transfers between devices with their start and end apart: 44 -> 8, of which waited for: 28 -> 8; matrix products, arithmetic and copies ran while one was open for 2% -> 0% of each run, Pallas kernels for 0% -> 0%
where the time goes in v1:
time: 61.3 us; the launch traced here: 60.4 us
  starting transfers between devices  20.5 us (33%)
  waiting for transfers between devices  19 us (31%)
  Pallas kernels  16.3 us (27%)
  local copies, waits for them, and re-layouts  3.9 us (6%)
  between operations  0.74 us (1%)
    pallas_call x5, Pallas kernels, call(): pl.pallas_call(kernel, out_shape=[jax.ShapeDtypeStruct(shape, jnp.float32...  16.3 us
    ppermute x4, waiting for transfers between devices, both_ways(): lax.ppermute(to_next, axis, on)  13.4 us
    ppermute x4, starting transfers between devices, both_ways(): lax.ppermute(to_next, axis, on)  12.2 us
    ppermute x4, starting transfers between devices, both_ways(): lax.ppermute(to_previous, axis, back)  8.24 us
    ppermute x4, waiting for transfers between devices, both_ways(): lax.ppermute(to_previous, axis, back)  5.61 us
    unnamed x12, local copies, waits for them, and re-layouts  3.9 us
  transfers between devices with their start and end apart: 8, of which 8 were waited for; matrix products, arithmetic and copies ran while one was open for 0% of the time, Pallas kernels for 0%

profile of v1, /device:TPU:12, one launch (start us, length us, event | category | flops | bytes accessed | tf_op | source)
XLA Modules:
  0.0 60.4 jit_solution(1387169273894712933)
XLA Ops:
  0.6 1.3 %copy-done = f32[19,8,16,128]{3,2,1,0:T(8,128)S(1)} copy-done((f32[19,8,16,128]{3,2,1,0:T(8,128)S(1)}, f32[19,8,16,128]{3,2,1,0:T(8,128)}, u32[]{:S(2)}) %copy-start) | copy-done | bytes 1245208
  1.9 0.9 %copy-done.1 = f32[3,8,16,128]{3,2,1,0:T(8,128)S(1)} copy-done((f32[3,8,16,128]{3,2,1,0:T(8,128)S(1)}, f32[3,8,16,128]{3,2,1,0:T(8,128)}, u32[]{:S(2)}) %copy-start.1) | copy-done | bytes 196632
  2.9 0.8 %copy-done.2 = f32[8,16,128]{2,1,0:T(8,128)S(1)} copy-done((f32[8,16,128]{2,1,0:T(8,128)S(1)}, f32[8,16,128]{2,1,0:T(8,128)}, u32[]{:S(2)}) %copy-start.2) | copy-done | bytes 65560
  3.7 0.8 %copy-done.3 = s32[8,16,128]{2,1,0:T(8,128)S(1)} copy-done((s32[8,16,128]{2,1,0:T(8,128)S(1)}, s32[8,16,128]{2,1,0:T(8,128)}, u32[]{:S(2)}) %copy-start.3) | copy-done | bytes 65560
  4.5 0.1 rim_rows.1
  4.7 2.5 %collective-permute-start = (f32[384,128]{1,0:T(8,128)S(1)}, f32[384,128]{1,0:T(8,128)S(1)}, u32[]{:S(2)}, u32[]{:S(2)}) collective-permute-start(f32[384,128]{1,0:T(8,128)S(1)} %get-tuple-element.10), channel_id=1, source_target_pairs={{1,0},{2,1},{3,2},{5,4},{6,5},{7,6},{9,8},{10,9},{11,10},{13,12},{... | collective-permute-start | bytes 589832 | tf_op jit(solution)/shard_map/ppermute | solution.py:370
  7.2 3.5 %collective-permute-start.1 = (f32[384,128]{1,0:T(8,128)S(1)}, f32[384,128]{1,0:T(8,128)S(1)}, u32[]{:S(2)}, u32[]{:S(2)}) collective-permute-start(f32[384,128]{1,0:T(8,128)S(1)} %get-tuple-element.11), channel_id=1, source_target_pairs={{0,1},{1,2},{2,3},{4,5},{5,6},{6,7},{8,9},{9,10},{10,11},{12,13},{... | collective-permute-start | bytes 589832 | tf_op jit(solution)/shard_map/ppermute | solution.py:370
  10.7 2.7 %collective-permute-done.above = f32[384,128]{1,0:T(8,128)S(1)} collective-permute-done((f32[384,128]{1,0:T(8,128)S(1)}, f32[384,128]{1,0:T(8,128)S(1)}, u32[]{:S(2)}, u32[]{:S(2)}) %collective-permute-start) | collective-permute-done | bytes 196640 | tf_op jit(solution)/shard_map/ppermute | solution.py:370
  13.4 2.1 %collective-permute-done.1.below = f32[384,128]{1,0:T(8,128)S(1)} collective-permute-done((f32[384,128]{1,0:T(8,128)S(1)}, f32[384,128]{1,0:T(8,128)S(1)}, u32[]{:S(2)}, u32[]{:S(2)}) %collective-permute-start.1) | collective-permute-done | bytes 196640 | tf_op jit(solution)/shard_map/ppermute | solution.py:370
  15.5 0.7 %edge_planes.1 = (f32[456,128]{1,0:T(8,128)S(1)}, f32[456,128]{1,0:T(8,128)S(1)}) custom-call(f32[152,16,128]{2,1,0:T(8,128)S(1)} %bitcast.4, f32[24,16,128]{2,1,0:T(8,128)S(1)} %bitcast.7, f32[8,16,128]{2,1,0:T(8,128)S(1)} %copy-done.2, s32[8,16,128]{2,1,0:T(8,128)S(1)} %copy-done.3, f32[384,128]{1,0:T(8,128)S(1)} %collective-permute-done.above, ...), custom_call_target="tpu_custom_call" | custom-call | tf_op jit(solution)/shard_map/edge_planes/pallas_call | solution.py:355
  16.1 1.9 %collective-permute-start.2 = (f32[456,128]{1,0:T(8,128)S(1)}, f32[456,128]{1,0:T(8,128)S(1)}, u32[]{:S(2)}, u32[]{:S(2)}) collective-permute-start(f32[456,128]{1,0:T(8,128)S(1)} %get-tuple-element.12), channel_id=1, source_target_pairs={{4,0},{8,4},{12,8},{16,12},{20,16},{24,20},{28,24},{5,1},{9,5},{13... | collective-permute-start | bytes 700424 | tf_op jit(solution)/shard_map/ppermute | solution.py:370
  18.1 2.4 %collective-permute-start.3 = (f32[456,128]{1,0:T(8,128)S(1)}, f32[456,128]{1,0:T(8,128)S(1)}, u32[]{:S(2)}, u32[]{:S(2)}) collective-permute-start(f32[456,128]{1,0:T(8,128)S(1)} %get-tuple-element.13), channel_id=1, source_target_pairs={{0,4},{4,8},{8,12},{12,16},{16,20},{20,24},{24,28},{1,5},{5,9},{9,... | collective-permute-start | bytes 700424 | tf_op jit(solution)/shard_map/ppermute | solution.py:370
  20.5 1.1 %collective-permute-done.2.from_right = f32[456,128]{1,0:T(8,128)S(1)} collective-permute-done((f32[456,128]{1,0:T(8,128)S(1)}, f32[456,128]{1,0:T(8,128)S(1)}, u32[]{:S(2)}, u32[]{:S(2)}) %collective-permute-start.2) | collective-permute-done | bytes 233504 | tf_op jit(solution)/shard_map/ppermute | solution.py:370
  21.6 4.7 %collective-permute-done.3.from_left = f32[456,128]{1,0:T(8,128)S(1)} collective-permute-done((f32[456,128]{1,0:T(8,128)S(1)}, f32[456,128]{1,0:T(8,128)S(1)}, u32[]{:S(2)}, u32[]{:S(2)}) %collective-permute-start.3) | collective-permute-done | bytes 233504 | tf_op jit(solution)/shard_map/ppermute | solution.py:370
  26.4 4.8 %three_steps.1 = (f32[152,16,128]{2,1,0:T(8,128)}, f32[16,16,128]{2,1,0:T(8,128)S(1)}) custom-call(f32[152,16,128]{2,1,0:T(8,128)S(1)} %bitcast.5, f32[24,16,128]{2,1,0:T(8,128)S(1)} %bitcast.8, f32[8,16,128]{2,1,0:T(8,128)S(1)} %copy-done.2, s32[8,16,128]{2,1,0:T(8,128)S(1)} %copy-done.3, f32[384,128]{1,0:T(8,128)S(1)} %collective-permute-done.above, ...), custom_call_target="tpu_custom_call" | custom-call | tf_op jit(solution)/shard_map/three_steps/pallas_call | solution.py:355
  31.2 1.9 %collective-permute-start.5 = (f32[16,16,128]{2,1,0:T(8,128)S(1)}, f32[16,16,128]{2,1,0:T(8,128)S(1)}, u32[]{:S(2)}, u32[]{:S(2)}) collective-permute-start(f32[16,16,128]{2,1,0:T(8,128)S(1)} %get-tuple-element.15.own), channel_id=1, source_target_pairs={{4,0},{8,4},{12,8},{16,12},{20,16},{24,20},{28,24},{5,1},{9,5},{13... | collective-permute-start | bytes 393224 | tf_op jit(solution)/shard_map/ppermute | solution.py:370
  33.1 2.4 %collective-permute-start.4 = (f32[16,16,128]{2,1,0:T(8,128)S(1)}, f32[16,16,128]{2,1,0:T(8,128)S(1)}, u32[]{:S(2)}, u32[]{:S(2)}) collective-permute-start(f32[16,16,128]{2,1,0:T(8,128)S(1)} %get-tuple-element.15.own), channel_id=1, source_target_pairs={{0,4},{4,8},{8,12},{12,16},{16,20},{20,24},{24,28},{1,5},{5,9},{9,... | collective-permute-start | bytes 393224 | tf_op jit(solution)/shard_map/ppermute | solution.py:370
  35.5 0.1 collective-permute-done.5.right
  35.6 4.7 %collective-permute-done.4.left = f32[16,16,128]{2,1,0:T(8,128)S(1)} collective-permute-done((f32[16,16,128]{2,1,0:T(8,128)S(1)}, f32[16,16,128]{2,1,0:T(8,128)S(1)}, u32[]{:S(2)}, u32[]{:S(2)}) %collective-permute-start.4) | collective-permute-done | bytes 131104 | tf_op jit(solution)/shard_map/ppermute | solution.py:370
  40.3 1.9 %collective-permute-start.6 = (f32[48,8,128]{2,1,0:T(8,128)S(1)}, f32[48,8,128]{2,1,0:T(8,128)S(1)}, u32[]{:S(2)}, u32[]{:S(2)}) collective-permute-start(f32[48,8,128]{2,1,0:T(8,128)S(1)} %get-tuple-element.16), channel_id=1, source_target_pairs={{1,0},{2,1},{3,2},{5,4},{6,5},{7,6},{9,8},{10,9},{11,10},{13,12},{... | collective-permute-start | bytes 589832 | tf_op jit(solution)/shard_map/ppermute | solution.py:370
  42.3 3.9 %collective-permute-start.7 = (f32[48,8,128]{2,1,0:T(8,128)S(1)}, f32[48,8,128]{2,1,0:T(8,128)S(1)}, u32[]{:S(2)}, u32[]{:S(2)}) collective-permute-start(f32[48,8,128]{2,1,0:T(8,128)S(1)} %get-tuple-element.17), channel_id=1, source_target_pairs={{0,1},{1,2},{2,3},{4,5},{5,6},{6,7},{8,9},{9,10},{10,11},{12,13},{... | collective-permute-start | bytes 589832 | tf_op jit(solution)/shard_map/ppermute | solution.py:370
  46.2 1.7 %collective-permute-done.6.above = f32[48,8,128]{2,1,0:T(8,128)S(1)} collective-permute-done((f32[48,8,128]{2,1,0:T(8,128)S(1)}, f32[48,8,128]{2,1,0:T(8,128)S(1)}, u32[]{:S(2)}, u32[]{:S(2)}) %collective-permute-start.6) | collective-permute-done | bytes 196640 | tf_op jit(solution)/shard_map/ppermute | solution.py:370
  47.9 1.9 %collective-permute-done.7.below = f32[48,8,128]{2,1,0:T(8,128)S(1)} collective-permute-done((f32[48,8,128]{2,1,0:T(8,128)S(1)}, f32[48,8,128]{2,1,0:T(8,128)S(1)}, u32[]{:S(2)}, u32[]{:S(2)}) %collective-permute-start.7) | collective-permute-done | bytes 196640 | tf_op jit(solution)/shard_map/ppermute | solution.py:370
  49.8 10.6 %eight_sweeps.1 = f32[8,16,128]{2,1,0:T(8,128)} custom-call(f32[16,16,128]{2,1,0:T(8,128)S(1)} %get-tuple-element.15.own, f32[16,16,128]{2,1,0:T(8,128)S(1)} %collective-permute-done.4.left, f32[16,16,128]{2,1,0:T(8,128)S(1)} %collective-permute-done.5.right, f32[48,8,128]{2,1,0:T(8,128)S(1)} %collective-permute-done.6.above, ...), custom_call_target="tpu_custom_call" | custom-call | tf_op jit(solution)/shard_map/eight_sweeps/pallas_call | solution.py:355
  (9 shorter events, 0.0 us)
Async XLA Ops:
  0.6 1.3 %copy-start = (f32[19,8,16,128]{3,2,1,0:T(8,128)S(1)}, f32[19,8,16,128]{3,2,1,0:T(8,128)}, u32[]{:S(2)}) copy-start(f32[19,8,16,128]{3,2,1,0:T(8,128)} %param.6) | copy-start | bytes 3735556
  1.9 0.9 %copy-start.1 = (f32[3,8,16,128]{3,2,1,0:T(8,128)S(1)}, f32[3,8,16,128]{3,2,1,0:T(8,128)}, u32[]{:S(2)}) copy-start(f32[3,8,16,128]{3,2,1,0:T(8,128)} %param.7) | copy-start | bytes 589828
  2.9 0.8 %copy-start.2 = (f32[8,16,128]{2,1,0:T(8,128)S(1)}, f32[8,16,128]{2,1,0:T(8,128)}, u32[]{:S(2)}) copy-start(f32[8,16,128]{2,1,0:T(8,128)} %grad.5) | copy-start | bytes 196612
  3.7 0.8 %copy-start.3 = (s32[8,16,128]{2,1,0:T(8,128)S(1)}, s32[8,16,128]{2,1,0:T(8,128)}, u32[]{:S(2)}) copy-start(s32[8,16,128]{2,1,0:T(8,128)} %fluid.5) | copy-start | bytes 196612
  4.7 21.7 %copy-start.4 = (f32[8,16,128]{2,1,0:T(8,128)S(1)}, f32[8,16,128]{2,1,0:T(8,128)}, u32[]{:S(2)}) copy-start(f32[8,16,128]{2,1,0:T(8,128)} %heat.1) | copy-start | bytes 196612
  4.7 21.7 %copy-start.5 = (s32[8,16,128]{2,1,0:T(8,128)S(1)}, s32[8,16,128]{2,1,0:T(8,128)}, u32[]{:S(2)}) copy-start(s32[8,16,128]{2,1,0:T(8,128)} %span.1) | copy-start | bytes 196612
  4.7 8.7 %collective-permute-start = (f32[384,128]{1,0:T(8,128)S(1)}, f32[384,128]{1,0:T(8,128)S(1)}, u32[]{:S(2)}, u32[]{:S(2)}) collective-permute-start(f32[384,128]{1,0:T(8,128)S(1)} %get-tuple-element.10), channel_id=1, source_target_pairs={{1,0},{2,1},{3,2},{5,4},{6,5},{7,6},{9,8},{10,9},{11,10},{13,12},{... | collective-permute-start | bytes 589832 | tf_op jit(solution)/shard_map/ppermute | solution.py:370
  7.2 8.3 %collective-permute-start.1 = (f32[384,128]{1,0:T(8,128)S(1)}, f32[384,128]{1,0:T(8,128)S(1)}, u32[]{:S(2)}, u32[]{:S(2)}) collective-permute-start(f32[384,128]{1,0:T(8,128)S(1)} %get-tuple-element.11), channel_id=1, source_target_pairs={{0,1},{1,2},{2,3},{4,5},{5,6},{6,7},{8,9},{9,10},{10,11},{12,13},{... | collective-permute-start | bytes 589832 | tf_op jit(solution)/shard_map/ppermute | solution.py:370
  16.1 5.5 %collective-permute-start.2 = (f32[456,128]{1,0:T(8,128)S(1)}, f32[456,128]{1,0:T(8,128)S(1)}, u32[]{:S(2)}, u32[]{:S(2)}) collective-permute-start(f32[456,128]{1,0:T(8,128)S(1)} %get-tuple-element.12), channel_id=1, source_target_pairs={{4,0},{8,4},{12,8},{16,12},{20,16},{24,20},{28,24},{5,1},{9,5},{13... | collective-permute-start | bytes 700424 | tf_op jit(solution)/shard_map/ppermute | solution.py:370
  18.1 8.3 %collective-permute-start.3 = (f32[456,128]{1,0:T(8,128)S(1)}, f32[456,128]{1,0:T(8,128)S(1)}, u32[]{:S(2)}, u32[]{:S(2)}) collective-permute-start(f32[456,128]{1,0:T(8,128)S(1)} %get-tuple-element.13), channel_id=1, source_target_pairs={{0,4},{4,8},{8,12},{12,16},{16,20},{20,24},{24,28},{1,5},{5,9},{9,... | collective-permute-start | bytes 700424 | tf_op jit(solution)/shard_map/ppermute | solution.py:370
  31.2 4.4 %collective-permute-start.5 = (f32[16,16,128]{2,1,0:T(8,128)S(1)}, f32[16,16,128]{2,1,0:T(8,128)S(1)}, u32[]{:S(2)}, u32[]{:S(2)}) collective-permute-start(f32[16,16,128]{2,1,0:T(8,128)S(1)} %get-tuple-element.15.own), channel_id=1, source_target_pairs={{4,0},{8,4},{12,8},{16,12},{20,16},{24,20},{28,24},{5,1},{9,5},{13... | collective-permute-start | bytes 393224 | tf_op jit(solution)/shard_map/ppermute | solution.py:370
  33.1 7.2 %collective-permute-start.4 = (f32[16,16,128]{2,1,0:T(8,128)S(1)}, f32[16,16,128]{2,1,0:T(8,128)S(1)}, u32[]{:S(2)}, u32[]{:S(2)}) collective-permute-start(f32[16,16,128]{2,1,0:T(8,128)S(1)} %get-tuple-element.15.own), channel_id=1, source_target_pairs={{0,4},{4,8},{8,12},{12,16},{16,20},{20,24},{24,28},{1,5},{5,9},{9,... | collective-permute-start | bytes 393224 | tf_op jit(solution)/shard_map/ppermute | solution.py:370
  40.3 7.6 %collective-permute-start.6 = (f32[48,8,128]{2,1,0:T(8,128)S(1)}, f32[48,8,128]{2,1,0:T(8,128)S(1)}, u32[]{:S(2)}, u32[]{:S(2)}) collective-permute-start(f32[48,8,128]{2,1,0:T(8,128)S(1)} %get-tuple-element.16), channel_id=1, source_target_pairs={{1,0},{2,1},{3,2},{5,4},{6,5},{7,6},{9,8},{10,9},{11,10},{13,12},{... | collective-permute-start | bytes 589832 | tf_op jit(solution)/shard_map/ppermute | solution.py:370
  42.3 7.6 %collective-permute-start.7 = (f32[48,8,128]{2,1,0:T(8,128)S(1)}, f32[48,8,128]{2,1,0:T(8,128)S(1)}, u32[]{:S(2)}, u32[]{:S(2)}) collective-permute-start(f32[48,8,128]{2,1,0:T(8,128)S(1)} %get-tuple-element.17), channel_id=1, source_target_pairs={{0,1},{1,2},{2,3},{4,5},{5,6},{6,7},{8,9},{9,10},{10,11},{12,13},{... | collective-permute-start | bytes 589832 | tf_op jit(solution)/shard_map/ppermute | solution.py:370

commit v2 on v1

--- a/solution.py
+++ b/solution.py
@@ -254,7 +254,7 @@
                     target[i * planes + x + 1, pl.ds(at, 8), :] = posts[i]
             return 0
 
-        lax.fori_loop(0, x_size, plane, 0)
+        lax.fori_loop(0, x_size, plane, 0, unroll=True)
         for side, (ref, edge, halo, pops, back) in enumerate(sides):
             for j in range(groups):
                 at = FIRST + 8 * j
@@ -292,7 +292,7 @@
         sens[x_size + x] = span[x].astype(jnp.float32) + 1.0
         return 0
 
-    lax.fori_loop(0, x_size, last, 0)
+    lax.fori_loop(0, x_size, last, 0, unroll=True)
 
 
 def band_kernel(x_size, y_size, own, left, right, low, high):
@@ -324,7 +324,7 @@
                 beta[k, pl.ds(start, count), :] = jnp.where(there > 0.5, r2 * inverse, 0.0)
             return 0
 
-        lax.fori_loop(0, x_size, plane, 0)
+        lax.fori_loop(0, x_size, plane, 0, unroll=True)
 
     for n, ref in enumerate((left, own, right)):
         prepare(n, ref)
@@ -333,21 +333,19 @@
         final = number == SWEEPS
         margin = SWEEPS - number
 
-        def plane(x, _, source=source, target=target, final=final):
-            for j in range(1, 1 + y_size // 8) if final else range(rows // 8):
-                at = PAD + 8 * j
-                middle = source[x, pl.ds(at, 8), :]
-                beside = source[x + 1, pl.ds(at, 8), :] + source[x - 1, pl.ds(at, 8), :]
+        for j in range(1, 1 + y_size // 8) if final else range(rows // 8):
+            at = PAD + 8 * j
+            begin, end = x_size - margin, 2 * x_size + margin
+            column = {x: source[x, pl.ds(at, 8), :] for x in range(begin - 1, end + 1)}
+            for x in range(begin, end):
+                beside = column[x + 1] + column[x - 1]
                 beside = beside + source[x, pl.ds(at + 1, 8), :] + source[x, pl.ds(at - 1, 8), :]
-                beside = beside + lane_pull(middle, 1) + lane_pull(middle, -1)
+                beside = beside + lane_pull(column[x], 1) + lane_pull(column[x], -1)
                 value = given[x, pl.ds(8 * j, 8), :] + beta[x, pl.ds(8 * j, 8), :] * beside
                 if final:
                     filtered[x - x_size, pl.ds(8 * j - REACH, 8), :] = value
                 else:
                     target[x, pl.ds(at, 8), :] = value
-            return 0
-
-        lax.fori_loop(x_size - margin, 2 * x_size + margin, plane, 0)
         source, target = target, source
 
 

time: 61.3 us -> 50.7 us (0.83)
  Pallas kernels: 16.3 us -> 5.64 us
    pallas_call x5, Pallas kernels: 16.3 us -> 5.64 us  [call(): pl.pallas_call(kernel, out_shape=[jax.ShapeDtypeStruct(shape, jnp.float32...]
where the time goes in v2:
time: 50.7 us; the launch traced here: 49.8 us
  starting transfers between devices  20.5 us (40%)
  waiting for transfers between devices  19 us (37%)
  Pallas kernels  5.64 us (11%)
  local copies, waits for them, and re-layouts  3.9 us (8%)
  between operations  0.74 us (1%)
    ppermute x4, waiting for transfers between devices, both_ways(): lax.ppermute(to_next, axis, on)  13.4 us
    ppermute x4, starting transfers between devices, both_ways(): lax.ppermute(to_next, axis, on)  12.2 us
    ppermute x4, starting transfers between devices, both_ways(): lax.ppermute(to_previous, axis, back)  8.24 us
    pallas_call x5, Pallas kernels, call(): pl.pallas_call(kernel, out_shape=[jax.ShapeDtypeStruct(shape, jnp.float32...  5.64 us
    ppermute x4, waiting for transfers between devices, both_ways(): lax.ppermute(to_previous, axis, back)  5.61 us
    unnamed x12, local copies, waits for them, and re-layouts  3.9 us
  transfers between devices with their start and end apart: 8, of which 8 were waited for; matrix products, arithmetic and copies ran while one was open for 0% of the time, Pallas kernels for 0%

profile of v2, /device:TPU:12, one launch (start us, length us, event | category | flops | bytes accessed | tf_op | source)
XLA Modules:
  0.0 49.8 jit_solution(7103401800608023123)
XLA Ops:
  0.6 1.3 %copy-done = f32[19,8,16,128]{3,2,1,0:T(8,128)S(1)} copy-done((f32[19,8,16,128]{3,2,1,0:T(8,128)S(1)}, f32[19,8,16,128]{3,2,1,0:T(8,128)}, u32[]{:S(2)}) %copy-start) | copy-done | bytes 1245208
  1.9 0.9 %copy-done.1 = f32[3,8,16,128]{3,2,1,0:T(8,128)S(1)} copy-done((f32[3,8,16,128]{3,2,1,0:T(8,128)S(1)}, f32[3,8,16,128]{3,2,1,0:T(8,128)}, u32[]{:S(2)}) %copy-start.1) | copy-done | bytes 196632
  2.9 0.8 %copy-done.2 = f32[8,16,128]{2,1,0:T(8,128)S(1)} copy-done((f32[8,16,128]{2,1,0:T(8,128)S(1)}, f32[8,16,128]{2,1,0:T(8,128)}, u32[]{:S(2)}) %copy-start.2) | copy-done | bytes 65560
  3.7 0.8 %copy-done.3 = s32[8,16,128]{2,1,0:T(8,128)S(1)} copy-done((s32[8,16,128]{2,1,0:T(8,128)S(1)}, s32[8,16,128]{2,1,0:T(8,128)}, u32[]{:S(2)}) %copy-start.3) | copy-done | bytes 65560
  4.5 0.1 rim_rows.1
  4.7 2.5 %collective-permute-start = (f32[384,128]{1,0:T(8,128)S(1)}, f32[384,128]{1,0:T(8,128)S(1)}, u32[]{:S(2)}, u32[]{:S(2)}) collective-permute-start(f32[384,128]{1,0:T(8,128)S(1)} %get-tuple-element.10), channel_id=1, source_target_pairs={{1,0},{2,1},{3,2},{5,4},{6,5},{7,6},{9,8},{10,9},{11,10},{13,12},{... | collective-permute-start | bytes 589832 | tf_op jit(solution)/shard_map/ppermute | solution.py:368
  7.2 3.5 %collective-permute-start.1 = (f32[384,128]{1,0:T(8,128)S(1)}, f32[384,128]{1,0:T(8,128)S(1)}, u32[]{:S(2)}, u32[]{:S(2)}) collective-permute-start(f32[384,128]{1,0:T(8,128)S(1)} %get-tuple-element.11), channel_id=1, source_target_pairs={{0,1},{1,2},{2,3},{4,5},{5,6},{6,7},{8,9},{9,10},{10,11},{12,13},{... | collective-permute-start | bytes 589832 | tf_op jit(solution)/shard_map/ppermute | solution.py:368
  10.7 2.7 %collective-permute-done.above = f32[384,128]{1,0:T(8,128)S(1)} collective-permute-done((f32[384,128]{1,0:T(8,128)S(1)}, f32[384,128]{1,0:T(8,128)S(1)}, u32[]{:S(2)}, u32[]{:S(2)}) %collective-permute-start) | collective-permute-done | bytes 196640 | tf_op jit(solution)/shard_map/ppermute | solution.py:368
  13.4 2.1 %collective-permute-done.1.below = f32[384,128]{1,0:T(8,128)S(1)} collective-permute-done((f32[384,128]{1,0:T(8,128)S(1)}, f32[384,128]{1,0:T(8,128)S(1)}, u32[]{:S(2)}, u32[]{:S(2)}) %collective-permute-start.1) | collective-permute-done | bytes 196640 | tf_op jit(solution)/shard_map/ppermute | solution.py:368
  15.5 0.7 %edge_planes.1 = (f32[456,128]{1,0:T(8,128)S(1)}, f32[456,128]{1,0:T(8,128)S(1)}) custom-call(f32[152,16,128]{2,1,0:T(8,128)S(1)} %bitcast.4, f32[24,16,128]{2,1,0:T(8,128)S(1)} %bitcast.7, f32[8,16,128]{2,1,0:T(8,128)S(1)} %copy-done.2, s32[8,16,128]{2,1,0:T(8,128)S(1)} %copy-done.3, f32[384,128]{1,0:T(8,128)S(1)} %collective-permute-done.above, ...), custom_call_target="tpu_custom_call" | custom-call | tf_op jit(solution)/shard_map/edge_planes/pallas_call | solution.py:353
  16.1 1.9 %collective-permute-start.2 = (f32[456,128]{1,0:T(8,128)S(1)}, f32[456,128]{1,0:T(8,128)S(1)}, u32[]{:S(2)}, u32[]{:S(2)}) collective-permute-start(f32[456,128]{1,0:T(8,128)S(1)} %get-tuple-element.12), channel_id=1, source_target_pairs={{4,0},{8,4},{12,8},{16,12},{20,16},{24,20},{28,24},{5,1},{9,5},{13... | collective-permute-start | bytes 700424 | tf_op jit(solution)/shard_map/ppermute | solution.py:368
  18.1 2.4 %collective-permute-start.3 = (f32[456,128]{1,0:T(8,128)S(1)}, f32[456,128]{1,0:T(8,128)S(1)}, u32[]{:S(2)}, u32[]{:S(2)}) collective-permute-start(f32[456,128]{1,0:T(8,128)S(1)} %get-tuple-element.13), channel_id=1, source_target_pairs={{0,4},{4,8},{8,12},{12,16},{16,20},{20,24},{24,28},{1,5},{5,9},{9,... | collective-permute-start | bytes 700424 | tf_op jit(solution)/shard_map/ppermute | solution.py:368
  20.5 1.1 %collective-permute-done.2.from_right = f32[456,128]{1,0:T(8,128)S(1)} collective-permute-done((f32[456,128]{1,0:T(8,128)S(1)}, f32[456,128]{1,0:T(8,128)S(1)}, u32[]{:S(2)}, u32[]{:S(2)}) %collective-permute-start.2) | collective-permute-done | bytes 233504 | tf_op jit(solution)/shard_map/ppermute | solution.py:368
  21.6 4.7 %collective-permute-done.3.from_left = f32[456,128]{1,0:T(8,128)S(1)} collective-permute-done((f32[456,128]{1,0:T(8,128)S(1)}, f32[456,128]{1,0:T(8,128)S(1)}, u32[]{:S(2)}, u32[]{:S(2)}) %collective-permute-start.3) | collective-permute-done | bytes 233504 | tf_op jit(solution)/shard_map/ppermute | solution.py:368
  26.4 3.1 %three_steps.1 = (f32[152,16,128]{2,1,0:T(8,128)}, f32[16,16,128]{2,1,0:T(8,128)S(1)}) custom-call(f32[152,16,128]{2,1,0:T(8,128)S(1)} %bitcast.5, f32[24,16,128]{2,1,0:T(8,128)S(1)} %bitcast.8, f32[8,16,128]{2,1,0:T(8,128)S(1)} %copy-done.2, s32[8,16,128]{2,1,0:T(8,128)S(1)} %copy-done.3, f32[384,128]{1,0:T(8,128)S(1)} %collective-permute-done.above, ...), custom_call_target="tpu_custom_call" | custom-call | tf_op jit(solution)/shard_map/three_steps/pallas_call | solution.py:353
  29.4 1.9 %collective-permute-start.5 = (f32[16,16,128]{2,1,0:T(8,128)S(1)}, f32[16,16,128]{2,1,0:T(8,128)S(1)}, u32[]{:S(2)}, u32[]{:S(2)}) collective-permute-start(f32[16,16,128]{2,1,0:T(8,128)S(1)} %get-tuple-element.15.own), channel_id=1, source_target_pairs={{4,0},{8,4},{12,8},{16,12},{20,16},{24,20},{28,24},{5,1},{9,5},{13... | collective-permute-start | bytes 393224 | tf_op jit(solution)/shard_map/ppermute | solution.py:368
  31.4 2.4 %collective-permute-start.4 = (f32[16,16,128]{2,1,0:T(8,128)S(1)}, f32[16,16,128]{2,1,0:T(8,128)S(1)}, u32[]{:S(2)}, u32[]{:S(2)}) collective-permute-start(f32[16,16,128]{2,1,0:T(8,128)S(1)} %get-tuple-element.15.own), channel_id=1, source_target_pairs={{0,4},{4,8},{8,12},{12,16},{16,20},{20,24},{24,28},{1,5},{5,9},{9,... | collective-permute-start | bytes 393224 | tf_op jit(solution)/shard_map/ppermute | solution.py:368
  33.8 0.1 collective-permute-done.5.right
  33.9 4.7 %collective-permute-done.4.left = f32[16,16,128]{2,1,0:T(8,128)S(1)} collective-permute-done((f32[16,16,128]{2,1,0:T(8,128)S(1)}, f32[16,16,128]{2,1,0:T(8,128)S(1)}, u32[]{:S(2)}, u32[]{:S(2)}) %collective-permute-start.4) | collective-permute-done | bytes 131104 | tf_op jit(solution)/shard_map/ppermute | solution.py:368
  38.6 1.9 %collective-permute-start.6 = (f32[48,8,128]{2,1,0:T(8,128)S(1)}, f32[48,8,128]{2,1,0:T(8,128)S(1)}, u32[]{:S(2)}, u32[]{:S(2)}) collective-permute-start(f32[48,8,128]{2,1,0:T(8,128)S(1)} %get-tuple-element.16), channel_id=1, source_target_pairs={{1,0},{2,1},{3,2},{5,4},{6,5},{7,6},{9,8},{10,9},{11,10},{13,12},{... | collective-permute-start | bytes 589832 | tf_op jit(solution)/shard_map/ppermute | solution.py:368
  40.5 3.9 %collective-permute-start.7 = (f32[48,8,128]{2,1,0:T(8,128)S(1)}, f32[48,8,128]{2,1,0:T(8,128)S(1)}, u32[]{:S(2)}, u32[]{:S(2)}) collective-permute-start(f32[48,8,128]{2,1,0:T(8,128)S(1)} %get-tuple-element.17), channel_id=1, source_target_pairs={{0,1},{1,2},{2,3},{4,5},{5,6},{6,7},{8,9},{9,10},{10,11},{12,13},{... | collective-permute-start | bytes 589832 | tf_op jit(solution)/shard_map/ppermute | solution.py:368
  44.4 1.7 %collective-permute-done.6.above = f32[48,8,128]{2,1,0:T(8,128)S(1)} collective-permute-done((f32[48,8,128]{2,1,0:T(8,128)S(1)}, f32[48,8,128]{2,1,0:T(8,128)S(1)}, u32[]{:S(2)}, u32[]{:S(2)}) %collective-permute-start.6) | collective-permute-done | bytes 196640 | tf_op jit(solution)/shard_map/ppermute | solution.py:368
  46.1 1.9 %collective-permute-done.7.below = f32[48,8,128]{2,1,0:T(8,128)S(1)} collective-permute-done((f32[48,8,128]{2,1,0:T(8,128)S(1)}, f32[48,8,128]{2,1,0:T(8,128)S(1)}, u32[]{:S(2)}, u32[]{:S(2)}) %collective-permute-start.7) | collective-permute-done | bytes 196640 | tf_op jit(solution)/shard_map/ppermute | solution.py:368
  48.1 1.7 %eight_sweeps.1 = f32[8,16,128]{2,1,0:T(8,128)} custom-call(f32[16,16,128]{2,1,0:T(8,128)S(1)} %get-tuple-element.15.own, f32[16,16,128]{2,1,0:T(8,128)S(1)} %collective-permute-done.4.left, f32[16,16,128]{2,1,0:T(8,128)S(1)} %collective-permute-done.5.right, f32[48,8,128]{2,1,0:T(8,128)S(1)} %collective-permute-done.6.above, ...), custom_call_target="tpu_custom_call" | custom-call | tf_op jit(solution)/shard_map/eight_sweeps/pallas_call | solution.py:353
  (9 shorter events, 0.0 us)
Async XLA Ops:
  0.6 1.3 %copy-start = (f32[19,8,16,128]{3,2,1,0:T(8,128)S(1)}, f32[19,8,16,128]{3,2,1,0:T(8,128)}, u32[]{:S(2)}) copy-start(f32[19,8,16,128]{3,2,1,0:T(8,128)} %param.6) | copy-start | bytes 3735556
  1.9 0.9 %copy-start.1 = (f32[3,8,16,128]{3,2,1,0:T(8,128)S(1)}, f32[3,8,16,128]{3,2,1,0:T(8,128)}, u32[]{:S(2)}) copy-start(f32[3,8,16,128]{3,2,1,0:T(8,128)} %param.7) | copy-start | bytes 589828
  2.9 0.8 %copy-start.2 = (f32[8,16,128]{2,1,0:T(8,128)S(1)}, f32[8,16,128]{2,1,0:T(8,128)}, u32[]{:S(2)}) copy-start(f32[8,16,128]{2,1,0:T(8,128)} %grad.5) | copy-start | bytes 196612
  3.7 0.8 %copy-start.3 = (s32[8,16,128]{2,1,0:T(8,128)S(1)}, s32[8,16,128]{2,1,0:T(8,128)}, u32[]{:S(2)}) copy-start(s32[8,16,128]{2,1,0:T(8,128)} %fluid.5) | copy-start | bytes 196612
  4.7 21.7 %copy-start.4 = (f32[8,16,128]{2,1,0:T(8,128)S(1)}, f32[8,16,128]{2,1,0:T(8,128)}, u32[]{:S(2)}) copy-start(f32[8,16,128]{2,1,0:T(8,128)} %heat.1) | copy-start | bytes 196612
  4.7 21.7 %copy-start.5 = (s32[8,16,128]{2,1,0:T(8,128)S(1)}, s32[8,16,128]{2,1,0:T(8,128)}, u32[]{:S(2)}) copy-start(s32[8,16,128]{2,1,0:T(8,128)} %span.1) | copy-start | bytes 196612
  4.7 8.7 %collective-permute-start = (f32[384,128]{1,0:T(8,128)S(1)}, f32[384,128]{1,0:T(8,128)S(1)}, u32[]{:S(2)}, u32[]{:S(2)}) collective-permute-start(f32[384,128]{1,0:T(8,128)S(1)} %get-tuple-element.10), channel_id=1, source_target_pairs={{1,0},{2,1},{3,2},{5,4},{6,5},{7,6},{9,8},{10,9},{11,10},{13,12},{... | collective-permute-start | bytes 589832 | tf_op jit(solution)/shard_map/ppermute | solution.py:368
  7.2 8.3 %collective-permute-start.1 = (f32[384,128]{1,0:T(8,128)S(1)}, f32[384,128]{1,0:T(8,128)S(1)}, u32[]{:S(2)}, u32[]{:S(2)}) collective-permute-start(f32[384,128]{1,0:T(8,128)S(1)} %get-tuple-element.11), channel_id=1, source_target_pairs={{0,1},{1,2},{2,3},{4,5},{5,6},{6,7},{8,9},{9,10},{10,11},{12,13},{... | collective-permute-start | bytes 589832 | tf_op jit(solution)/shard_map/ppermute | solution.py:368
  16.1 5.5 %collective-permute-start.2 = (f32[456,128]{1,0:T(8,128)S(1)}, f32[456,128]{1,0:T(8,128)S(1)}, u32[]{:S(2)}, u32[]{:S(2)}) collective-permute-start(f32[456,128]{1,0:T(8,128)S(1)} %get-tuple-element.12), channel_id=1, source_target_pairs={{4,0},{8,4},{12,8},{16,12},{20,16},{24,20},{28,24},{5,1},{9,5},{13... | collective-permute-start | bytes 700424 | tf_op jit(solution)/shard_map/ppermute | solution.py:368
  18.1 8.3 %collective-permute-start.3 = (f32[456,128]{1,0:T(8,128)S(1)}, f32[456,128]{1,0:T(8,128)S(1)}, u32[]{:S(2)}, u32[]{:S(2)}) collective-permute-start(f32[456,128]{1,0:T(8,128)S(1)} %get-tuple-element.13), channel_id=1, source_target_pairs={{0,4},{4,8},{8,12},{12,16},{16,20},{20,24},{24,28},{1,5},{5,9},{9,... | collective-permute-start | bytes 700424 | tf_op jit(solution)/shard_map/ppermute | solution.py:368
  29.4 4.4 %collective-permute-start.5 = (f32[16,16,128]{2,1,0:T(8,128)S(1)}, f32[16,16,128]{2,1,0:T(8,128)S(1)}, u32[]{:S(2)}, u32[]{:S(2)}) collective-permute-start(f32[16,16,128]{2,1,0:T(8,128)S(1)} %get-tuple-element.15.own), channel_id=1, source_target_pairs={{4,0},{8,4},{12,8},{16,12},{20,16},{24,20},{28,24},{5,1},{9,5},{13... | collective-permute-start | bytes 393224 | tf_op jit(solution)/shard_map/ppermute | solution.py:368
  31.4 7.2 %collective-permute-start.4 = (f32[16,16,128]{2,1,0:T(8,128)S(1)}, f32[16,16,128]{2,1,0:T(8,128)S(1)}, u32[]{:S(2)}, u32[]{:S(2)}) collective-permute-start(f32[16,16,128]{2,1,0:T(8,128)S(1)} %get-tuple-element.15.own), channel_id=1, source_target_pairs={{0,4},{4,8},{8,12},{12,16},{16,20},{20,24},{24,28},{1,5},{5,9},{9,... | collective-permute-start | bytes 393224 | tf_op jit(solution)/shard_map/ppermute | solution.py:368
  38.6 7.6 %collective-permute-start.6 = (f32[48,8,128]{2,1,0:T(8,128)S(1)}, f32[48,8,128]{2,1,0:T(8,128)S(1)}, u32[]{:S(2)}, u32[]{:S(2)}) collective-permute-start(f32[48,8,128]{2,1,0:T(8,128)S(1)} %get-tuple-element.16), channel_id=1, source_target_pairs={{1,0},{2,1},{3,2},{5,4},{6,5},{7,6},{9,8},{10,9},{11,10},{13,12},{... | collective-permute-start | bytes 589832 | tf_op jit(solution)/shard_map/ppermute | solution.py:368
  40.5 7.6 %collective-permute-start.7 = (f32[48,8,128]{2,1,0:T(8,128)S(1)}, f32[48,8,128]{2,1,0:T(8,128)S(1)}, u32[]{:S(2)}, u32[]{:S(2)}) collective-permute-start(f32[48,8,128]{2,1,0:T(8,128)S(1)} %get-tuple-element.17), channel_id=1, source_target_pairs={{0,1},{1,2},{2,3},{4,5},{5,6},{6,7},{8,9},{9,10},{10,11},{12,13},{... | collective-permute-start | bytes 589832 | tf_op jit(solution)/shard_map/ppermute | solution.py:368

commit v3 on v2

--- a/solution.py
+++ b/solution.py
@@ -42,14 +42,29 @@
 EDGES = 19
 
 
-def rim_entries(sign):
+def rim_entries():
     entries = [(0, i, 1) for i in range(POPS)]
-    entries += [(0, i, 2) for i in range(POPS) if VELOCITIES[i][1] != -sign]
-    entries += [(0, i, 3) for i in range(POPS) if VELOCITIES[i][1] == sign]
+    entries += [(0, i, 2) for i in range(POPS) if VELOCITIES[i][1] != -1]
+    entries += [(0, i, 3) for i in range(POPS) if VELOCITIES[i][1] == 1]
     for distance in (1, 2):
         entries += [(1, i, distance) for i in range(3)]
         entries += [(2, 0, distance), (3, 0, distance)]
     return entries
+
+
+def mirrored(i, axis):
+    velocity = list(VELOCITIES[i])
+    velocity[axis] = -velocity[axis]
+    return VELOCITIES.index(tuple(velocity))
+
+
+def pick(condition, a, b):
+    return a if a == b else jnp.where(condition, a, b)
+
+
+def toward_next(axis):
+    even = lax.axis_index(axis) % 2 == 0
+    return even, jnp.logical_not(even)
 
 
 def lane_pull(v, cz):
@@ -109,7 +124,7 @@
     return {i: keep * p[i] + terms[MULTIPLE[i]] for i in pops}
 
 
-def extend(x_size, y_size, dual, vel, grad, fluid, above, below, state, coef):
+def extend(x_size, y_size, dual, vel, grad, fluid, messages, state, coef):
     pitch = y_size + 2 * PAD
     planes = x_size + 2
     lanes = dual.shape[-1]
@@ -121,15 +136,19 @@
         return 0
 
     lax.fori_loop(0, POPS, copy_own, 0)
-    rows = {}
-    for sign, ref in ((1, above), (-1, below)):
-        for k, (kind, i, distance) in enumerate(rim_entries(sign)):
-            at = PAD + (y_size - 1 + distance if sign == 1 else -distance)
+    rows = []
+    for after, ref in zip(toward_next("blk"), messages):
+        places = {d: jnp.where(after, PAD + y_size - 1 + d, PAD - d) for d in (1, 2, 3)}
+        side = {}
+        for k, (kind, i, distance) in enumerate(rim_entries()):
             value = ref[pl.ds(k * x_size, x_size), :]
             if kind == 0:
-                flat[pl.ds((i * planes + 1) * pitch + at, x_size, stride=pitch), :] = value
+                pop = pick(after, i, mirrored(i, 1))
+                at = (pop * planes + 1) * pitch + places[distance]
+                flat[pl.ds(at, x_size, stride=pitch), :] = value
             else:
-                rows[(kind, i, at)] = value
+                side[(kind, i, distance)] = value
+        rows += [(places[d], [side[key, n, d] for key, n in ((2, 0), (1, 0), (1, 1), (1, 2), (3, 0))]) for d in (1, 2)]
     coef_flat = coef.reshape(coef.shape[0] * pitch, lanes)
 
     def coefficients(there, ux, uy, uz, g):
@@ -148,31 +167,34 @@
         return 0
 
     lax.fori_loop(0, x_size, own_coefficients, 0)
-    for at in sorted({key[2] for key in rows}):
-        values = coefficients(rows[(2, 0, at)], *(rows[(1, n, at)] for n in range(3)), rows[(3, 0, at)])
-        for n, value in enumerate(values):
+    for at, values in rows:
+        for n, value in enumerate(coefficients(*values)):
             coef_flat[pl.ds(n * x_size * pitch + at, x_size, stride=pitch), :] = value
 
 
-def rim_kernel(x_size, y_size, dual, vel, grad, fluid, low, high):
+def rim_kernel(x_size, y_size, dual, vel, grad, fluid, *messages):
     lanes = dual.shape[-1]
     flat = [ref.reshape(ref.shape[0] * y_size, lanes) for ref in (dual, vel, fluid, grad)]
-    for sign, out in ((1, low), (-1, high)):
-        for k, (kind, i, distance) in enumerate(rim_entries(sign)):
-            row = distance - 1 if sign == 1 else y_size - distance
-            value = flat[kind][pl.ds(i * x_size * y_size + row, x_size, stride=y_size), :]
+    for after, out in zip(toward_next("blk"), messages):
+        for k, (kind, i, distance) in enumerate(rim_entries()):
+            row = jnp.where(after, y_size - distance, distance - 1)
+            field = pick(after, mirrored(i, 1), i) if kind == 0 else i
+            value = flat[kind][pl.ds(field * x_size * y_size + row, x_size, stride=y_size), :]
             if kind == 2:
                 value = value.astype(jnp.float32) + 1.0
             out[pl.ds(k * x_size, x_size), :] = value
 
 
-def edge_kernel(x_size, y_size, dual, vel, grad, fluid, above, below, to_left, to_right, state, coef, near, far):
-    extend(x_size, y_size, dual, vel, grad, fluid, above, below, state, coef)
+def edge_kernel(x_size, y_size, dual, vel, grad, fluid, rim_a, rim_b, edge_a, edge_b, state, coef, near, far):
+    extend(x_size, y_size, dual, vel, grad, fluid, (rim_a, rim_b), state, coef)
     planes = x_size + 2
     window = y_size + 8
     groups = window // 8
-    for out, plane, inward, pops in ((to_left, 0, 1, RIGHT), (to_right, x_size - 1, -1, LEFT)):
-        known = pops + LEVEL
+    known = RIGHT + LEVEL
+    for after, out in zip(toward_next("grp"), (edge_a, edge_b)):
+        inward = jnp.where(after, -1, 1)
+        plane = jnp.where(after, x_size - 1, 0)
+        turn = jnp.where(after, -1.0, 1.0)
 
         def coefs(x, at):
             return [coef[n * x_size + x, pl.ds(at, 8), :] for n in range(6)]
@@ -180,59 +202,66 @@
         def read_state(x, at):
             def read(i):
                 cx, cy, _ = VELOCITIES[i]
-                return state[i * planes + x + 1 + cx, pl.ds(at + cy, 8), :]
+                pop = pick(after, mirrored(i, 0), i)
+                return state[pop * planes + x + 1 + cx * inward, pl.ds(at + cy, 8), :]
 
             return read
 
         for j in range(groups):
             at = FIRST + 8 * j
             keep, rate, *u, source = coefs(plane, at)
-            for n, i in enumerate(pops):
-                out[pl.ds(n * window + 8 * j, 8), :] = state[i * planes + plane + 1, pl.ds(at, 8), :]
+            for n, i in enumerate(RIGHT):
+                pop = pick(after, mirrored(i, 0), i)
+                out[pl.ds(n * window + 8 * j, 8), :] = state[pop * planes + plane + 1, pl.ds(at, 8), :]
             for n, value in enumerate((rate, *u)):
                 out[pl.ds((15 + n) * window + 8 * j, 8), :] = value
+            u[0] = turn * u[0]
             p = pulled_from(read_state(plane, at), known)
             _, equilib = relaxed(p, u)
             posts = posts_of(p, keep, equilib, rate, source, known)
-            for n, i in enumerate(pops):
+            for n, i in enumerate(RIGHT):
                 out[pl.ds((5 + n) * window + 8 * j, 8), :] = posts[i]
             for n, i in enumerate(LEVEL):
                 near[n, pl.ds(at, 8), :] = posts[i]
             keep, rate, *u, source = coefs(plane + inward, at)
+            u[0] = turn * u[0]
             p = pulled_from(read_state(plane + inward, at), range(POPS))
             _, equilib = relaxed(p, u)
-            posts = posts_of(p, keep, equilib, rate, source, pops)
-            for n, i in enumerate(pops):
+            posts = posts_of(p, keep, equilib, rate, source, RIGHT)
+            for n, i in enumerate(RIGHT):
                 far[n, pl.ds(at, 8), :] = posts[i]
         for j in range(groups):
             at = FIRST + 8 * j
             keep, rate, *u, source = coefs(plane, at)
+            u[0] = turn * u[0]
 
             def read(i):
-                ref, n = (far, pops.index(i)) if i in pops else (near, LEVEL.index(i))
+                ref, n = (far, RIGHT.index(i)) if i in RIGHT else (near, LEVEL.index(i))
                 return ref[n, pl.ds(at + VELOCITIES[i][1], 8), :]
 
             p = pulled_from(read, known)
             _, equilib = relaxed(p, u)
-            posts = posts_of(p, keep, equilib, rate, source, pops)
-            for n, i in enumerate(pops):
+            posts = posts_of(p, keep, equilib, rate, source, RIGHT)
+            for n, i in enumerate(RIGHT):
                 out[pl.ds((10 + n) * window + 8 * j, 8), :] = posts[i]
 
 
 def steps_kernel(
-    x_size, y_size, dual, vel, grad, fluid, above, below, heat, span, from_right, from_left,
+    x_size, y_size, dual, vel, grad, fluid, rim_a, rim_b, heat, span, edge_a, edge_b,
     adjoint, sens, state, later, coef, shifts, extra,
 ):
-    extend(x_size, y_size, dual, vel, grad, fluid, above, below, state, coef)
+    extend(x_size, y_size, dual, vel, grad, fluid, (rim_a, rim_b), state, coef)
     planes = x_size + 2
     window = y_size + 8
     groups = window // 8
-    sides = ((from_right, x_size - 1, x_size + 1, RIGHT, LEFT), (from_left, 0, 0, LEFT, RIGHT))
-
-    for ref, _, halo, pops, _ in sides:
-        for n, i in enumerate(pops):
+    sides = tuple(zip(toward_next("grp"), (edge_a, edge_b)))
+
+    for after, ref in sides:
+        halo = jnp.where(after, x_size + 1, 0)
+        for n, i in enumerate(RIGHT):
+            pop = pick(after, i, mirrored(i, 0))
             for j in range(groups):
-                state[i * planes + halo, pl.ds(FIRST + 8 * j, 8), :] = ref[pl.ds(n * window + 8 * j, 8), :]
+                state[pop * planes + halo, pl.ds(FIRST + 8 * j, 8), :] = ref[pl.ds(n * window + 8 * j, 8), :]
 
     def read_from(source, x, at):
         def read(i):
@@ -255,23 +284,27 @@
             return 0
 
         lax.fori_loop(0, x_size, plane, 0, unroll=True)
-        for side, (ref, edge, halo, pops, back) in enumerate(sides):
+        for side, (after, ref) in enumerate(sides):
+            halo = jnp.where(after, x_size + 1, 0)
+            edge = jnp.where(after, x_size, 1)
+            turn = jnp.where(after, 1.0, -1.0)
             for j in range(groups):
                 at = FIRST + 8 * j
                 rate, *u = [ref[pl.ds((15 + n) * window + 8 * j, 8), :] for n in range(4)]
+                u[0] = turn * u[0]
 
                 def read(i):
                     cy = VELOCITIES[i][1]
-                    if i in back:
-                        return source[i * planes + edge + 1, pl.ds(at + cy, 8), :]
+                    if i in LEFT:
+                        return source[pick(after, i, mirrored(i, 0)) * planes + edge, pl.ds(at + cy, 8), :]
                     return extra[side, pl.ds(at + cy, 8), :]
 
-                p = pulled_from(read, back if number == 1 else back + LEVEL)
+                p = pulled_from(read, LEFT if number == 1 else LEFT + LEVEL)
                 added = rate * relaxed(p, u)[1]
                 if number == 1:
                     extra[side, pl.ds(at, 8), :] = added
-                for n, i in enumerate(pops):
-                    target[i * planes + halo, pl.ds(at, 8), :] = (
+                for n, i in enumerate(RIGHT):
+                    target[pick(after, i, mirrored(i, 0)) * planes + halo, pl.ds(at, 8), :] = (
                         ref[pl.ds((5 * number + n) * window + 8 * j, 8), :] + added
                     )
 
@@ -295,39 +328,35 @@
     lax.fori_loop(0, x_size, last, 0, unroll=True)
 
 
-def band_kernel(x_size, y_size, own, left, right, low, high):
-    for kind in range(2):
-        for n, ref in enumerate((left, own, right)):
-            for x in range(x_size):
-                k = kind * 3 * x_size + n * x_size + x
-                low[k] = ref[kind * x_size + x, pl.ds(0, REACH), :]
-                high[k] = ref[kind * x_size + x, pl.ds(y_size - REACH, REACH), :]
-
-
-def filter_kernel(x_size, y_size, own, left, right, above, below, filtered, first, second, given, beta):
+def band_kernel(x_size, y_size, own, beside_a, beside_b, band_a, band_b):
+    bases = [x_size] + [jnp.where(after, 2 * x_size, 0) for after in toward_next("grp")]
+    for after, out in zip(toward_next("blk"), (band_a, band_b)):
+        start = pl.multiple_of(jnp.where(after, y_size - REACH, 0), 8)
+        for kind in range(2):
+            for base, ref in zip(bases, (own, beside_a, beside_b)):
+                for x in range(x_size):
+                    out[kind * 3 * x_size + base + x] = ref[kind * x_size + x, pl.ds(start, REACH), :]
+
+
+def filter_kernel(x_size, y_size, own, beside_a, beside_b, band_a, band_b, filtered, first, second, given, beta):
     wide = 3 * x_size
     rows = y_size + 2 * REACH
 
-    def prepare(n, ref):
-        def plane(x, _):
-            k = n * x_size + x
-            parts = (
-                (0, REACH, below[k], below[wide + k]),
-                (REACH, y_size, ref[x], ref[x_size + x]),
-                (REACH + y_size, REACH, above[k], above[wide + k]),
-            )
-            for start, count, s, there in parts:
-                r2 = jnp.where(there < 1.5, 0.25, jnp.where(there < 2.5, 1.0, jnp.where(there < 3.5, 4.0, 16.0)))
-                inverse = 1.0 / (1.0 + 6.0 * r2)
-                first[k, pl.ds(PAD + start, count), :] = s
-                given[k, pl.ds(start, count), :] = s * inverse
-                beta[k, pl.ds(start, count), :] = jnp.where(there > 0.5, r2 * inverse, 0.0)
-            return 0
-
-        lax.fori_loop(0, x_size, plane, 0, unroll=True)
-
-    for n, ref in enumerate((left, own, right)):
-        prepare(n, ref)
+    def prepare(k, start, count, s, there):
+        r2 = jnp.where(there < 1.5, 0.25, jnp.where(there < 2.5, 1.0, jnp.where(there < 3.5, 4.0, 16.0)))
+        inverse = 1.0 / (1.0 + 6.0 * r2)
+        first[k, pl.ds(pl.multiple_of(PAD + start, 8), count), :] = s
+        given[k, pl.ds(start, count), :] = s * inverse
+        beta[k, pl.ds(start, count), :] = jnp.where(there > 0.5, r2 * inverse, 0.0)
+
+    bases = [x_size] + [jnp.where(after, 2 * x_size, 0) for after in toward_next("grp")]
+    for base, ref in zip(bases, (own, beside_a, beside_b)):
+        for x in range(x_size):
+            prepare(base + x, REACH, y_size, ref[x], ref[x_size + x])
+    for after, ref in zip(toward_next("blk"), (band_a, band_b)):
+        start = pl.multiple_of(jnp.where(after, REACH + y_size, 0), 8)
+        for k in range(wide):
+            prepare(k, start, REACH, ref[k], ref[wide + k])
     source, target = first, second
     for number in range(1, SWEEPS + 1):
         final = number == SWEEPS
@@ -361,11 +390,13 @@
     )(*args)
 
 
-def both_ways(axis, to_previous, to_next):
+def swapped(axis, message_a, message_b):
     size = lax.axis_size(axis)
-    on = [(i, i + 1) for i in range(size - 1)]
-    back = [(i + 1, i) for i in range(size - 1)]
-    return lax.ppermute(to_previous, axis, back), lax.ppermute(to_next, axis, on)
+    received = []
+    for begin, message in ((0, message_a), (1, message_b)):
+        pairs = [(i, i + 1) for i in range(begin, size - 1, 2)]
+        received.append(lax.ppermute(message, axis, pairs + [(j, i) for i, j in pairs]))
+    return received
 
 
 def on_device(dual_populace, forward_motion_vector, forward_heat_level, objective_heat_gradient, liquid_indicator,
@@ -375,43 +406,39 @@
     dual = dual_populace.reshape(POPS * x_size, y_size, lanes)
     vel = forward_motion_vector.reshape(3 * x_size, y_size, lanes)
     fields = (dual, vel, objective_heat_gradient, liquid_indicator)
-    rim = (len(rim_entries(1)) * x_size, lanes)
+    rim = (len(rim_entries()) * x_size, lanes)
     edge = (EDGES * window, lanes)
     state = (POPS * planes, pitch, lanes)
     coef = (6 * x_size, pitch, lanes)
 
-    low, high = call(
-        functools.partial(rim_kernel, x_size, y_size), [rim, rim], [], fields, "rim_rows"
-    )
-    above, below = both_ways("blk", low, high)
-    to_left, to_right = call(
+    rims = call(functools.partial(rim_kernel, x_size, y_size), [rim, rim], [], fields, "rim_rows")
+    rims = swapped("blk", *rims)
+    edges = call(
         functools.partial(edge_kernel, x_size, y_size),
         [edge, edge],
         [state, coef, (len(LEVEL), pitch, lanes), (len(RIGHT), pitch, lanes)],
-        (*fields, above, below),
+        (*fields, *rims),
         "edge_planes",
     )
-    from_right, from_left = both_ways("grp", to_left, to_right)
+    edges = swapped("grp", *edges)
     adjoint, sens = call(
         functools.partial(steps_kernel, x_size, y_size),
         [(POPS * x_size, y_size, lanes), (2 * x_size, y_size, lanes)],
         [state, state, coef, (2 * x_size, pitch, lanes), (2, pitch, lanes)],
-        (*fields, above, below, forward_heat_level, filter_span_group, from_right, from_left),
+        (*fields, *rims, forward_heat_level, filter_span_group, *edges),
         "three_steps",
     )
-    right, left = both_ways("grp", sens, sens)
+    beside = swapped("grp", sens, sens)
     band = (6 * x_size, REACH, lanes)
-    low, high = call(
-        functools.partial(band_kernel, x_size, y_size), [band, band], [], (sens, left, right), "band_rows"
-    )
-    above, below = both_ways("blk", low, high)
+    bands = call(functools.partial(band_kernel, x_size, y_size), [band, band], [], (sens, *beside), "band_rows")
+    bands = swapped("blk", *bands)
     wide = 3 * x_size
     rows = y_size + 2 * REACH
     (filtered,) = call(
         functools.partial(filter_kernel, x_size, y_size),
         [(x_size, y_size, lanes)],
         [(wide, rows + 2 * PAD, lanes)] * 2 + [(wide, rows, lanes)] * 2,
-        (sens, left, right, above, below),
+        (sens, *beside, *bands),
         "eight_sweeps",
     )
     return adjoint.reshape(dual_populace.shape), filtered

time: 50.7 us -> 46.5 us (0.917)
  starting transfers between devices: 20.5 us -> 15.5 us
  waiting for transfers between devices: 19 us -> 19.8 us
    ppermute x8, starting transfers between devices: 20.5 us -> 15.5 us  [swapped(): lax.ppermute(message, axis, pairs + [(j, i) for i, j in pairs])]
    ppermute x8, waiting for transfers between devices: 19 us -> 19.8 us  [swapped(): lax.ppermute(message, axis, pairs + [(j, i) for i, j in pairs])]
  transfers between devices with their start and end apart: 8 -> 8, of which waited for: 8 -> 6; matrix products, arithmetic and copies ran while one was open for 0% -> 0% of each run, Pallas kernels for 0% -> 0%
where the time goes in v3:
time: 46.5 us; the launch traced here: 45.9 us
  waiting for transfers between devices  19.8 us (43%)
  starting transfers between devices  15.5 us (33%)
  Pallas kernels  6.04 us (13%)
  local copies, waits for them, and re-layouts  3.9 us (8%)
  between operations  0.74 us (2%)
    ppermute x8, waiting for transfers between devices, swapped(): lax.ppermute(message, axis, pairs + [(j, i) for i, j in pairs])  19.8 us
    ppermute x8, starting transfers between devices, swapped(): lax.ppermute(message, axis, pairs + [(j, i) for i, j in pairs])  15.5 us
    pallas_call x5, Pallas kernels, call(): pl.pallas_call(kernel, out_shape=[jax.ShapeDtypeStruct(shape, jnp.float32...  6.04 us
    unnamed x12, local copies, waits for them, and re-layouts  3.9 us
  transfers between devices with their start and end apart: 8, of which 6 were waited for; matrix products, arithmetic and copies ran while one was open for 0% of the time, Pallas kernels for 0%

profile of v3, /device:TPU:12, one launch (start us, length us, event | category | flops | bytes accessed | tf_op | source)
XLA Modules:
  0.0 45.9 jit_solution(6862296309078534401)
XLA Ops:
  0.6 1.3 %copy-done = f32[19,8,16,128]{3,2,1,0:T(8,128)S(1)} copy-done((f32[19,8,16,128]{3,2,1,0:T(8,128)S(1)}, f32[19,8,16,128]{3,2,1,0:T(8,128)}, u32[]{:S(2)}) %copy-start) | copy-done | bytes 1245208
  1.9 0.9 %copy-done.1 = f32[3,8,16,128]{3,2,1,0:T(8,128)S(1)} copy-done((f32[3,8,16,128]{3,2,1,0:T(8,128)S(1)}, f32[3,8,16,128]{3,2,1,0:T(8,128)}, u32[]{:S(2)}) %copy-start.1) | copy-done | bytes 196632
  2.9 0.8 %copy-done.2 = f32[8,16,128]{2,1,0:T(8,128)S(1)} copy-done((f32[8,16,128]{2,1,0:T(8,128)S(1)}, f32[8,16,128]{2,1,0:T(8,128)}, u32[]{:S(2)}) %copy-start.2) | copy-done | bytes 65560
  3.7 0.8 %copy-done.3 = s32[8,16,128]{2,1,0:T(8,128)S(1)} copy-done((s32[8,16,128]{2,1,0:T(8,128)S(1)}, s32[8,16,128]{2,1,0:T(8,128)}, u32[]{:S(2)}) %copy-start.3) | copy-done | bytes 65560
  4.5 0.2 rim_rows.1
  4.7 0.0 copy-start.4
  4.8 0.0 copy-start.5
  4.8 0.5 %collective-permute-start = (f32[384,128]{1,0:T(8,128)S(1)}, f32[384,128]{1,0:T(8,128)S(1)}, u32[]{:S(2)}, u32[]{:S(2)}) collective-permute-start(f32[384,128]{1,0:T(8,128)S(1)} %get-tuple-element.10), channel_id=1, source_target_pairs={{0,1},{2,3},{1,0},{3,2},{4,5},{6,7},{5,4},{7,6},{8,9},{10,11},{9,8... | collective-permute-start | bytes 589832 | tf_op jit(solution)/shard_map/ppermute | solution.py:398
  5.3 4.6 %collective-permute-start.1 = (f32[384,128]{1,0:T(8,128)S(1)}, f32[384,128]{1,0:T(8,128)S(1)}, u32[]{:S(2)}, u32[]{:S(2)}) collective-permute-start(f32[384,128]{1,0:T(8,128)S(1)} %get-tuple-element.11), channel_id=1, source_target_pairs={{1,2},{2,1},{5,6},{6,5},{9,10},{10,9},{13,14},{14,13},{17,18},{18,... | collective-permute-start | bytes 589832 | tf_op jit(solution)/shard_map/ppermute | solution.py:398
  9.9 1.6 %collective-permute-done.rim_a = f32[384,128]{1,0:T(8,128)S(1)} collective-permute-done((f32[384,128]{1,0:T(8,128)S(1)}, f32[384,128]{1,0:T(8,128)S(1)}, u32[]{:S(2)}, u32[]{:S(2)}) %collective-permute-start) | collective-permute-done | bytes 196640 | tf_op jit(solution)/shard_map/ppermute | solution.py:398
  11.5 3.0 %collective-permute-done.1.rim_b = f32[384,128]{1,0:T(8,128)S(1)} collective-permute-done((f32[384,128]{1,0:T(8,128)S(1)}, f32[384,128]{1,0:T(8,128)S(1)}, u32[]{:S(2)}, u32[]{:S(2)}) %collective-permute-start.1) | collective-permute-done | bytes 196640 | tf_op jit(solution)/shard_map/ppermute | solution.py:398
  14.5 0.9 %edge_planes.1 = (f32[456,128]{1,0:T(8,128)S(1)}, f32[456,128]{1,0:T(8,128)S(1)}) custom-call(f32[152,16,128]{2,1,0:T(8,128)S(1)} %bitcast.4, f32[24,16,128]{2,1,0:T(8,128)S(1)} %bitcast.7, f32[8,16,128]{2,1,0:T(8,128)S(1)} %copy-done.2, s32[8,16,128]{2,1,0:T(8,128)S(1)} %copy-done.3, f32[384,128]{1,0:T(8,128)S(1)} %collective-permute-done.rim_a, ...), custom_call_target="tpu_custom_call" | custom-call | tf_op jit(solution)/shard_map/edge_planes/pallas_call | solution.py:382
  15.4 0.1 collective-permute-start.2
  15.4 3.4 %collective-permute-start.3 = (f32[456,128]{1,0:T(8,128)S(1)}, f32[456,128]{1,0:T(8,128)S(1)}, u32[]{:S(2)}, u32[]{:S(2)}) collective-permute-start(f32[456,128]{1,0:T(8,128)S(1)} %get-tuple-element.13), channel_id=1, source_target_pairs={{4,8},{12,16},{20,24},{8,4},{16,12},{24,20},{5,9},{13,17},{21,25},... | collective-permute-start | bytes 700424 | tf_op jit(solution)/shard_map/ppermute | solution.py:398
  18.9 7.0 %collective-permute-done.3.edge_b = f32[456,128]{1,0:T(8,128)S(1)} collective-permute-done((f32[456,128]{1,0:T(8,128)S(1)}, f32[456,128]{1,0:T(8,128)S(1)}, u32[]{:S(2)}, u32[]{:S(2)}) %collective-permute-start.3) | collective-permute-done | bytes 233504 | tf_op jit(solution)/shard_map/ppermute | solution.py:398
  25.9 3.1 %three_steps.1 = (f32[152,16,128]{2,1,0:T(8,128)}, f32[16,16,128]{2,1,0:T(8,128)S(1)}) custom-call(f32[152,16,128]{2,1,0:T(8,128)S(1)} %bitcast.5, f32[24,16,128]{2,1,0:T(8,128)S(1)} %bitcast.8, f32[8,16,128]{2,1,0:T(8,128)S(1)} %copy-done.2, s32[8,16,128]{2,1,0:T(8,128)S(1)} %copy-done.3, f32[384,128]{1,0:T(8,128)S(1)} %collective-permute-done.rim_a, ...), custom_call_target="tpu_custom_call" | custom-call | tf_op jit(solution)/shard_map/three_steps/pallas_call | solution.py:382
  29.0 3.1 %collective-permute-start.5 = (f32[16,16,128]{2,1,0:T(8,128)S(1)}, f32[16,16,128]{2,1,0:T(8,128)S(1)}, u32[]{:S(2)}, u32[]{:S(2)}) collective-permute-start(f32[16,16,128]{2,1,0:T(8,128)S(1)} %get-tuple-element.15.own), channel_id=1, source_target_pairs={{4,8},{12,16},{20,24},{8,4},{16,12},{24,20},{5,9},{13,17},{21,25},... | collective-permute-start | bytes 393224 | tf_op jit(solution)/shard_map/ppermute | solution.py:398
  32.2 0.1 collective-permute-start.4
  32.2 4.2 %collective-permute-done.5.beside_b = f32[16,16,128]{2,1,0:T(8,128)S(1)} collective-permute-done((f32[16,16,128]{2,1,0:T(8,128)S(1)}, f32[16,16,128]{2,1,0:T(8,128)S(1)}, u32[]{:S(2)}, u32[]{:S(2)}) %collective-permute-start.5) | collective-permute-done | bytes 131104 | tf_op jit(solution)/shard_map/ppermute | solution.py:398
  36.5 0.1 collective-permute-start.6
  36.5 3.6 %collective-permute-start.7 = (f32[48,8,128]{2,1,0:T(8,128)S(1)}, f32[48,8,128]{2,1,0:T(8,128)S(1)}, u32[]{:S(2)}, u32[]{:S(2)}) collective-permute-start(f32[48,8,128]{2,1,0:T(8,128)S(1)} %get-tuple-element.17), channel_id=1, source_target_pairs={{1,2},{2,1},{5,6},{6,5},{9,10},{10,9},{13,14},{14,13},{17,18},{18,... | collective-permute-start | bytes 589832 | tf_op jit(solution)/shard_map/ppermute | solution.py:398
  40.2 2.0 %collective-permute-done.6.band_a = f32[48,8,128]{2,1,0:T(8,128)S(1)} collective-permute-done((f32[48,8,128]{2,1,0:T(8,128)S(1)}, f32[48,8,128]{2,1,0:T(8,128)S(1)}, u32[]{:S(2)}, u32[]{:S(2)}) %collective-permute-start.6) | collective-permute-done | bytes 196640 | tf_op jit(solution)/shard_map/ppermute | solution.py:398
  42.2 1.9 %collective-permute-done.7.band_b = f32[48,8,128]{2,1,0:T(8,128)S(1)} collective-permute-done((f32[48,8,128]{2,1,0:T(8,128)S(1)}, f32[48,8,128]{2,1,0:T(8,128)S(1)}, u32[]{:S(2)}, u32[]{:S(2)}) %collective-permute-start.7) | collective-permute-done | bytes 196640 | tf_op jit(solution)/shard_map/ppermute | solution.py:398
  44.1 1.8 %eight_sweeps.1 = f32[8,16,128]{2,1,0:T(8,128)} custom-call(f32[16,16,128]{2,1,0:T(8,128)S(1)} %get-tuple-element.15.own, f32[16,16,128]{2,1,0:T(8,128)S(1)} %collective-permute-done.4.beside_a, f32[16,16,128]{2,1,0:T(8,128)S(1)} %collective-permute-done.5.beside_b, f32[48,8,128]{2,1,0:T(8,128)S(1)} %collective-permute-done.6.band_a, ...), custom_call_target="tpu_custom_call" | custom-call | tf_op jit(solution)/shard_map/eight_sweeps/pallas_call | solution.py:382
  (9 shorter events, 0.0 us)
Async XLA Ops:
  0.6 1.3 %copy-start = (f32[19,8,16,128]{3,2,1,0:T(8,128)S(1)}, f32[19,8,16,128]{3,2,1,0:T(8,128)}, u32[]{:S(2)}) copy-start(f32[19,8,16,128]{3,2,1,0:T(8,128)} %param.6) | copy-start | bytes 3735556
  1.9 0.9 %copy-start.1 = (f32[3,8,16,128]{3,2,1,0:T(8,128)S(1)}, f32[3,8,16,128]{3,2,1,0:T(8,128)}, u32[]{:S(2)}) copy-start(f32[3,8,16,128]{3,2,1,0:T(8,128)} %param.7) | copy-start | bytes 589828
  2.9 0.8 %copy-start.2 = (f32[8,16,128]{2,1,0:T(8,128)S(1)}, f32[8,16,128]{2,1,0:T(8,128)}, u32[]{:S(2)}) copy-start(f32[8,16,128]{2,1,0:T(8,128)} %grad.5) | copy-start | bytes 196612
  3.7 0.8 %copy-start.3 = (s32[8,16,128]{2,1,0:T(8,128)S(1)}, s32[8,16,128]{2,1,0:T(8,128)}, u32[]{:S(2)}) copy-start(s32[8,16,128]{2,1,0:T(8,128)} %fluid.5) | copy-start | bytes 196612
  4.7 21.2 %copy-start.4 = (f32[8,16,128]{2,1,0:T(8,128)S(1)}, f32[8,16,128]{2,1,0:T(8,128)}, u32[]{:S(2)}) copy-start(f32[8,16,128]{2,1,0:T(8,128)} %heat.1) | copy-start | bytes 196612
  4.8 21.2 %copy-start.5 = (s32[8,16,128]{2,1,0:T(8,128)S(1)}, s32[8,16,128]{2,1,0:T(8,128)}, u32[]{:S(2)}) copy-start(s32[8,16,128]{2,1,0:T(8,128)} %span.1) | copy-start | bytes 196612
  4.8 6.7 %collective-permute-start = (f32[384,128]{1,0:T(8,128)S(1)}, f32[384,128]{1,0:T(8,128)S(1)}, u32[]{:S(2)}, u32[]{:S(2)}) collective-permute-start(f32[384,128]{1,0:T(8,128)S(1)} %get-tuple-element.10), channel_id=1, source_target_pairs={{0,1},{2,3},{1,0},{3,2},{4,5},{6,7},{5,4},{7,6},{8,9},{10,11},{9,8... | collective-permute-start | bytes 589832 | tf_op jit(solution)/shard_map/ppermute | solution.py:398
  5.3 9.2 %collective-permute-start.1 = (f32[384,128]{1,0:T(8,128)S(1)}, f32[384,128]{1,0:T(8,128)S(1)}, u32[]{:S(2)}, u32[]{:S(2)}) collective-permute-start(f32[384,128]{1,0:T(8,128)S(1)} %get-tuple-element.11), channel_id=1, source_target_pairs={{1,2},{2,1},{5,6},{6,5},{9,10},{10,9},{13,14},{14,13},{17,18},{18,... | collective-permute-start | bytes 589832 | tf_op jit(solution)/shard_map/ppermute | solution.py:398
  15.4 3.5 %collective-permute-start.2 = (f32[456,128]{1,0:T(8,128)S(1)}, f32[456,128]{1,0:T(8,128)S(1)}, u32[]{:S(2)}, u32[]{:S(2)}) collective-permute-start(f32[456,128]{1,0:T(8,128)S(1)} %get-tuple-element.12), channel_id=1, source_target_pairs={{0,4},{8,12},{16,20},{24,28},{4,0},{12,8},{20,16},{28,24},{1,5},{9... | collective-permute-start | bytes 700424 | tf_op jit(solution)/shard_map/ppermute | solution.py:398
  15.4 10.5 %collective-permute-start.3 = (f32[456,128]{1,0:T(8,128)S(1)}, f32[456,128]{1,0:T(8,128)S(1)}, u32[]{:S(2)}, u32[]{:S(2)}) collective-permute-start(f32[456,128]{1,0:T(8,128)S(1)} %get-tuple-element.13), channel_id=1, source_target_pairs={{4,8},{12,16},{20,24},{8,4},{16,12},{24,20},{5,9},{13,17},{21,25},... | collective-permute-start | bytes 700424 | tf_op jit(solution)/shard_map/ppermute | solution.py:398
  29.0 7.4 %collective-permute-start.5 = (f32[16,16,128]{2,1,0:T(8,128)S(1)}, f32[16,16,128]{2,1,0:T(8,128)S(1)}, u32[]{:S(2)}, u32[]{:S(2)}) collective-permute-start(f32[16,16,128]{2,1,0:T(8,128)S(1)} %get-tuple-element.15.own), channel_id=1, source_target_pairs={{4,8},{12,16},{20,24},{8,4},{16,12},{24,20},{5,9},{13,17},{21,25},... | collective-permute-start | bytes 393224 | tf_op jit(solution)/shard_map/ppermute | solution.py:398
  32.2 4.3 %collective-permute-start.4 = (f32[16,16,128]{2,1,0:T(8,128)S(1)}, f32[16,16,128]{2,1,0:T(8,128)S(1)}, u32[]{:S(2)}, u32[]{:S(2)}) collective-permute-start(f32[16,16,128]{2,1,0:T(8,128)S(1)} %get-tuple-element.15.own), channel_id=1, source_target_pairs={{0,4},{8,12},{16,20},{24,28},{4,0},{12,8},{20,16},{28,24},{1,5},{9... | collective-permute-start | bytes 393224 | tf_op jit(solution)/shard_map/ppermute | solution.py:398
  36.5 5.7 %collective-permute-start.6 = (f32[48,8,128]{2,1,0:T(8,128)S(1)}, f32[48,8,128]{2,1,0:T(8,128)S(1)}, u32[]{:S(2)}, u32[]{:S(2)}) collective-permute-start(f32[48,8,128]{2,1,0:T(8,128)S(1)} %get-tuple-element.16), channel_id=1, source_target_pairs={{0,1},{2,3},{1,0},{3,2},{4,5},{6,7},{5,4},{7,6},{8,9},{10,11},{9,8... | collective-permute-start | bytes 589832 | tf_op jit(solution)/shard_map/ppermute | solution.py:398
  36.5 7.6 %collective-permute-start.7 = (f32[48,8,128]{2,1,0:T(8,128)S(1)}, f32[48,8,128]{2,1,0:T(8,128)S(1)}, u32[]{:S(2)}, u32[]{:S(2)}) collective-permute-start(f32[48,8,128]{2,1,0:T(8,128)S(1)} %get-tuple-element.17), channel_id=1, source_target_pairs={{1,2},{2,1},{5,6},{6,5},{9,10},{10,9},{13,14},{14,13},{17,18},{18,... | collective-permute-start | bytes 589832 | tf_op jit(solution)/shard_map/ppermute | solution.py:398

commit v4 on v3

v4 whole, which is shorter than its diff:
```python
import functools

import jax
import jax.numpy as jnp
from jax import lax
from jax.experimental import pallas as pl
from jax.experimental.pallas import tpu as pltpu
from jax.sharding import PartitionSpec as P

SWEEPS = 8
REACH = 8

VELOCITIES = (
    (0, 0, 0),
    (1, 0, 0),
    (-1, 0, 0),
    (0, 1, 0),
    (0, -1, 0),
    (0, 0, 1),
    (0, 0, -1),
    (1, 1, 0),
    (-1, -1, 0),
    (1, -1, 0),
    (-1, 1, 0),
    (1, 0, 1),
    (-1, 0, -1),
    (1, 0, -1),
    (-1, 0, 1),
    (0, 1, 1),
    (0, -1, -1),
    (0, 1, -1),
    (0, -1, 1),
)
POPS = 19
SHARE = 1.0 / 36.0
MULTIPLE = (12.0,) + (2.0,) * 6 + (1.0,) * 12
RIGHT = tuple(i for i in range(POPS) if VELOCITIES[i][0] == 1)
LEFT = tuple(i for i in range(POPS) if VELOCITIES[i][0] == -1)
LEVEL = tuple(i for i in range(POPS) if VELOCITIES[i][0] == 0)
PAD = 8
FIRST = 5
EDGES = 19


def rim_entries():
    entries = [(0, i, 1) for i in range(POPS)]
    entries += [(0, i, 2) for i in range(POPS) if VELOCITIES[i][1] != -1]
    entries += [(0, i, 3) for i in range(POPS) if VELOCITIES[i][1] == 1]
    for distance in (1, 2):
        entries += [(1, i, distance) for i in range(3)]
        entries += [(2, 0, distance), (3, 0, distance)]
    return entries


def mirrored(i, axis):
    velocity = list(VELOCITIES[i])
    velocity[axis] = -velocity[axis]
    return VELOCITIES.index(tuple(velocity))


def pick(condition, a, b):
    return a if a == b else jnp.where(condition, a, b)


def toward_next(axis):
    even = lax.axis_index(axis) % 2 == 0
    return even, jnp.logical_not(even)


def lane_pull(v, cz):
    if cz == 0:
        return v
    lanes = v.shape[-1]
    lane = lax.broadcasted_iota(jnp.int32, v.shape, 1)
    if cz == 1:
        return jnp.where(lane != lanes - 1, pltpu.roll(v, lanes - 1, 1), 0.0)
    return jnp.where(lane != 0, pltpu.roll(v, 1, 1), 0.0)


def total(terms):
    terms = [t for t in terms if t is not None]
    return functools.reduce(lambda a, b: a + b, terms) if terms else None


def scaled(v, factor):
    return None if v is None else factor * v


def negated(v):
    return None if v is None else -v


def moments(p):
    s, d = {}, {}
    for i in range(1, POPS, 2):
        a, b = p[i], p[i + 1]
        s[i] = total([a, b])
        d[i] = a - b if a is not None and b is not None else (a if b is None else negated(b))
    average = total(
        [scaled(p[0], 12.0), scaled(total([s[1], s[3], s[5]]), 2.0)] + [s[i] for i in (7, 9, 11, 13, 15, 17)]
    )
    along_x = total([scaled(d[1], 2.0), d[7], d[9], d[11], d[13]])
    along_y = total([scaled(d[3], 2.0), d[7], negated(d[9]), d[15], d[17]])
    along_z = total([scaled(d[5], 2.0), d[11], negated(d[13]), d[15], negated(d[17])])
    return average, (along_x, along_y, along_z)


def relaxed(p, u):
    average, along = moments(p)
    shift = total([u[k] * along[k] for k in range(3) if along[k] is not None])
    return shift, SHARE * average + shift


def pulled_from(read, pops):
    p = [None] * POPS
    for i in pops:
        p[i] = lane_pull(read(i), VELOCITIES[i][2])
    return p


def posts_of(p, keep, equilib, rate, source, pops):
    base = rate * equilib
    terms = {m: base + (source if m == 1.0 else m * source) for m in (12.0, 2.0, 1.0)}
    return {i: keep * p[i] + terms[MULTIPLE[i]] for i in pops}


def coefficients(there, ux, uy, uz, g):
    inside = there > 0.5
    wet = jnp.where(inside, there - 1.0, 0.0)
    keep = jnp.where(inside, 0.1 - 0.7 * wet, 0.0)
    rate = jnp.where(inside, 0.9 + 0.7 * wet, 0.0)
    scale = (3.0 * SHARE) * wet
    return keep, rate, scale * ux, scale * uy, scale * uz, SHARE * g


def extend_own(x_size, y_size, dual, vel, grad, fluid, state, coef):
    planes = x_size + 2

    def copy_own(i, _):
        for x in range(x_size):
            state[i * planes + x + 1, pl.ds(PAD, y_size), :] = dual[i * x_size + x]
        return 0

    lax.fori_loop(0, POPS, copy_own, 0)

    def own_coefficients(x, _):
        there = fluid[x].astype(jnp.float32) + 1.0
        values = coefficients(there, vel[x], vel[x_size + x], vel[2 * x_size + x], grad[x])
        for n, value in enumerate(values):
            coef[n * x_size + x, pl.ds(PAD, y_size), :] = value
        return 0

    lax.fori_loop(0, x_size, own_coefficients, 0)


def extend_rims(x_size, y_size, messages, state, coef):
    pitch = y_size + 2 * PAD
    planes = x_size + 2
    lanes = state.shape[-1]
    flat = state.reshape(state.shape[0] * pitch, lanes)
    coef_flat = coef.reshape(coef.shape[0] * pitch, lanes)
    for after, ref in zip(toward_next("blk"), messages):
        places = {d: jnp.where(after, PAD + y_size - 1 + d, PAD - d) for d in (1, 2, 3)}
        side = {}
        for k, (kind, i, distance) in enumerate(rim_entries()):
            value = ref[pl.ds(k * x_size, x_size), :]
            if kind == 0:
                pop = pick(after, i, mirrored(i, 1))
                at = (pop * planes + 1) * pitch + places[distance]
                flat[pl.ds(at, x_size, stride=pitch), :] = value
            else:
                side[(kind, i, distance)] = value
        for d in (1, 2):
            values = [side[key, n, d] for key, n in ((2, 0), (1, 0), (1, 1), (1, 2), (3, 0))]
            for n, value in enumerate(coefficients(*values)):
                coef_flat[pl.ds(n * x_size * pitch + places[d], x_size, stride=pitch), :] = value


def rim_kernel(x_size, y_size, *refs):
    sources, messages, held, arrived = refs[:4], refs[4:6], refs[6:10], refs[10]
    copies = [pltpu.make_async_copy(a, b, arrived.at[n]) for n, (a, b) in enumerate(zip(sources, held))]
    for copy in copies:
        copy.start()
    for copy in copies:
        copy.wait()
    dual, vel, grad, fluid = held
    lanes = dual.shape[-1]
    flat = [ref.reshape(ref.shape[0] * y_size, lanes) for ref in (dual, vel, fluid, grad)]
    for after, out in zip(toward_next("blk"), messages):
        for k, (kind, i, distance) in enumerate(rim_entries()):
            row = jnp.where(after, y_size - distance, distance - 1)
            field = pick(after, mirrored(i, 1), i) if kind == 0 else i
            value = flat[kind][pl.ds(field * x_size * y_size + row, x_size, stride=y_size), :]
            if kind == 2:
                value = value.astype(jnp.float32) + 1.0
            out[pl.ds(k * x_size, x_size), :] = value


def edge_steps(x_size, after, state, coef, near, far, raw, first, second, put):
    known = RIGHT + LEVEL
    planes = x_size + 2
    inward = jnp.where(after, -1, 1)
    plane = jnp.where(after, x_size - 1, 0)
    turn = jnp.where(after, -1.0, 1.0)

    def coefs(x, at):
        return [coef[n * x_size + x, pl.ds(at, 8), :] for n in range(6)]

    def read_state(x, at):
        def read(i):
            cx, cy, _ = VELOCITIES[i]
            pop = pick(after, mirrored(i, 0), i)
            return state[pop * planes + x + 1 + cx * inward, pl.ds(at + cy, 8), :]

        return read

    for at in raw:
        for n, i in enumerate(RIGHT):
            pop = pick(after, mirrored(i, 0), i)
            put(0, n, at, state[pop * planes + plane + 1, pl.ds(at, 8), :])
    for at in first:
        keep, rate, *u, source = coefs(plane, at)
        for n, value in enumerate((rate, *u)):
            put(3, n, at, value)
        u[0] = turn * u[0]
        p = pulled_from(read_state(plane, at), known)
        _, equilib = relaxed(p, u)
        posts = posts_of(p, keep, equilib, rate, source, known)
        for n, i in enumerate(RIGHT):
            put(1, n, at, posts[i])
        for n, i in enumerate(LEVEL):
            near[n, pl.ds(at, 8), :] = posts[i]
        keep, rate, *u, source = coefs(plane + inward, at)
        u[0] = turn * u[0]
        p = pulled_from(read_state(plane + inward, at), range(POPS))
        _, equilib = relaxed(p, u)
        posts = posts_of(p, keep, equilib, rate, source, RIGHT)
        for n, i in enumerate(RIGHT):
            far[n, pl.ds(at, 8), :] = posts[i]
    for at in second:
        keep, rate, *u, source = coefs(plane, at)
        u[0] = turn * u[0]

        def read(i):
            ref, n = (far, RIGHT.index(i)) if i in RIGHT else (near, LEVEL.index(i))
            return ref[n, pl.ds(at + VELOCITIES[i][1], 8), :]

        p = pulled_from(read, known)
        _, equilib = relaxed(p, u)
        posts = posts_of(p, keep, equilib, rate, source, RIGHT)
        for n, i in enumerate(RIGHT):
            put(2, n, at, posts[i])


EARLY = (0, 5, 10, 15)


def early_kernel(x_size, y_size, dual, vel, grad, fluid, span, early_a, early_b, state, coef, near, far):
    extend_own(x_size, y_size, dual, vel, grad, fluid, state, coef)
    rows = range(PAD, PAD + y_size, 8)
    for after, out in zip(toward_next("grp"), (early_a, early_b)):

        def put(kind, n, at, value, out=out):
            out[pl.ds((EARLY[kind] + n) * y_size + at - PAD, 8), :] = value

        edge_steps(x_size, after, state, coef, near, far, rows, rows, rows, put)
        for x in range(x_size):
            out[pl.ds((EDGES + x) * y_size, y_size), :] = span[x].astype(jnp.float32) + 1.0


def late_pieces(y_size):
    pieces, offset = {}, 0
    for end in (0, 1):
        for kind, count, reach in ((0, 5, 3), (1, 5, 2), (2, 5, 1), (3, 4, 2)):
            rows = 2 if kind == 3 else 3
            begin = PAD + y_size + reach - rows if end else PAD - reach
            pieces[kind, end] = (begin, rows, offset)
            offset += count * rows
    return pieces, -(-offset // 8) * 8


def late_kernel(x_size, y_size, dual, vel, grad, fluid, rim_a, rim_b, late_a, late_b, state, coef, near, far):
    extend_own(x_size, y_size, dual, vel, grad, fluid, state, coef)
    extend_rims(x_size, y_size, (rim_a, rim_b), state, coef)
    pieces, _ = late_pieces(y_size)
    starts = [(PAD - reach, PAD + y_size + reach - 8) for reach in (3, 2, 1)]
    for after, out in zip(toward_next("grp"), (late_a, late_b)):

        def put(kind, n, at, value, out=out):
            begin, rows, offset = pieces[kind, 1 if at > PAD else 0]
            out[pl.ds(offset + n * rows, rows), :] = value[begin - at : begin - at + rows]

        edge_steps(x_size, after, state, coef, near, far, *starts, put)


def steps_kernel(
    x_size, y_size, dual, vel, grad, fluid, rim_a, rim_b, heat, early_a, early_b, late_a, late_b,
    adjoint, sens, state, later, coef, shifts, extra, halos,
):
    extend_own(x_size, y_size, dual, vel, grad, fluid, state, coef)
    extend_rims(x_size, y_size, (rim_a, rim_b), state, coef)
    planes = x_size + 2
    window = y_size + 8
    groups = window // 8
    afters = toward_next("grp")
    pieces, _ = late_pieces(y_size)

    for side, (after, early, late) in enumerate(zip(afters, (early_a, early_b), (late_a, late_b))):
        halo = jnp.where(after, x_size + 1, 0)
        for kind, count in enumerate((5, 5, 5, 4)):
            for n in range(count):
                if kind == 0:
                    ref, plane = state, pick(after, RIGHT[n], mirrored(RIGHT[n], 0)) * planes + halo
                else:
                    ref, plane = halos, side * 14 + EARLY[kind] - 5 + n
                ref[plane, pl.ds(PAD, y_size), :] = early[pl.ds((EARLY[kind] + n) * y_size, y_size), :]
                for end in (0, 1):
                    begin, rows, offset = pieces[kind, end]
                    ref[plane, pl.ds(begin, rows), :] = late[pl.ds(offset + n * rows, rows), :]

    def read_from(source, x, at):
        def read(i):
            cx, cy, _ = VELOCITIES[i]
            return source[i * planes + x + 1 + cx, pl.ds(at + cy, 8), :]

        return read

    def step(number, source, target):
        def plane(x, _):
            for j in range(groups):
                at = FIRST + 8 * j
                keep, rate, *u, drive = [coef[n * x_size + x, pl.ds(at, 8), :] for n in range(6)]
                p = pulled_from(read_from(source, x, at), range(POPS))
                shift, equilib = relaxed(p, u)
                shifts[(number - 1) * x_size + x, pl.ds(at, 8), :] = shift
                posts = posts_of(p, keep, equilib, rate, drive, range(POPS))
                for i in range(POPS):
                    target[i * planes + x + 1, pl.ds(at, 8), :] = posts[i]
            return 0

        lax.fori_loop(0, x_size, plane, 0, unroll=True)
        for side, after in enumerate(afters):
            halo = jnp.where(after, x_size + 1, 0)
            edge = jnp.where(after, x_size, 1)
            turn = jnp.where(after, 1.0, -1.0)
            for j in range(groups):
                at = FIRST + 8 * j
                rate, *u = [halos[side * 14 + 10 + n, pl.ds(at, 8), :] for n in range(4)]
                u[0] = turn * u[0]

                def read(i):
                    cy = VELOCITIES[i][1]
                    if i in LEFT:
                        return source[pick(after, i, mirrored(i, 0)) * planes + edge, pl.ds(at + cy, 8), :]
                    return extra[side, pl.ds(at + cy, 8), :]

                p = pulled_from(read, LEFT if number == 1 else LEFT + LEVEL)
                added = rate * relaxed(p, u)[1]
                if number == 1:
                    extra[side, pl.ds(at, 8), :] = added
                for n, i in enumerate(RIGHT):
                    target[pick(after, i, mirrored(i, 0)) * planes + halo, pl.ds(at, 8), :] = (
                        halos[side * 14 + 5 * number - 5 + n, pl.ds(at, 8), :] + added
                    )

    step(1, state, later)
    step(2, later, state)

    def last(x, _):
        for j in range(y_size // 8):
            at = PAD + 8 * j
            keep, rate, *u, drive = [coef[n * x_size + x, pl.ds(at, 8), :] for n in range(6)]
            p = pulled_from(read_from(state, x, at), range(POPS))
            shift, equilib = relaxed(p, u)
            posts = posts_of(p, keep, equilib, rate, drive, range(POPS))
            for i in range(POPS):
                adjoint[i * x_size + x, pl.ds(8 * j, 8), :] = posts[i]
            shift = shifts[x, pl.ds(at, 8), :] + shifts[x_size + x, pl.ds(at, 8), :] + shift
            sens[x, pl.ds(8 * j, 8), :] = heat[x, pl.ds(8 * j, 8), :] * shift
        return 0

    lax.fori_loop(0, x_size, last, 0, unroll=True)


def diamond(x_size, reach):
    pieces, offset = [], 0
    for slot in range(3):
        for k in range(x_size if slot == 0 else min(x_size, reach - 1)):
            rows = reach if slot == 0 else reach - 1 - k
            pieces.append((slot, k, rows, offset))
            offset += rows
    return pieces, -(-offset // 8) * 8


def slot_plane(x_size, slot, k):
    if slot == 0:
        return x_size + k, k
    after = toward_next("grp")[slot - 1]
    return jnp.where(after, 2 * x_size + k, x_size - 1 - k), jnp.where(after, k, x_size - 1 - k)


def band_kernel(x_size, y_size, reach, own, beside_a, beside_b, band_a, band_b):
    pieces, _ = diamond(x_size, reach)
    skip = EDGES if beside_a.shape[0] > x_size else 0
    for after, out in zip(toward_next("blk"), (band_a, band_b)):
        for slot, k, rows, offset in pieces:
            _, plane = slot_plane(x_size, slot, k)
            start = jnp.where(after, y_size - rows, 0)
            if slot == 0:
                value = own[plane, pl.ds(start, rows), :]
                if skip:
                    value = value.astype(jnp.float32) + 1.0
            else:
                value = (beside_a, beside_b)[slot - 1][skip + plane, pl.ds(start, rows), :]
            out[pl.ds(offset, rows), :] = value


def radius_kernel(x_size, y_size, own, early_a, early_b, band_a, band_b, inverse, beta, there):
    for x in range(x_size):
        there[x_size + x, pl.ds(REACH, y_size), :] = own[x].astype(jnp.float32) + 1.0
        for slot, ref in ((1, early_a), (2, early_b)):
            place, plane = slot_plane(x_size, slot, x)
            there[place, pl.ds(REACH, y_size), :] = ref[EDGES + plane]
    for after, ref in zip(toward_next("blk"), (band_a, band_b)):
        for slot, k, rows, offset in diamond(x_size, REACH - 1)[0]:
            place, _ = slot_plane(x_size, slot, k)
            there[place, pl.ds(jnp.where(after, REACH + y_size, REACH - rows), rows), :] = ref[pl.ds(offset, rows), :]

    def plane(k, _):
        t = there[k]
        r2 = jnp.where(t < 1.5, 0.25, jnp.where(t < 2.5, 1.0, jnp.where(t < 3.5, 4.0, 16.0)))
        share = 1.0 / (1.0 + 6.0 * r2)
        inverse[k] = share
        beta[k] = jnp.where(t > 0.5, r2 * share, 0.0)
        return 0

    lax.fori_loop(0, 3 * x_size, plane, 0, unroll=4)


def filter_kernel(x_size, y_size, own, beside_a, beside_b, band_a, band_b, inverse, beta, filtered, first, second, given):
    wide = 3 * x_size
    rows = y_size + 2 * REACH
    for x in range(x_size):
        first[x_size + x, pl.ds(PAD + REACH, y_size), :] = own[x]
        for slot, ref in ((1, beside_a), (2, beside_b)):
            place, plane = slot_plane(x_size, slot, x)
            first[place, pl.ds(PAD + REACH, y_size), :] = ref[plane]
    for after, ref in zip(toward_next("blk"), (band_a, band_b)):
        for slot, k, count, offset in diamond(x_size, REACH)[0]:
            place, _ = slot_plane(x_size, slot, k)
            at = PAD + jnp.where(after, REACH + y_size, REACH - count)
            first[place, pl.ds(at, count), :] = ref[pl.ds(offset, count), :]
    for k in range(wide):
        given[k] = first[k, pl.ds(PAD, rows), :] * inverse[k]
    source, target = first, second
    for number in range(1, SWEEPS + 1):
        final = number == SWEEPS
        margin = SWEEPS - number

        for j in range(1, 1 + y_size // 8) if final else range(rows // 8):
            at = PAD + 8 * j
            begin, end = x_size - margin, 2 * x_size + margin
            column = {x: source[x, pl.ds(at, 8), :] for x in range(begin - 1, end + 1)}
            for x in range(begin, end):
                beside = column[x + 1] + column[x - 1]
                beside = beside + source[x, pl.ds(at + 1, 8), :] + source[x, pl.ds(at - 1, 8), :]
                beside = beside + lane_pull(column[x], 1) + lane_pull(column[x], -1)
                value = given[x, pl.ds(8 * j, 8), :] + beta[x, pl.ds(8 * j, 8), :] * beside
                if final:
                    filtered[x - x_size, pl.ds(8 * j - REACH, 8), :] = value
                else:
                    target[x, pl.ds(at, 8), :] = value
        source, target = target, source


def call(kernel, outs, scratch, args, name, place=pltpu.VMEM, grant=32):
    return pl.pallas_call(
        kernel,
        out_shape=[jax.ShapeDtypeStruct(shape, jnp.float32) for shape in outs],
        in_specs=[pl.BlockSpec(memory_space=place)] * len(args),
        out_specs=[pl.BlockSpec(memory_space=pltpu.VMEM)] * len(outs),
        scratch_shapes=[pltpu.VMEM(s, jnp.float32) if isinstance(s, tuple) else s for s in scratch],
        compiler_params=pltpu.CompilerParams(vmem_limit_bytes=grant * 1024 * 1024),
        name=name,
    )(*args)


def swapped(axis, message_a, message_b):
    size = lax.axis_size(axis)
    received = []
    for begin, message in ((1, message_b), (0, message_a)):
        pairs = [(i, i + 1) for i in range(begin, size - 1, 2)]
        received.append(lax.ppermute(message, axis, pairs + [(j, i) for i, j in pairs]))
    return received[1], received[0]


def on_device(dual_populace, forward_motion_vector, forward_heat_level, objective_heat_gradient, liquid_indicator,
              filter_span_group):
    _, x_size, y_size, lanes = dual_populace.shape
    planes, pitch = x_size + 2, y_size + 2 * PAD
    sizes = (x_size, y_size)
    dual = dual_populace.reshape(POPS * x_size, y_size, lanes)
    vel = forward_motion_vector.reshape(3 * x_size, y_size, lanes)
    fields = (dual, vel, objective_heat_gradient, liquid_indicator)
    rim = (len(rim_entries()) * x_size, lanes)
    state = (POPS * planes, pitch, lanes)
    coef = (6 * x_size, pitch, lanes)
    edge_scratch = [state, coef, (len(LEVEL), pitch, lanes), (len(RIGHT), pitch, lanes)]

    rims = call(
        functools.partial(rim_kernel, *sizes),
        [rim, rim],
        [pltpu.VMEM(f.shape, f.dtype) for f in fields] + [pltpu.SemaphoreType.DMA((len(fields),))],
        fields,
        "rim_rows",
        pltpu.HBM,
        63,
    )
    rims = swapped("blk", *rims)
    early = ((EDGES + x_size) * y_size, lanes)
    earlies = call(
        functools.partial(early_kernel, *sizes),
        [early, early],
        edge_scratch,
        (*fields, filter_span_group),
        "edges_early",
    )
    earlies = swapped("grp", *earlies)
    late = (late_pieces(y_size)[1], lanes)
    lates = call(functools.partial(late_kernel, *sizes), [late, late], edge_scratch, (*fields, *rims), "edges_late")
    lates = swapped("grp", *lates)
    adjoint, sens = call(
        functools.partial(steps_kernel, *sizes),
        [(POPS * x_size, y_size, lanes), (x_size, y_size, lanes)],
        [state, state, coef, (2 * x_size, pitch, lanes), (2, pitch, lanes), (28, pitch, lanes)],
        (*fields, *rims, forward_heat_level, *earlies, *lates),
        "three_steps",
    )
    beside = swapped("grp", sens, sens)

    wide, rows = 3 * x_size, y_size + 2 * REACH
    spans = [e.reshape(EDGES + x_size, y_size, lanes) for e in earlies]
    band = (diamond(x_size, REACH - 1)[1], lanes)
    span_bands = call(
        functools.partial(band_kernel, *sizes, REACH - 1), [band, band], [], (filter_span_group, *spans), "span_bands"
    )
    span_bands = swapped("blk", *span_bands)
    beside, span_bands = lax.optimization_barrier((beside, span_bands))
    inverse, beta = call(
        functools.partial(radius_kernel, *sizes),
        [(wide, rows, lanes)] * 2,
        [(wide, rows, lanes)],
        (filter_span_group, *spans, *span_bands),
        "radius",
    )
    band = (diamond(x_size, REACH)[1], lanes)
    bands = call(functools.partial(band_kernel, *sizes, REACH), [band, band], [], (sens, *beside), "sens_bands")
    bands = swapped("blk", *bands)
    (filtered,) = call(
        functools.partial(filter_kernel, *sizes),
        [(x_size, y_size, lanes)],
        [(wide, rows + 2 * PAD, lanes)] * 2 + [(wide, rows, lanes)],
        (sens, *beside, *bands, inverse, beta),
        "eight_sweeps",
    )
    return adjoint.reshape(dual_populace.shape), filtered


def solution(mesh):
    in_specs = (
        P(None, "grp", "blk", None),
        P(None, "grp", "blk", None),
        P("grp", "blk", None),
        P("grp", "blk", None),
        P("grp", "blk", None),
        P("grp", "blk", None),
    )
    out_specs = (P(None, "grp", "blk", None), P("grp", "blk", None))
    return jax.shard_map(
        on_device, mesh=mesh, in_specs=in_specs, out_specs=out_specs, check_vma=False
    )
```

time: 46.5 us -> 42.3 us (0.910)
  waiting for transfers between devices: 19.8 us -> 10.4 us
  starting transfers between devices: 15.5 us -> 20.4 us
  Pallas kernels: 6.04 us -> 8.92 us
  local copies, waits for them, and re-layouts: 3.9 us -> 1.31 us
    ppermute x8 -> x12, waiting for transfers between devices: 19.8 us -> 10.4 us  [swapped(): lax.ppermute(message, axis, pairs + [(j, i) for i, j in pairs])]
    ppermute x8 -> x12, starting transfers between devices: 15.5 us -> 20.4 us  [swapped(): lax.ppermute(message, axis, pairs + [(j, i) for i, j in pairs])]
    pallas_call x5 -> x8, Pallas kernels: 6.04 us -> 8.92 us  [call(): pl.pallas_call(kernel, out_shape=[jax.ShapeDtypeStruct(shape, jnp.float32...]
    unnamed x12, local copies, waits for them, and re-layouts: 3.9 us -> 1.31 us
  transfers between devices with their start and end apart: 8 -> 12, of which waited for: 6 -> 6; matrix products, arithmetic and copies ran while one was open for 0% -> 0% of each run, Pallas kernels for 0% -> 4%
where the time goes in v4:
time: 42.3 us; the launch traced here: 41.9 us
  starting transfers between devices  20.4 us (48%)
  waiting for transfers between devices  10.4 us (25%)
  Pallas kernels  8.92 us (21%)
  local copies, waits for them, and re-layouts  1.31 us (3%)
  between operations  0.86 us (2%)
    ppermute x12, starting transfers between devices, swapped(): lax.ppermute(message, axis, pairs + [(j, i) for i, j in pairs])  20.4 us
    ppermute x12, waiting for transfers between devices, swapped(): lax.ppermute(message, axis, pairs + [(j, i) for i, j in pairs])  10.4 us
    pallas_call x8, Pallas kernels, call(): pl.pallas_call(kernel, out_shape=[jax.ShapeDtypeStruct(shape, jnp.float32...  8.92 us
    unnamed x12, local copies, waits for them, and re-layouts  1.31 us
  transfers between devices with their start and end apart: 12, of which 6 were waited for; matrix products, arithmetic and copies ran while one was open for 0% of the time, Pallas kernels for 4%

profile of v4, /device:TPU:12, one launch (start us, length us, event | category | flops | bytes accessed | tf_op | source)
XLA Modules:
  0.0 41.9 jit_solution(15359060840296300340)
XLA Ops:
  0.7 2.3 %rim_rows.1 = (f32[384,128]{1,0:T(8,128)}, f32[384,128]{1,0:T(8,128)}) custom-call(f32[152,16,128]{2,1,0:T(8,128)} %bitcast.5, f32[24,16,128]{2,1,0:T(8,128)} %bitcast.9, f32[8,16,128]{2,1,0:T(8,128)} %grad.5, s32[8,16,128]{2,1,0:T(8,128)} %fluid.5), custom_call_target="tpu_custom_call" | custom-call | tf_op jit(solution)/shard_map/rim_rows/pallas_call | solution.py:477
  3.0 0.5 %collective-permute-start = (f32[384,128]{1,0:T(8,128)}, f32[384,128]{1,0:T(8,128)S(1)}, u32[]{:S(2)}, u32[]{:S(2)}) collective-permute-start(f32[384,128]{1,0:T(8,128)} %get-tuple-element.20), channel_id=1, source_target_pairs={{0,1},{2,3},{1,0},{3,2},{4,5},{6,7},{5,4},{7,6},{8,9},{10,11},{9,8... | collective-permute-start | bytes 589832 | tf_op jit(solution)/shard_map/ppermute | solution.py:493
  3.5 4.6 %collective-permute-start.1 = (f32[384,128]{1,0:T(8,128)}, f32[384,128]{1,0:T(8,128)S(1)}, u32[]{:S(2)}, u32[]{:S(2)}) collective-permute-start(f32[384,128]{1,0:T(8,128)} %get-tuple-element.21), channel_id=1, source_target_pairs={{1,2},{2,1},{5,6},{6,5},{9,10},{10,9},{13,14},{14,13},{17,18},{18,... | collective-permute-start | bytes 589832 | tf_op jit(solution)/shard_map/ppermute | solution.py:493
  8.2 1.3 %copy-done = f32[19,8,16,128]{3,2,1,0:T(8,128)S(1)} copy-done((f32[19,8,16,128]{3,2,1,0:T(8,128)S(1)}, f32[19,8,16,128]{3,2,1,0:T(8,128)}, u32[]{:S(2)}) %copy-start) | copy-done | bytes 1245208
  9.5 0.5 %edges_early.1 = (f32[432,128]{1,0:T(8,128)S(1)}, f32[432,128]{1,0:T(8,128)S(1)}) custom-call(f32[152,16,128]{2,1,0:T(8,128)S(1)} %bitcast.6, f32[24,16,128]{2,1,0:T(8,128)S(1)} %bitcast.10, f32[8,16,128]{2,1,0:T(8,128)S(1)} %copy-done.2, s32[8,16,128]{2,1,0:T(8,128)S(1)} %copy-done.3, s32[8,16,128]{2,1,0:T(8,128)S(1)} %copy-done.4), custom_call_target="tpu_custom_call" | custom-call | tf_op jit(solution)/shard_map/edges_early/pallas_call | solution.py:477
  10.0 0.1 collective-permute-start.2
  10.0 3.4 %collective-permute-start.3 = (f32[432,128]{1,0:T(8,128)S(1)}, f32[432,128]{1,0:T(8,128)S(1)}, u32[]{:S(2)}, u32[]{:S(2)}) collective-permute-start(f32[432,128]{1,0:T(8,128)S(1)} %get-tuple-element.23), channel_id=1, source_target_pairs={{4,8},{12,16},{20,24},{8,4},{16,12},{24,20},{5,9},{13,17},{21,25},... | collective-permute-start | bytes 663560 | tf_op jit(solution)/shard_map/ppermute | solution.py:493
  13.5 0.8 %edges_late.1 = (f32[112,128]{1,0:T(8,128)S(1)}, f32[112,128]{1,0:T(8,128)S(1)}) custom-call(f32[152,16,128]{2,1,0:T(8,128)S(1)} %bitcast.7, f32[24,16,128]{2,1,0:T(8,128)S(1)} %bitcast.11, f32[8,16,128]{2,1,0:T(8,128)S(1)} %copy-done.2, s32[8,16,128]{2,1,0:T(8,128)S(1)} %copy-done.3, f32[384,128]{1,0:T(8,128)S(1)} %collective-permute-done.rim_a, ...), custom_call_target="tpu_custom_call" | custom-call | tf_op jit(solution)/shard_map/edges_late/pallas_call | solution.py:477
  14.3 0.1 collective-permute-start.4
  14.5 3.0 %collective-permute-start.5 = (f32[112,128]{1,0:T(8,128)S(1)}, f32[112,128]{1,0:T(8,128)S(1)}, u32[]{:S(2)}, u32[]{:S(2)}) collective-permute-start(f32[112,128]{1,0:T(8,128)S(1)} %get-tuple-element.25), channel_id=1, source_target_pairs={{4,8},{12,16},{20,24},{8,4},{16,12},{24,20},{5,9},{13,17},{21,25},... | collective-permute-start | bytes 172040 | tf_op jit(solution)/shard_map/ppermute | solution.py:493
  17.4 3.1 %collective-permute-done.3.early_b = f32[432,128]{1,0:T(8,128)S(1)} collective-permute-done((f32[432,128]{1,0:T(8,128)S(1)}, f32[432,128]{1,0:T(8,128)S(1)}, u32[]{:S(2)}, u32[]{:S(2)}) %collective-permute-start.3) | collective-permute-done | bytes 221216 | tf_op jit(solution)/shard_map/ppermute | solution.py:493
  20.6 0.9 %collective-permute-done.5.late_b = f32[112,128]{1,0:T(8,128)S(1)} collective-permute-done((f32[112,128]{1,0:T(8,128)S(1)}, f32[112,128]{1,0:T(8,128)S(1)}, u32[]{:S(2)}, u32[]{:S(2)}) %collective-permute-start.5) | collective-permute-done | bytes 57376 | tf_op jit(solution)/shard_map/ppermute | solution.py:493
  21.5 3.1 %three_steps.1 = (f32[152,16,128]{2,1,0:T(8,128)}, f32[8,16,128]{2,1,0:T(8,128)S(1)}) custom-call(f32[152,16,128]{2,1,0:T(8,128)S(1)} %bitcast.8, f32[24,16,128]{2,1,0:T(8,128)S(1)} %bitcast.12, f32[8,16,128]{2,1,0:T(8,128)S(1)} %copy-done.2, s32[8,16,128]{2,1,0:T(8,128)S(1)} %copy-done.3, f32[384,128]{1,0:T(8,128)S(1)} %collective-permute-done.rim_a, ...), custom_call_target="tpu_custom_call" | custom-call | tf_op jit(solution)/shard_map/three_steps/pallas_call | solution.py:477
  24.6 3.1 %collective-permute-start.7 = (f32[8,16,128]{2,1,0:T(8,128)S(1)}, f32[8,16,128]{2,1,0:T(8,128)S(1)}, u32[]{:S(2)}, u32[]{:S(2)}) collective-permute-start(f32[8,16,128]{2,1,0:T(8,128)S(1)} %get-tuple-element.27.own), channel_id=1, source_target_pairs={{4,8},{12,16},{20,24},{8,4},{16,12},{24,20},{5,9},{13,17},{21,25},... | collective-permute-start | bytes 196616 | tf_op jit(solution)/shard_map/ppermute | solution.py:493
  27.8 0.1 collective-permute-start.8
  27.8 2.7 %collective-permute-start.9 = (f32[104,128]{1,0:T(8,128)S(1)}, f32[104,128]{1,0:T(8,128)S(1)}, u32[]{:S(2)}, u32[]{:S(2)}) collective-permute-start(f32[104,128]{1,0:T(8,128)S(1)} %get-tuple-element.29), channel_id=1, source_target_pairs={{1,2},{2,1},{5,6},{6,5},{9,10},{10,9},{13,14},{14,13},{17,18},{18,... | collective-permute-start | bytes 159752 | tf_op jit(solution)/shard_map/ppermute | solution.py:493
  30.6 1.4 %collective-permute-done.8.band_a = f32[104,128]{1,0:T(8,128)S(1)} collective-permute-done((f32[104,128]{1,0:T(8,128)S(1)}, f32[104,128]{1,0:T(8,128)S(1)}, u32[]{:S(2)}, u32[]{:S(2)}) %collective-permute-start.8) | collective-permute-done | bytes 53280 | tf_op jit(solution)/shard_map/ppermute | solution.py:493
  32.0 1.9 %collective-permute-done.9.band_b = f32[104,128]{1,0:T(8,128)S(1)} collective-permute-done((f32[104,128]{1,0:T(8,128)S(1)}, f32[104,128]{1,0:T(8,128)S(1)}, u32[]{:S(2)}, u32[]{:S(2)}) %collective-permute-start.9) | collective-permute-done | bytes 53280 | tf_op jit(solution)/shard_map/ppermute | solution.py:493
  33.9 0.1 collective-permute-start.10
  34.0 2.7 %collective-permute-start.11 = (f32[120,128]{1,0:T(8,128)S(1)}, f32[120,128]{1,0:T(8,128)S(1)}, u32[]{:S(2)}, u32[]{:S(2)}) collective-permute-start(f32[120,128]{1,0:T(8,128)S(1)} %get-tuple-element.33), channel_id=1, source_target_pairs={{1,2},{2,1},{5,6},{6,5},{9,10},{10,9},{13,14},{14,13},{17,18},{18,... | collective-permute-start | bytes 184328 | tf_op jit(solution)/shard_map/ppermute | solution.py:493
  36.7 0.3 radius.1
  37.0 1.2 %collective-permute-done.10.band_a = f32[120,128]{1,0:T(8,128)S(1)} collective-permute-done((f32[120,128]{1,0:T(8,128)S(1)}, f32[120,128]{1,0:T(8,128)S(1)}, u32[]{:S(2)}, u32[]{:S(2)}) %collective-permute-start.10) | collective-permute-done | bytes 61472 | tf_op jit(solution)/shard_map/ppermute | solution.py:493
  38.2 1.9 %collective-permute-done.11.band_b = f32[120,128]{1,0:T(8,128)S(1)} collective-permute-done((f32[120,128]{1,0:T(8,128)S(1)}, f32[120,128]{1,0:T(8,128)S(1)}, u32[]{:S(2)}, u32[]{:S(2)}) %collective-permute-start.11) | collective-permute-done | bytes 61472 | tf_op jit(solution)/shard_map/ppermute | solution.py:493
  40.1 1.8 %eight_sweeps.1 = f32[8,16,128]{2,1,0:T(8,128)} custom-call(f32[8,16,128]{2,1,0:T(8,128)S(1)} %get-tuple-element.27.own, f32[8,16,128]{2,1,0:T(8,128)S(1)} %collective-permute-done.6.beside_a, f32[8,16,128]{2,1,0:T(8,128)S(1)} %collective-permute-done.7.beside_b, f32[120,128]{1,0:T(8,128)S(1)} %collective-permute-done.10.band_a, ...), custom_call_target="tpu_custom_call" | custom-call | tf_op jit(solution)/shard_map/eight_sweeps/pallas_call | solution.py:477
  (20 shorter events, 0.1 us)
Async XLA Ops:
  0.6 7.5 %copy-start.1 = (f32[3,8,16,128]{3,2,1,0:T(8,128)S(1)}, f32[3,8,16,128]{3,2,1,0:T(8,128)}, u32[]{:S(2)}) copy-start(f32[3,8,16,128]{3,2,1,0:T(8,128)} %param.7) | copy-start | bytes 589828
  0.6 7.5 %copy-start.3 = (s32[8,16,128]{2,1,0:T(8,128)S(1)}, s32[8,16,128]{2,1,0:T(8,128)}, u32[]{:S(2)}) copy-start(s32[8,16,128]{2,1,0:T(8,128)} %fluid.5) | copy-start | bytes 196612
  0.7 7.5 %copy-start.2 = (f32[8,16,128]{2,1,0:T(8,128)S(1)}, f32[8,16,128]{2,1,0:T(8,128)}, u32[]{:S(2)}) copy-start(f32[8,16,128]{2,1,0:T(8,128)} %grad.5) | copy-start | bytes 196612
  0.7 7.5 %copy-start.4 = (s32[8,16,128]{2,1,0:T(8,128)S(1)}, s32[8,16,128]{2,1,0:T(8,128)}, u32[]{:S(2)}) copy-start(s32[8,16,128]{2,1,0:T(8,128)} %own.3) | copy-start | bytes 196612
  3.0 10.4 %collective-permute-start = (f32[384,128]{1,0:T(8,128)}, f32[384,128]{1,0:T(8,128)S(1)}, u32[]{:S(2)}, u32[]{:S(2)}) collective-permute-start(f32[384,128]{1,0:T(8,128)} %get-tuple-element.20), channel_id=1, source_target_pairs={{0,1},{2,3},{1,0},{3,2},{4,5},{6,7},{5,4},{7,6},{8,9},{10,11},{9,8... | collective-permute-start | bytes 589832 | tf_op jit(solution)/shard_map/ppermute | solution.py:493
  3.5 9.9 %collective-permute-start.1 = (f32[384,128]{1,0:T(8,128)}, f32[384,128]{1,0:T(8,128)S(1)}, u32[]{:S(2)}, u32[]{:S(2)}) collective-permute-start(f32[384,128]{1,0:T(8,128)} %get-tuple-element.21), channel_id=1, source_target_pairs={{1,2},{2,1},{5,6},{6,5},{9,10},{10,9},{13,14},{14,13},{17,18},{18,... | collective-permute-start | bytes 589832 | tf_op jit(solution)/shard_map/ppermute | solution.py:493
  8.2 1.3 %copy-start = (f32[19,8,16,128]{3,2,1,0:T(8,128)S(1)}, f32[19,8,16,128]{3,2,1,0:T(8,128)}, u32[]{:S(2)}) copy-start(f32[19,8,16,128]{3,2,1,0:T(8,128)} %param.6) | copy-start | bytes 3735556
  9.9 11.6 %copy-start.5 = (f32[8,16,128]{2,1,0:T(8,128)S(1)}, f32[8,16,128]{2,1,0:T(8,128)}, u32[]{:S(2)}) copy-start(f32[8,16,128]{2,1,0:T(8,128)} %heat.1) | copy-start | bytes 196612
  10.0 7.5 %collective-permute-start.2 = (f32[432,128]{1,0:T(8,128)S(1)}, f32[432,128]{1,0:T(8,128)S(1)}, u32[]{:S(2)}, u32[]{:S(2)}) collective-permute-start(f32[432,128]{1,0:T(8,128)S(1)} %get-tuple-element.22), channel_id=1, source_target_pairs={{0,4},{8,12},{16,20},{24,28},{4,0},{12,8},{20,16},{28,24},{1,5},{9... | collective-permute-start | bytes 663560 | tf_op jit(solution)/shard_map/ppermute | solution.py:493
  10.0 10.5 %collective-permute-start.3 = (f32[432,128]{1,0:T(8,128)S(1)}, f32[432,128]{1,0:T(8,128)S(1)}, u32[]{:S(2)}, u32[]{:S(2)}) collective-permute-start(f32[432,128]{1,0:T(8,128)S(1)} %get-tuple-element.23), channel_id=1, source_target_pairs={{4,8},{12,16},{20,24},{8,4},{16,12},{24,20},{5,9},{13,17},{21,25},... | collective-permute-start | bytes 663560 | tf_op jit(solution)/shard_map/ppermute | solution.py:493
  14.3 6.2 %collective-permute-start.4 = (f32[112,128]{1,0:T(8,128)S(1)}, f32[112,128]{1,0:T(8,128)S(1)}, u32[]{:S(2)}, u32[]{:S(2)}) collective-permute-start(f32[112,128]{1,0:T(8,128)S(1)} %get-tuple-element.24), channel_id=1, source_target_pairs={{0,4},{8,12},{16,20},{24,28},{4,0},{12,8},{20,16},{28,24},{1,5},{9... | collective-permute-start | bytes 172040 | tf_op jit(solution)/shard_map/ppermute | solution.py:493
  14.5 7.0 %collective-permute-start.5 = (f32[112,128]{1,0:T(8,128)S(1)}, f32[112,128]{1,0:T(8,128)S(1)}, u32[]{:S(2)}, u32[]{:S(2)}) collective-permute-start(f32[112,128]{1,0:T(8,128)S(1)} %get-tuple-element.25), channel_id=1, source_target_pairs={{4,8},{12,16},{20,24},{8,4},{16,12},{24,20},{5,9},{13,17},{21,25},... | collective-permute-start | bytes 172040 | tf_op jit(solution)/shard_map/ppermute | solution.py:493
  24.6 9.3 %collective-permute-start.6 = (f32[8,16,128]{2,1,0:T(8,128)S(1)}, f32[8,16,128]{2,1,0:T(8,128)S(1)}, u32[]{:S(2)}, u32[]{:S(2)}) collective-permute-start(f32[8,16,128]{2,1,0:T(8,128)S(1)} %get-tuple-element.27.own), channel_id=1, source_target_pairs={{0,4},{8,12},{16,20},{24,28},{4,0},{12,8},{20,16},{28,24},{1,5},{9... | collective-permute-start | bytes 196616 | tf_op jit(solution)/shard_map/ppermute | solution.py:493
  24.6 9.3 %collective-permute-start.7 = (f32[8,16,128]{2,1,0:T(8,128)S(1)}, f32[8,16,128]{2,1,0:T(8,128)S(1)}, u32[]{:S(2)}, u32[]{:S(2)}) collective-permute-start(f32[8,16,128]{2,1,0:T(8,128)S(1)} %get-tuple-element.27.own), channel_id=1, source_target_pairs={{4,8},{12,16},{20,24},{8,4},{16,12},{24,20},{5,9},{13,17},{21,25},... | collective-permute-start | bytes 196616 | tf_op jit(solution)/shard_map/ppermute | solution.py:493
  27.8 4.2 %collective-permute-start.8 = (f32[104,128]{1,0:T(8,128)S(1)}, f32[104,128]{1,0:T(8,128)S(1)}, u32[]{:S(2)}, u32[]{:S(2)}) collective-permute-start(f32[104,128]{1,0:T(8,128)S(1)} %get-tuple-element.28), channel_id=1, source_target_pairs={{0,1},{2,3},{1,0},{3,2},{4,5},{6,7},{5,4},{7,6},{8,9},{10,11},{9,8... | collective-permute-start | bytes 159752 | tf_op jit(solution)/shard_map/ppermute | solution.py:493
  27.8 6.0 %collective-permute-start.9 = (f32[104,128]{1,0:T(8,128)S(1)}, f32[104,128]{1,0:T(8,128)S(1)}, u32[]{:S(2)}, u32[]{:S(2)}) collective-permute-start(f32[104,128]{1,0:T(8,128)S(1)} %get-tuple-element.29), channel_id=1, source_target_pairs={{1,2},{2,1},{5,6},{6,5},{9,10},{10,9},{13,14},{14,13},{17,18},{18,... | collective-permute-start | bytes 159752 | tf_op jit(solution)/shard_map/ppermute | solution.py:493
  33.9 4.3 %collective-permute-start.10 = (f32[120,128]{1,0:T(8,128)S(1)}, f32[120,128]{1,0:T(8,128)S(1)}, u32[]{:S(2)}, u32[]{:S(2)}) collective-permute-start(f32[120,128]{1,0:T(8,128)S(1)} %get-tuple-element.32), channel_id=1, source_target_pairs={{0,1},{2,3},{1,0},{3,2},{4,5},{6,7},{5,4},{7,6},{8,9},{10,11},{9,8... | collective-permute-start | bytes 184328 | tf_op jit(solution)/shard_map/ppermute | solution.py:493
  34.0 6.1 %collective-permute-start.11 = (f32[120,128]{1,0:T(8,128)S(1)}, f32[120,128]{1,0:T(8,128)S(1)}, u32[]{:S(2)}, u32[]{:S(2)}) collective-permute-start(f32[120,128]{1,0:T(8,128)S(1)} %get-tuple-element.33), channel_id=1, source_target_pairs={{1,2},{2,1},{5,6},{6,5},{9,10},{10,9},{13,14},{14,13},{17,18},{18,... | collective-permute-start | bytes 184328 | tf_op jit(solution)/shard_map/ppermute | solution.py:493

commit v5 on v4

--- a/solution.py
+++ b/solution.py
@@ -177,7 +177,7 @@
 
 
 def rim_kernel(x_size, y_size, *refs):
-    sources, messages, held, arrived = refs[:4], refs[4:6], refs[6:10], refs[10]
+    sources, messages, held, arrived = refs[:4], (refs[5], refs[4]), refs[6:10], refs[10]
     copies = [pltpu.make_async_copy(a, b, arrived.at[n]) for n, (a, b) in enumerate(zip(sources, held))]
     for copy in copies:
         copy.start()
@@ -255,7 +255,7 @@
 EARLY = (0, 5, 10, 15)
 
 
-def early_kernel(x_size, y_size, dual, vel, grad, fluid, span, early_a, early_b, state, coef, near, far):
+def early_kernel(x_size, y_size, dual, vel, grad, fluid, early_b, early_a, state, coef, near, far):
     extend_own(x_size, y_size, dual, vel, grad, fluid, state, coef)
     rows = range(PAD, PAD + y_size, 8)
     for after, out in zip(toward_next("grp"), (early_a, early_b)):
@@ -264,8 +264,6 @@
             out[pl.ds((EARLY[kind] + n) * y_size + at - PAD, 8), :] = value
 
         edge_steps(x_size, after, state, coef, near, far, rows, rows, rows, put)
-        for x in range(x_size):
-            out[pl.ds((EDGES + x) * y_size, y_size), :] = span[x].astype(jnp.float32) + 1.0
 
 
 def late_pieces(y_size):
@@ -279,7 +277,7 @@
     return pieces, -(-offset // 8) * 8
 
 
-def late_kernel(x_size, y_size, dual, vel, grad, fluid, rim_a, rim_b, late_a, late_b, state, coef, near, far):
+def late_kernel(x_size, y_size, dual, vel, grad, fluid, rim_b, rim_a, late_b, late_a, state, coef, near, far):
     extend_own(x_size, y_size, dual, vel, grad, fluid, state, coef)
     extend_rims(x_size, y_size, (rim_a, rim_b), state, coef)
     pieces, _ = late_pieces(y_size)
@@ -294,8 +292,8 @@
 
 
 def steps_kernel(
-    x_size, y_size, dual, vel, grad, fluid, rim_a, rim_b, heat, early_a, early_b, late_a, late_b,
-    adjoint, sens, state, later, coef, shifts, extra, halos,
+    x_size, y_size, dual, vel, grad, fluid, rim_b, rim_a, heat, early_b, early_a, late_b, late_a,
+    sens, state, coef, later, shifts, extra, halos,
 ):
     extend_own(x_size, y_size, dual, vel, grad, fluid, state, coef)
     extend_rims(x_size, y_size, (rim_a, rim_b), state, coef)
@@ -369,17 +367,35 @@
     def last(x, _):
         for j in range(y_size // 8):
             at = PAD + 8 * j
-            keep, rate, *u, drive = [coef[n * x_size + x, pl.ds(at, 8), :] for n in range(6)]
-            p = pulled_from(read_from(state, x, at), range(POPS))
-            shift, equilib = relaxed(p, u)
-            posts = posts_of(p, keep, equilib, rate, drive, range(POPS))
-            for i in range(POPS):
-                adjoint[i * x_size + x, pl.ds(8 * j, 8), :] = posts[i]
+            u = [coef[n * x_size + x, pl.ds(at, 8), :] for n in (2, 3, 4)]
+            p = pulled_from(read_from(state, x, at), range(1, POPS))
+            shift = relaxed(p, u)[0]
             shift = shifts[x, pl.ds(at, 8), :] + shifts[x_size + x, pl.ds(at, 8), :] + shift
             sens[x, pl.ds(8 * j, 8), :] = heat[x, pl.ds(8 * j, 8), :] * shift
         return 0
 
     lax.fori_loop(0, x_size, last, 0, unroll=True)
+
+
+def adjoint_kernel(x_size, y_size, state, coef, adjoint):
+    planes = x_size + 2
+
+    def plane(x, _):
+        for j in range(y_size // 8):
+            at = PAD + 8 * j
+            keep, rate, *u, drive = [coef[n * x_size + x, pl.ds(at, 8), :] for n in range(6)]
+
+            def read(i):
+                cx, cy, _ = VELOCITIES[i]
+                return state[i * planes + x + 1 + cx, pl.ds(at + cy, 8), :]
+
+            p = pulled_from(read, range(POPS))
+            posts = posts_of(p, keep, relaxed(p, u)[1], rate, drive, range(POPS))
+            for i in range(POPS):
+                adjoint[i * x_size + x, pl.ds(8 * j, 8), :] = posts[i]
+        return 0
+
+    lax.fori_loop(0, x_size, plane, 0, unroll=True)
 
 
 def diamond(x_size, reach):
@@ -399,59 +415,69 @@
     return jnp.where(after, 2 * x_size + k, x_size - 1 - k), jnp.where(after, k, x_size - 1 - k)
 
 
-def band_kernel(x_size, y_size, reach, own, beside_a, beside_b, band_a, band_b):
-    pieces, _ = diamond(x_size, reach)
-    skip = EDGES if beside_a.shape[0] > x_size else 0
+def band_kernel(x_size, y_size, own, beside_b, beside_a, span, span_b, span_a, band_b, band_a):
+    pieces, skip = diamond(x_size, REACH)
     for after, out in zip(toward_next("blk"), (band_a, band_b)):
-        for slot, k, rows, offset in pieces:
-            _, plane = slot_plane(x_size, slot, k)
-            start = jnp.where(after, y_size - rows, 0)
-            if slot == 0:
-                value = own[plane, pl.ds(start, rows), :]
-                if skip:
-                    value = value.astype(jnp.float32) + 1.0
-            else:
-                value = (beside_a, beside_b)[slot - 1][skip + plane, pl.ds(start, rows), :]
-            out[pl.ds(offset, rows), :] = value
-
-
-def radius_kernel(x_size, y_size, own, early_a, early_b, band_a, band_b, inverse, beta, there):
-    for x in range(x_size):
-        there[x_size + x, pl.ds(REACH, y_size), :] = own[x].astype(jnp.float32) + 1.0
-        for slot, ref in ((1, early_a), (2, early_b)):
-            place, plane = slot_plane(x_size, slot, x)
-            there[place, pl.ds(REACH, y_size), :] = ref[EDGES + plane]
-    for after, ref in zip(toward_next("blk"), (band_a, band_b)):
-        for slot, k, rows, offset in diamond(x_size, REACH - 1)[0]:
-            place, _ = slot_plane(x_size, slot, k)
-            there[place, pl.ds(jnp.where(after, REACH + y_size, REACH - rows), rows), :] = ref[pl.ds(offset, rows), :]
-
-    def plane(k, _):
-        t = there[k]
-        r2 = jnp.where(t < 1.5, 0.25, jnp.where(t < 2.5, 1.0, jnp.where(t < 3.5, 4.0, 16.0)))
-        share = 1.0 / (1.0 + 6.0 * r2)
-        inverse[k] = share
-        beta[k] = jnp.where(t > 0.5, r2 * share, 0.0)
-        return 0
-
-    lax.fori_loop(0, 3 * x_size, plane, 0, unroll=4)
-
-
-def filter_kernel(x_size, y_size, own, beside_a, beside_b, band_a, band_b, inverse, beta, filtered, first, second, given):
-    wide = 3 * x_size
+        for refs, reach, base in (((own, beside_a, beside_b), REACH, 0), ((span, span_a, span_b), REACH - 1, skip)):
+            for slot, k, rows, offset in diamond(x_size, reach)[0]:
+                _, plane = slot_plane(x_size, slot, k)
+                value = refs[slot][plane, pl.ds(jnp.where(after, y_size - rows, 0), rows), :]
+                out[pl.ds(base + offset, rows), :] = value.astype(jnp.float32)
+
+
+def shares(span, inside):
+    r2 = jnp.where(span < 0.5, 0.25, jnp.where(span < 1.5, 1.0, jnp.where(span < 2.5, 4.0, 16.0)))
+    share = 1.0 / (1.0 + 6.0 * r2)
+    return share, jnp.where(inside, r2 * share, 0.0)
+
+
+def slot_inside(slot):
+    if slot == 0:
+        return True
+    after = toward_next("grp")[slot - 1]
+    me, size = lax.axis_index("grp"), lax.axis_size("grp")
+    return jnp.where(after, me < size - 1, me > 0)
+
+
+def radius_kernel(x_size, y_size, span, span_b, span_a, inverse, beta):
+    for slot, ref in enumerate((span, span_a, span_b)):
+        inside = slot_inside(slot)
+
+        def plane(x, _, slot=slot, ref=ref, inside=inside):
+            place, k = slot_plane(x_size, slot, x)
+            inverse[place], beta[place] = shares(ref[k].astype(jnp.float32), inside)
+            return 0
+
+        lax.fori_loop(0, x_size, plane, 0, unroll=4)
+
+
+def filter_kernel(
+    x_size, y_size, own, beside_b, beside_a, band_b, band_a, inverse, own_beta, filtered, first, second, given, beta
+):
     rows = y_size + 2 * REACH
     for x in range(x_size):
-        first[x_size + x, pl.ds(PAD + REACH, y_size), :] = own[x]
-        for slot, ref in ((1, beside_a), (2, beside_b)):
+        for slot, ref in enumerate((own, beside_a, beside_b)):
             place, plane = slot_plane(x_size, slot, x)
-            first[place, pl.ds(PAD + REACH, y_size), :] = ref[plane]
+            s = ref[plane]
+            first[place, pl.ds(PAD + REACH, y_size), :] = s
+            given[place, pl.ds(REACH, y_size), :] = s * inverse[place]
+            beta[place, pl.ds(REACH, y_size), :] = own_beta[place]
+    pieces, skip = diamond(x_size, REACH)
+    radii = {(slot, k): (rows, skip + offset) for slot, k, rows, offset in diamond(x_size, REACH - 1)[0]}
+    me, size = lax.axis_index("blk"), lax.axis_size("blk")
     for after, ref in zip(toward_next("blk"), (band_a, band_b)):
-        for slot, k, count, offset in diamond(x_size, REACH)[0]:
+        there = jnp.where(after, me < size - 1, me > 0)
+        for slot, k, count, offset in pieces:
             place, _ = slot_plane(x_size, slot, k)
-            at = PAD + jnp.where(after, REACH + y_size, REACH - count)
-            first[place, pl.ds(at, count), :] = ref[pl.ds(offset, count), :]
-    for k in range(wide):
-        given[k] = first[k, pl.ds(PAD, rows), :] * inverse[k]
+            at = jnp.where(after, REACH + y_size, REACH - count)
+            s = ref[pl.ds(offset, count), :]
+            first[place, pl.ds(PAD + at, count), :] = s
+            if (slot, k) in radii:
+                count, offset = radii[slot, k]
+                at = jnp.where(after, REACH + y_size, REACH - count)
+                inside = jnp.logical_and(there, slot_inside(slot))
+                share, beta[place, pl.ds(at, count), :] = shares(ref[pl.ds(offset, count), :], inside)
+                given[place, pl.ds(at, count), :] = first[place, pl.ds(PAD + at, count), :] * share
     source, target = first, second
     for number in range(1, SWEEPS + 1):
         final = number == SWEEPS
@@ -485,13 +511,13 @@
     )(*args)
 
 
-def swapped(axis, message_a, message_b):
+def swapped(axis, message_b, message_a):
     size = lax.axis_size(axis)
     received = []
     for begin, message in ((1, message_b), (0, message_a)):
         pairs = [(i, i + 1) for i in range(begin, size - 1, 2)]
         received.append(lax.ppermute(message, axis, pairs + [(j, i) for i, j in pairs]))
-    return received[1], received[0]
+    return received
 
 
 def on_device(dual_populace, forward_motion_vector, forward_heat_level, objective_heat_gradient, liquid_indicator,
@@ -507,6 +533,7 @@
     coef = (6 * x_size, pitch, lanes)
     edge_scratch = [state, coef, (len(LEVEL), pitch, lanes), (len(RIGHT), pitch, lanes)]
 
+    spans = swapped("grp", filter_span_group, filter_span_group)
     rims = call(
         functools.partial(rim_kernel, *sizes),
         [rim, rim],
@@ -517,49 +544,42 @@
         63,
     )
     rims = swapped("blk", *rims)
-    early = ((EDGES + x_size) * y_size, lanes)
+    early = (EDGES * y_size, lanes)
     earlies = call(
         functools.partial(early_kernel, *sizes),
         [early, early],
         edge_scratch,
-        (*fields, filter_span_group),
+        fields,
         "edges_early",
     )
     earlies = swapped("grp", *earlies)
     late = (late_pieces(y_size)[1], lanes)
     lates = call(functools.partial(late_kernel, *sizes), [late, late], edge_scratch, (*fields, *rims), "edges_late")
     lates = swapped("grp", *lates)
-    adjoint, sens = call(
+    sens, state_2, coefs = call(
         functools.partial(steps_kernel, *sizes),
-        [(POPS * x_size, y_size, lanes), (x_size, y_size, lanes)],
-        [state, state, coef, (2 * x_size, pitch, lanes), (2, pitch, lanes), (28, pitch, lanes)],
+        [(x_size, y_size, lanes), state, coef],
+        [state, (2 * x_size, pitch, lanes), (2, pitch, lanes), (28, pitch, lanes)],
         (*fields, *rims, forward_heat_level, *earlies, *lates),
-        "three_steps",
+        "two_steps_and_sens",
     )
     beside = swapped("grp", sens, sens)
-
+    (adjoint,) = call(
+        functools.partial(adjoint_kernel, *sizes), [(POPS * x_size, y_size, lanes)], [], (state_2, coefs), "third_step"
+    )
+    inverse, beta = call(
+        functools.partial(radius_kernel, *sizes), [(3 * x_size, y_size, lanes)] * 2, [], (filter_span_group, *spans), "radius"
+    )
+    band = (diamond(x_size, REACH)[1] + diamond(x_size, REACH - 1)[1], lanes)
+    bands = call(
+        functools.partial(band_kernel, *sizes), [band, band], [], (sens, *beside, filter_span_group, *spans), "bands"
+    )
+    bands = swapped("blk", *bands)
     wide, rows = 3 * x_size, y_size + 2 * REACH
-    spans = [e.reshape(EDGES + x_size, y_size, lanes) for e in earlies]
-    band = (diamond(x_size, REACH - 1)[1], lanes)
-    span_bands = call(
-        functools.partial(band_kernel, *sizes, REACH - 1), [band, band], [], (filter_span_group, *spans), "span_bands"
-    )
-    span_bands = swapped("blk", *span_bands)
-    beside, span_bands = lax.optimization_barrier((beside, span_bands))
-    inverse, beta = call(
-        functools.partial(radius_kernel, *sizes),
-        [(wide, rows, lanes)] * 2,
-        [(wide, rows, lanes)],
-        (filter_span_group, *spans, *span_bands),
-        "radius",
-    )
-    band = (diamond(x_size, REACH)[1], lanes)
-    bands = call(functools.partial(band_kernel, *sizes, REACH), [band, band], [], (sens, *beside), "sens_bands")
-    bands = swapped("blk", *bands)
     (filtered,) = call(
         functools.partial(filter_kernel, *sizes),
         [(x_size, y_size, lanes)],
-        [(wide, rows + 2 * PAD, lanes)] * 2 + [(wide, rows, lanes)],
+        [(wide, rows + 2 * PAD, lanes)] * 2 + [(wide, rows, lanes)] * 2,
         (sens, *beside, *bands, inverse, beta),
         "eight_sweeps",
     )

time: 42.3 us -> 39.1 us (0.924)
  waiting for transfers between devices: 10.4 us -> 7.62 us
  starting transfers between devices: 20.4 us -> 19.9 us
    ppermute x12, waiting for transfers between devices: 10.4 us -> 7.62 us  [swapped(): lax.ppermute(message, axis, pairs + [(j, i) for i, j in pairs])]
    ppermute x12, starting transfers between devices: 20.4 us -> 19.9 us  [swapped(): lax.ppermute(message, axis, pairs + [(j, i) for i, j in pairs])]
  transfers between devices with their start and end apart: 12 -> 12, of which waited for: 6 -> 4; matrix products, arithmetic and copies ran while one was open for 0% -> 0% of each run, Pallas kernels for 4% -> 12%
where the time goes in v5:
time: 39.1 us; the launch traced here: 38.6 us
  starting transfers between devices  19.9 us (51%)
  Pallas kernels  8.94 us (23%)
  waiting for transfers between devices  7.62 us (19%)
  local copies, waits for them, and re-layouts  1.31 us (3%)
  between operations  0.88 us (2%)
    ppermute x12, starting transfers between devices, swapped(): lax.ppermute(message, axis, pairs + [(j, i) for i, j in pairs])  19.9 us
    pallas_call x8, Pallas kernels, call(): pl.pallas_call(kernel, out_shape=[jax.ShapeDtypeStruct(shape, jnp.float32...  8.94 us
    ppermute x12, waiting for transfers between devices, swapped(): lax.ppermute(message, axis, pairs + [(j, i) for i, j in pairs])  7.62 us
    unnamed x12, local copies, waits for them, and re-layouts  1.31 us
  transfers between devices with their start and end apart: 12, of which 4 were waited for; matrix products, arithmetic and copies ran while one was open for 0% of the time, Pallas kernels for 12%

profile of v5, /device:TPU:12, one launch (start us, length us, event | category | flops | bytes accessed | tf_op | source)
XLA Modules:
  0.0 38.6 jit_solution(8101240636970279009)
XLA Ops:
  0.7 2.3 %rim_rows.1 = (f32[384,128]{1,0:T(8,128)}, f32[384,128]{1,0:T(8,128)}) custom-call(f32[152,16,128]{2,1,0:T(8,128)} %bitcast.3, f32[24,16,128]{2,1,0:T(8,128)} %bitcast.7, f32[8,16,128]{2,1,0:T(8,128)} %grad.5, s32[8,16,128]{2,1,0:T(8,128)} %fluid.5), custom_call_target="tpu_custom_call" | custom-call | tf_op jit(solution)/shard_map/rim_rows/pallas_call | solution.py:503
  3.0 3.5 %collective-permute-start = (f32[384,128]{1,0:T(8,128)}, f32[384,128]{1,0:T(8,128)S(1)}, u32[]{:S(2)}, u32[]{:S(2)}) collective-permute-start(f32[384,128]{1,0:T(8,128)} %get-tuple-element.15), channel_id=1, source_target_pairs={{1,2},{2,1},{5,6},{6,5},{9,10},{10,9},{13,14},{14,13},{17,18},{18,... | collective-permute-start | bytes 589832 | tf_op jit(solution)/shard_map/ppermute | solution.py:519
  6.5 0.1 collective-permute-start.1
  6.6 1.3 %copy-done = f32[19,8,16,128]{3,2,1,0:T(8,128)S(1)} copy-done((f32[19,8,16,128]{3,2,1,0:T(8,128)S(1)}, f32[19,8,16,128]{3,2,1,0:T(8,128)}, u32[]{:S(2)}) %copy-start) | copy-done | bytes 1245208
  7.9 0.5 %edges_early.1 = (f32[304,128]{1,0:T(8,128)S(1)}, f32[304,128]{1,0:T(8,128)S(1)}) custom-call(f32[152,16,128]{2,1,0:T(8,128)S(1)} %bitcast.4, f32[24,16,128]{2,1,0:T(8,128)S(1)} %bitcast.8, f32[8,16,128]{2,1,0:T(8,128)S(1)} %copy-done.2, s32[8,16,128]{2,1,0:T(8,128)S(1)} %copy-done.3), custom_call_target="tpu_custom_call" | custom-call | tf_op jit(solution)/shard_map/edges_early/pallas_call | solution.py:503
  8.4 2.6 %collective-permute-start.2 = (f32[304,128]{1,0:T(8,128)S(1)}, f32[304,128]{1,0:T(8,128)S(1)}, u32[]{:S(2)}, u32[]{:S(2)}) collective-permute-start(f32[304,128]{1,0:T(8,128)S(1)} %get-tuple-element.17), channel_id=1, source_target_pairs={{4,8},{12,16},{20,24},{8,4},{16,12},{24,20},{5,9},{13,17},{21,25},... | collective-permute-start | bytes 466952 | tf_op jit(solution)/shard_map/ppermute | solution.py:519
  11.0 1.1 %collective-permute-start.3 = (f32[304,128]{1,0:T(8,128)S(1)}, f32[304,128]{1,0:T(8,128)S(1)}, u32[]{:S(2)}, u32[]{:S(2)}) collective-permute-start(f32[304,128]{1,0:T(8,128)S(1)} %get-tuple-element.18), channel_id=1, source_target_pairs={{0,4},{8,12},{16,20},{24,28},{4,0},{12,8},{20,16},{28,24},{1,5},{9... | collective-permute-start | bytes 466952 | tf_op jit(solution)/shard_map/ppermute | solution.py:519
  12.1 1.0 %collective-permute-done.1.rim_a = f32[384,128]{1,0:T(8,128)S(1)} collective-permute-done((f32[384,128]{1,0:T(8,128)}, f32[384,128]{1,0:T(8,128)S(1)}, u32[]{:S(2)}, u32[]{:S(2)}) %collective-permute-start.1) | collective-permute-done | bytes 196640 | tf_op jit(solution)/shard_map/ppermute | solution.py:519
  13.1 0.8 %edges_late.1 = (f32[112,128]{1,0:T(8,128)S(1)}, f32[112,128]{1,0:T(8,128)S(1)}) custom-call(f32[152,16,128]{2,1,0:T(8,128)S(1)} %bitcast.5, f32[24,16,128]{2,1,0:T(8,128)S(1)} %bitcast.9, f32[8,16,128]{2,1,0:T(8,128)S(1)} %copy-done.2, s32[8,16,128]{2,1,0:T(8,128)S(1)} %copy-done.3, f32[384,128]{1,0:T(8,128)S(1)} %collective-permute-done.rim_b, ...), custom_call_target="tpu_custom_call" | custom-call | tf_op jit(solution)/shard_map/edges_late/pallas_call | solution.py:503
  13.9 2.0 %collective-permute-start.4 = (f32[112,128]{1,0:T(8,128)S(1)}, f32[112,128]{1,0:T(8,128)S(1)}, u32[]{:S(2)}, u32[]{:S(2)}) collective-permute-start(f32[112,128]{1,0:T(8,128)S(1)} %get-tuple-element.19), channel_id=1, source_target_pairs={{4,8},{12,16},{20,24},{8,4},{16,12},{24,20},{5,9},{13,17},{21,25},... | collective-permute-start | bytes 172040 | tf_op jit(solution)/shard_map/ppermute | solution.py:519
  15.9 1.6 %collective-permute-start.5 = (f32[112,128]{1,0:T(8,128)S(1)}, f32[112,128]{1,0:T(8,128)S(1)}, u32[]{:S(2)}, u32[]{:S(2)}) collective-permute-start(f32[112,128]{1,0:T(8,128)S(1)} %get-tuple-element.20), channel_id=1, source_target_pairs={{0,4},{8,12},{16,20},{24,28},{4,0},{12,8},{20,16},{28,24},{1,5},{9... | collective-permute-start | bytes 172040 | tf_op jit(solution)/shard_map/ppermute | solution.py:519
  17.5 3.0 %collective-permute-start.8 = (s32[8,16,128]{2,1,0:T(8,128)S(1)}, s32[8,16,128]{2,1,0:T(8,128)S(1)}, u32[]{:S(2)}, u32[]{:S(2)}) collective-permute-start(s32[8,16,128]{2,1,0:T(8,128)S(1)} %copy-done.4), channel_id=1, source_target_pairs={{4,8},{12,16},{20,24},{8,4},{16,12},{24,20},{5,9},{13,17},{21,25},... | collective-permute-start | bytes 196616 | tf_op jit(solution)/shard_map/ppermute | solution.py:519
  20.5 0.1 collective-permute-start.9
  20.6 1.8 %two_steps_and_sens.1 = (f32[8,16,128]{2,1,0:T(8,128)S(1)}, f32[190,32,128]{2,1,0:T(8,128)S(1)}, f32[48,32,128]{2,1,0:T(8,128)S(1)}) custom-call(f32[152,16,128]{2,1,0:T(8,128)S(1)} %bitcast.6, f32[24,16,128]{2,1,0:T(8,128)S(1)} %bitcast.10, f32[8,16,128]{2,1,0:T(8,128)S(1)} %copy-done.2, s32[8,16,128]{2,1,0:T(8,128)S(1)} %copy-done.3, ...), custom_call_target="tpu_custom_call" | custom-call | tf_op jit(solution)/shard_map/two_steps_and_sens/pallas_call | solution.py:503
  22.5 3.5 %collective-permute-start.6 = (f32[8,16,128]{2,1,0:T(8,128)S(1)}, f32[8,16,128]{2,1,0:T(8,128)S(1)}, u32[]{:S(2)}, u32[]{:S(2)}) collective-permute-start(f32[8,16,128]{2,1,0:T(8,128)S(1)} %get-tuple-element.23.own), channel_id=1, source_target_pairs={{4,8},{12,16},{20,24},{8,4},{16,12},{24,20},{5,9},{13,17},{21,25},... | collective-permute-start | bytes 196616 | tf_op jit(solution)/shard_map/ppermute | solution.py:519
  26.0 0.1 collective-permute-start.7
  26.1 3.4 %collective-permute-done.6.beside_b = f32[8,16,128]{2,1,0:T(8,128)S(1)} collective-permute-done((f32[8,16,128]{2,1,0:T(8,128)S(1)}, f32[8,16,128]{2,1,0:T(8,128)S(1)}, u32[]{:S(2)}, u32[]{:S(2)}) %collective-permute-start.6) | collective-permute-done | bytes 65568 | tf_op jit(solution)/shard_map/ppermute | solution.py:519
  29.5 2.4 %collective-permute-start.10 = (f32[224,128]{1,0:T(8,128)S(1)}, f32[224,128]{1,0:T(8,128)S(1)}, u32[]{:S(2)}, u32[]{:S(2)}) collective-permute-start(f32[224,128]{1,0:T(8,128)S(1)} %get-tuple-element.24), channel_id=1, source_target_pairs={{1,2},{2,1},{5,6},{6,5},{9,10},{10,9},{13,14},{14,13},{17,18},{18,... | collective-permute-start | bytes 344072 | tf_op jit(solution)/shard_map/ppermute | solution.py:519
  31.9 0.1 collective-permute-start.11
  31.9 0.2 radius.1
  32.1 1.4 %third_step.1 = f32[152,16,128]{2,1,0:T(8,128)} custom-call(f32[190,32,128]{2,1,0:T(8,128)S(1)} %get-tuple-element.21.state, f32[48,32,128]{2,1,0:T(8,128)S(1)} %get-tuple-element.22.coef), custom_call_target="tpu_custom_call" | custom-call | tf_op jit(solution)/shard_map/third_step/pallas_call | solution.py:503
  33.5 2.7 %collective-permute-done.10.band_b = f32[224,128]{1,0:T(8,128)S(1)} collective-permute-done((f32[224,128]{1,0:T(8,128)S(1)}, f32[224,128]{1,0:T(8,128)S(1)}, u32[]{:S(2)}, u32[]{:S(2)}) %collective-permute-start.10) | collective-permute-done | bytes 114720 | tf_op jit(solution)/shard_map/ppermute | solution.py:519
  36.2 0.5 %collective-permute-done.11.band_a = f32[224,128]{1,0:T(8,128)S(1)} collective-permute-done((f32[224,128]{1,0:T(8,128)S(1)}, f32[224,128]{1,0:T(8,128)S(1)}, u32[]{:S(2)}, u32[]{:S(2)}) %collective-permute-start.11) | collective-permute-done | bytes 114720 | tf_op jit(solution)/shard_map/ppermute | solution.py:519
  36.7 1.9 %eight_sweeps.1 = f32[8,16,128]{2,1,0:T(8,128)} custom-call(f32[8,16,128]{2,1,0:T(8,128)S(1)} %get-tuple-element.23.own, f32[8,16,128]{2,1,0:T(8,128)S(1)} %collective-permute-done.6.beside_b, f32[8,16,128]{2,1,0:T(8,128)S(1)} %collective-permute-done.7.beside_a, f32[224,128]{1,0:T(8,128)S(1)} %collective-permute-done.10.band_b, ...), custom_call_target="tpu_custom_call" | custom-call | tf_op jit(solution)/shard_map/eight_sweeps/pallas_call | solution.py:503
  (20 shorter events, 0.1 us)
Async XLA Ops:
  0.6 5.9 %copy-start.1 = (f32[3,8,16,128]{3,2,1,0:T(8,128)S(1)}, f32[3,8,16,128]{3,2,1,0:T(8,128)}, u32[]{:S(2)}) copy-start(f32[3,8,16,128]{3,2,1,0:T(8,128)} %param.7) | copy-start | bytes 589828
  0.6 5.9 %copy-start.3 = (s32[8,16,128]{2,1,0:T(8,128)S(1)}, s32[8,16,128]{2,1,0:T(8,128)}, u32[]{:S(2)}) copy-start(s32[8,16,128]{2,1,0:T(8,128)} %fluid.5) | copy-start | bytes 196612
  0.7 5.9 %copy-start.2 = (f32[8,16,128]{2,1,0:T(8,128)S(1)}, f32[8,16,128]{2,1,0:T(8,128)}, u32[]{:S(2)}) copy-start(f32[8,16,128]{2,1,0:T(8,128)} %grad.5) | copy-start | bytes 196612
  3.0 9.1 %collective-permute-start = (f32[384,128]{1,0:T(8,128)}, f32[384,128]{1,0:T(8,128)S(1)}, u32[]{:S(2)}, u32[]{:S(2)}) collective-permute-start(f32[384,128]{1,0:T(8,128)} %get-tuple-element.15), channel_id=1, source_target_pairs={{1,2},{2,1},{5,6},{6,5},{9,10},{10,9},{13,14},{14,13},{17,18},{18,... | collective-permute-start | bytes 589832 | tf_op jit(solution)/shard_map/ppermute | solution.py:519
  6.5 6.6 %collective-permute-start.1 = (f32[384,128]{1,0:T(8,128)}, f32[384,128]{1,0:T(8,128)S(1)}, u32[]{:S(2)}, u32[]{:S(2)}) collective-permute-start(f32[384,128]{1,0:T(8,128)} %get-tuple-element.16), channel_id=1, source_target_pairs={{0,1},{2,3},{1,0},{3,2},{4,5},{6,7},{5,4},{7,6},{8,9},{10,11},{9,8... | collective-permute-start | bytes 589832 | tf_op jit(solution)/shard_map/ppermute | solution.py:519
  6.6 1.3 %copy-start = (f32[19,8,16,128]{3,2,1,0:T(8,128)S(1)}, f32[19,8,16,128]{3,2,1,0:T(8,128)}, u32[]{:S(2)}) copy-start(f32[19,8,16,128]{3,2,1,0:T(8,128)} %param.6) | copy-start | bytes 3735556
  8.4 9.2 %copy-start.4 = (s32[8,16,128]{2,1,0:T(8,128)S(1)}, s32[8,16,128]{2,1,0:T(8,128)}, u32[]{:S(2)}) copy-start(s32[8,16,128]{2,1,0:T(8,128)} %span.3) | copy-start | bytes 196612
  8.4 12.3 %copy-start.5 = (f32[8,16,128]{2,1,0:T(8,128)S(1)}, f32[8,16,128]{2,1,0:T(8,128)}, u32[]{:S(2)}) copy-start(f32[8,16,128]{2,1,0:T(8,128)} %heat.1) | copy-start | bytes 196612
  8.4 12.1 %collective-permute-start.2 = (f32[304,128]{1,0:T(8,128)S(1)}, f32[304,128]{1,0:T(8,128)S(1)}, u32[]{:S(2)}, u32[]{:S(2)}) collective-permute-start(f32[304,128]{1,0:T(8,128)S(1)} %get-tuple-element.17), channel_id=1, source_target_pairs={{4,8},{12,16},{20,24},{8,4},{16,12},{24,20},{5,9},{13,17},{21,25},... | collective-permute-start | bytes 466952 | tf_op jit(solution)/shard_map/ppermute | solution.py:519
  11.0 9.6 %collective-permute-start.3 = (f32[304,128]{1,0:T(8,128)S(1)}, f32[304,128]{1,0:T(8,128)S(1)}, u32[]{:S(2)}, u32[]{:S(2)}) collective-permute-start(f32[304,128]{1,0:T(8,128)S(1)} %get-tuple-element.18), channel_id=1, source_target_pairs={{0,4},{8,12},{16,20},{24,28},{4,0},{12,8},{20,16},{28,24},{1,5},{9... | collective-permute-start | bytes 466952 | tf_op jit(solution)/shard_map/ppermute | solution.py:519
  13.9 6.7 %collective-permute-start.4 = (f32[112,128]{1,0:T(8,128)S(1)}, f32[112,128]{1,0:T(8,128)S(1)}, u32[]{:S(2)}, u32[]{:S(2)}) collective-permute-start(f32[112,128]{1,0:T(8,128)S(1)} %get-tuple-element.19), channel_id=1, source_target_pairs={{4,8},{12,16},{20,24},{8,4},{16,12},{24,20},{5,9},{13,17},{21,25},... | collective-permute-start | bytes 172040 | tf_op jit(solution)/shard_map/ppermute | solution.py:519
  15.9 4.7 %collective-permute-start.5 = (f32[112,128]{1,0:T(8,128)S(1)}, f32[112,128]{1,0:T(8,128)S(1)}, u32[]{:S(2)}, u32[]{:S(2)}) collective-permute-start(f32[112,128]{1,0:T(8,128)S(1)} %get-tuple-element.20), channel_id=1, source_target_pairs={{0,4},{8,12},{16,20},{24,28},{4,0},{12,8},{20,16},{28,24},{1,5},{9... | collective-permute-start | bytes 172040 | tf_op jit(solution)/shard_map/ppermute | solution.py:519
  17.5 8.5 %collective-permute-start.8 = (s32[8,16,128]{2,1,0:T(8,128)S(1)}, s32[8,16,128]{2,1,0:T(8,128)S(1)}, u32[]{:S(2)}, u32[]{:S(2)}) collective-permute-start(s32[8,16,128]{2,1,0:T(8,128)S(1)} %copy-done.4), channel_id=1, source_target_pairs={{4,8},{12,16},{20,24},{8,4},{16,12},{24,20},{5,9},{13,17},{21,25},... | collective-permute-start | bytes 196616 | tf_op jit(solution)/shard_map/ppermute | solution.py:519
  20.5 5.5 %collective-permute-start.9 = (s32[8,16,128]{2,1,0:T(8,128)S(1)}, s32[8,16,128]{2,1,0:T(8,128)S(1)}, u32[]{:S(2)}, u32[]{:S(2)}) collective-permute-start(s32[8,16,128]{2,1,0:T(8,128)S(1)} %copy-done.4), channel_id=1, source_target_pairs={{0,4},{8,12},{16,20},{24,28},{4,0},{12,8},{20,16},{28,24},{1,5},{9... | collective-permute-start | bytes 196616 | tf_op jit(solution)/shard_map/ppermute | solution.py:519
  22.5 6.9 %collective-permute-start.6 = (f32[8,16,128]{2,1,0:T(8,128)S(1)}, f32[8,16,128]{2,1,0:T(8,128)S(1)}, u32[]{:S(2)}, u32[]{:S(2)}) collective-permute-start(f32[8,16,128]{2,1,0:T(8,128)S(1)} %get-tuple-element.23.own), channel_id=1, source_target_pairs={{4,8},{12,16},{20,24},{8,4},{16,12},{24,20},{5,9},{13,17},{21,25},... | collective-permute-start | bytes 196616 | tf_op jit(solution)/shard_map/ppermute | solution.py:519
  26.0 3.5 %collective-permute-start.7 = (f32[8,16,128]{2,1,0:T(8,128)S(1)}, f32[8,16,128]{2,1,0:T(8,128)S(1)}, u32[]{:S(2)}, u32[]{:S(2)}) collective-permute-start(f32[8,16,128]{2,1,0:T(8,128)S(1)} %get-tuple-element.23.own), channel_id=1, source_target_pairs={{0,4},{8,12},{16,20},{24,28},{4,0},{12,8},{20,16},{28,24},{1,5},{9... | collective-permute-start | bytes 196616 | tf_op jit(solution)/shard_map/ppermute | solution.py:519
  29.5 6.7 %collective-permute-start.10 = (f32[224,128]{1,0:T(8,128)S(1)}, f32[224,128]{1,0:T(8,128)S(1)}, u32[]{:S(2)}, u32[]{:S(2)}) collective-permute-start(f32[224,128]{1,0:T(8,128)S(1)} %get-tuple-element.24), channel_id=1, source_target_pairs={{1,2},{2,1},{5,6},{6,5},{9,10},{10,9},{13,14},{14,13},{17,18},{18,... | collective-permute-start | bytes 344072 | tf_op jit(solution)/shard_map/ppermute | solution.py:519
  31.9 4.9 %collective-permute-start.11 = (f32[224,128]{1,0:T(8,128)S(1)}, f32[224,128]{1,0:T(8,128)S(1)}, u32[]{:S(2)}, u32[]{:S(2)}) collective-permute-start(f32[224,128]{1,0:T(8,128)S(1)} %get-tuple-element.25), channel_id=1, source_target_pairs={{0,1},{2,3},{1,0},{3,2},{4,5},{6,7},{5,4},{7,6},{8,9},{10,11},{9,8... | collective-permute-start | bytes 344072 | tf_op jit(solution)/shard_map/ppermute | solution.py:519

commit v6 on v5

--- a/solution.py
+++ b/solution.py
@@ -541,7 +541,7 @@
         fields,
         "rim_rows",
         pltpu.HBM,
-        63,
+        62,
     )
     rims = swapped("blk", *rims)
     early = (EDGES * y_size, lanes)
@@ -553,6 +553,7 @@
         "edges_early",
     )
     earlies = swapped("grp", *earlies)
+    rims, spans = lax.optimization_barrier((rims, spans))
     late = (late_pieces(y_size)[1], lanes)
     lates = call(functools.partial(late_kernel, *sizes), [late, late], edge_scratch, (*fields, *rims), "edges_late")
     lates = swapped("grp", *lates)

time: 39.1 us -> 40.3 us (1.031)
  waiting for transfers between devices: 7.62 us -> 11.5 us
  local copies, waits for them, and re-layouts: 1.31 us -> 0.03 us
  starting transfers between devices: 19.9 us -> 18.7 us
    ppermute x12, waiting for transfers between devices: 7.62 us -> 11.5 us  [swapped(): lax.ppermute(message, axis, pairs + [(j, i) for i, j in pairs])]
    unnamed x12, local copies, waits for them, and re-layouts: 1.31 us -> 0.03 us
    ppermute x12, starting transfers between devices: 19.9 us -> 18.7 us  [swapped(): lax.ppermute(message, axis, pairs + [(j, i) for i, j in pairs])]
  transfers between devices with their start and end apart: 12 -> 12, of which waited for: 4 -> 5; matrix products, arithmetic and copies ran while one was open for 0% -> 0% of each run, Pallas kernels for 12% -> 7%
where the time goes in v6:
time: 40.3 us; the launch traced here: 40.1 us
  starting transfers between devices  18.7 us (46%)
  waiting for transfers between devices  11.5 us (29%)
  Pallas kernels  9 us (22%)
  between operations  0.85 us (2%)
    ppermute x12, starting transfers between devices, swapped(): lax.ppermute(message, axis, pairs + [(j, i) for i, j in pairs])  18.7 us
    ppermute x12, waiting for transfers between devices, swapped(): lax.ppermute(message, axis, pairs + [(j, i) for i, j in pairs])  11.5 us
    pallas_call x8, Pallas kernels, call(): pl.pallas_call(kernel, out_shape=[jax.ShapeDtypeStruct(shape, jnp.float32...  9 us
  transfers between devices with their start and end apart: 12, of which 5 were waited for; matrix products, arithmetic and copies ran while one was open for 0% of the time, Pallas kernels for 7%

profile of v6, /device:TPU:12, one launch (start us, length us, event | category | flops | bytes accessed | tf_op | source)
XLA Modules:
  0.0 40.1 jit_solution(7466836449262226906)
XLA Ops:
  0.7 2.4 %rim_rows.1 = (f32[384,128]{1,0:T(8,128)}, f32[384,128]{1,0:T(8,128)}) custom-call(f32[152,16,128]{2,1,0:T(8,128)} %bitcast.3, f32[24,16,128]{2,1,0:T(8,128)} %bitcast.7, f32[8,16,128]{2,1,0:T(8,128)} %grad.5, s32[8,16,128]{2,1,0:T(8,128)} %fluid.5), custom_call_target="tpu_custom_call" | custom-call | tf_op jit(solution)/shard_map/rim_rows/pallas_call | solution.py:503
  3.1 3.5 %collective-permute-start = (f32[384,128]{1,0:T(8,128)}, f32[384,128]{1,0:T(8,128)S(1)}, u32[]{:S(2)}, u32[]{:S(2)}) collective-permute-start(f32[384,128]{1,0:T(8,128)} %get-tuple-element.19), channel_id=1, source_target_pairs={{1,2},{2,1},{5,6},{6,5},{9,10},{10,9},{13,14},{14,13},{17,18},{18,... | collective-permute-start | bytes 589832 | tf_op jit(solution)/shard_map/ppermute | solution.py:519
  6.6 0.1 collective-permute-start.1
  6.7 2.5 %collective-permute-start.2 = (s32[8,16,128]{2,1,0:T(8,128)}, s32[8,16,128]{2,1,0:T(8,128)S(1)}, u32[]{:S(2)}, u32[]{:S(2)}) collective-permute-start(s32[8,16,128]{2,1,0:T(8,128)} %span.3), channel_id=1, source_target_pairs={{4,8},{12,16},{20,24},{8,4},{16,12},{24,20},{5,9},{13,17},{21,25},... | collective-permute-start | bytes 196616 | tf_op jit(solution)/shard_map/ppermute | solution.py:519
  9.2 0.5 %edges_early.1 = (f32[304,128]{1,0:T(8,128)S(1)}, f32[304,128]{1,0:T(8,128)S(1)}) custom-call(f32[152,16,128]{2,1,0:T(8,128)S(1)} %bitcast.4, f32[24,16,128]{2,1,0:T(8,128)S(1)} %bitcast.8, f32[8,16,128]{2,1,0:T(8,128)S(1)} %copy-done.2, s32[8,16,128]{2,1,0:T(8,128)S(1)} %copy-done.3), custom_call_target="tpu_custom_call" | custom-call | tf_op jit(solution)/shard_map/edges_early/pallas_call | solution.py:503
  9.7 4.1 %collective-permute-start.4 = (f32[304,128]{1,0:T(8,128)S(1)}, f32[304,128]{1,0:T(8,128)S(1)}, u32[]{:S(2)}, u32[]{:S(2)}) collective-permute-start(f32[304,128]{1,0:T(8,128)S(1)} %get-tuple-element.23), channel_id=1, source_target_pairs={{4,8},{12,16},{20,24},{8,4},{16,12},{24,20},{5,9},{13,17},{21,25},... | collective-permute-start | bytes 466952 | tf_op jit(solution)/shard_map/ppermute | solution.py:519
  13.8 0.1 collective-permute-start.5
  13.9 0.5 %collective-permute-start.3 = (s32[8,16,128]{2,1,0:T(8,128)S(1)}, s32[8,16,128]{2,1,0:T(8,128)S(1)}, u32[]{:S(2)}, u32[]{:S(2)}) collective-permute-start(s32[8,16,128]{2,1,0:T(8,128)S(1)} %copy-done.4), channel_id=1, source_target_pairs={{0,4},{8,12},{16,20},{24,28},{4,0},{12,8},{20,16},{28,24},{1,5},{9... | collective-permute-start | bytes 196616 | tf_op jit(solution)/shard_map/ppermute | solution.py:519
  14.4 1.0 %collective-permute-done.3.span_a = s32[8,16,128]{2,1,0:T(8,128)S(1)} collective-permute-done((s32[8,16,128]{2,1,0:T(8,128)S(1)}, s32[8,16,128]{2,1,0:T(8,128)S(1)}, u32[]{:S(2)}, u32[]{:S(2)}) %collective-permute-start.3) | collective-permute-done | bytes 65568 | tf_op jit(solution)/shard_map/ppermute | solution.py:519
  15.3 0.8 %edges_late.1 = (f32[112,128]{1,0:T(8,128)S(1)}, f32[112,128]{1,0:T(8,128)S(1)}) custom-call(f32[152,16,128]{2,1,0:T(8,128)S(1)} %bitcast.5, f32[24,16,128]{2,1,0:T(8,128)S(1)} %bitcast.9, f32[8,16,128]{2,1,0:T(8,128)S(1)} %copy-done.2, s32[8,16,128]{2,1,0:T(8,128)S(1)} %copy-done.3, f32[384,128]{1,0:T(8,128)S(1)} %collective-permute-done.rim_b, ...), custom_call_target="tpu_custom_call" | custom-call | tf_op jit(solution)/shard_map/edges_late/pallas_call | solution.py:503
  16.2 2.5 %collective-permute-start.6 = (f32[112,128]{1,0:T(8,128)S(1)}, f32[112,128]{1,0:T(8,128)S(1)}, u32[]{:S(2)}, u32[]{:S(2)}) collective-permute-start(f32[112,128]{1,0:T(8,128)S(1)} %get-tuple-element.25), channel_id=1, source_target_pairs={{4,8},{12,16},{20,24},{8,4},{16,12},{24,20},{5,9},{13,17},{21,25},... | collective-permute-start | bytes 172040 | tf_op jit(solution)/shard_map/ppermute | solution.py:519
  18.7 0.2 collective-permute-start.7
  18.9 3.7 %collective-permute-done.6.late_b = f32[112,128]{1,0:T(8,128)S(1)} collective-permute-done((f32[112,128]{1,0:T(8,128)S(1)}, f32[112,128]{1,0:T(8,128)S(1)}, u32[]{:S(2)}, u32[]{:S(2)}) %collective-permute-start.6) | collective-permute-done | bytes 57376 | tf_op jit(solution)/shard_map/ppermute | solution.py:519
  22.6 1.8 %two_steps_and_sens.1 = (f32[8,16,128]{2,1,0:T(8,128)S(1)}, f32[190,32,128]{2,1,0:T(8,128)S(1)}, f32[48,32,128]{2,1,0:T(8,128)S(1)}) custom-call(f32[152,16,128]{2,1,0:T(8,128)S(1)} %bitcast.6, f32[24,16,128]{2,1,0:T(8,128)S(1)} %bitcast.10, f32[8,16,128]{2,1,0:T(8,128)S(1)} %copy-done.2, s32[8,16,128]{2,1,0:T(8,128)S(1)} %copy-done.3, ...), custom_call_target="tpu_custom_call" | custom-call | tf_op jit(solution)/shard_map/two_steps_and_sens/pallas_call | solution.py:503
  24.4 2.5 %collective-permute-start.8 = (f32[8,16,128]{2,1,0:T(8,128)S(1)}, f32[8,16,128]{2,1,0:T(8,128)S(1)}, u32[]{:S(2)}, u32[]{:S(2)}) collective-permute-start(f32[8,16,128]{2,1,0:T(8,128)S(1)} %get-tuple-element.29.own), channel_id=1, source_target_pairs={{4,8},{12,16},{20,24},{8,4},{16,12},{24,20},{5,9},{13,17},{21,25},... | collective-permute-start | bytes 196616 | tf_op jit(solution)/shard_map/ppermute | solution.py:519
  26.9 0.1 collective-permute-start.9
  27.0 3.9 %collective-permute-done.8.beside_b = f32[8,16,128]{2,1,0:T(8,128)S(1)} collective-permute-done((f32[8,16,128]{2,1,0:T(8,128)S(1)}, f32[8,16,128]{2,1,0:T(8,128)S(1)}, u32[]{:S(2)}, u32[]{:S(2)}) %collective-permute-start.8) | collective-permute-done | bytes 65568 | tf_op jit(solution)/shard_map/ppermute | solution.py:519
  30.9 2.4 %collective-permute-start.10 = (f32[224,128]{1,0:T(8,128)S(1)}, f32[224,128]{1,0:T(8,128)S(1)}, u32[]{:S(2)}, u32[]{:S(2)}) collective-permute-start(f32[224,128]{1,0:T(8,128)S(1)} %get-tuple-element.32), channel_id=1, source_target_pairs={{1,2},{2,1},{5,6},{6,5},{9,10},{10,9},{13,14},{14,13},{17,18},{18,... | collective-permute-start | bytes 344072 | tf_op jit(solution)/shard_map/ppermute | solution.py:519
  33.3 0.4 collective-permute-start.11
  33.7 0.2 radius.1
  33.8 1.4 %third_step.1 = f32[152,16,128]{2,1,0:T(8,128)} custom-call(f32[190,32,128]{2,1,0:T(8,128)S(1)} %get-tuple-element.27.state, f32[48,32,128]{2,1,0:T(8,128)S(1)} %get-tuple-element.28.coef), custom_call_target="tpu_custom_call" | custom-call | tf_op jit(solution)/shard_map/third_step/pallas_call | solution.py:503
  35.2 2.4 %collective-permute-done.10.band_b = f32[224,128]{1,0:T(8,128)S(1)} collective-permute-done((f32[224,128]{1,0:T(8,128)S(1)}, f32[224,128]{1,0:T(8,128)S(1)}, u32[]{:S(2)}, u32[]{:S(2)}) %collective-permute-start.10) | collective-permute-done | bytes 114720 | tf_op jit(solution)/shard_map/ppermute | solution.py:519
  37.6 0.5 %collective-permute-done.11.band_a = f32[224,128]{1,0:T(8,128)S(1)} collective-permute-done((f32[224,128]{1,0:T(8,128)S(1)}, f32[224,128]{1,0:T(8,128)S(1)}, u32[]{:S(2)}, u32[]{:S(2)}) %collective-permute-start.11) | collective-permute-done | bytes 114720 | tf_op jit(solution)/shard_map/ppermute | solution.py:519
  38.2 1.9 %eight_sweeps.1 = f32[8,16,128]{2,1,0:T(8,128)} custom-call(f32[8,16,128]{2,1,0:T(8,128)S(1)} %get-tuple-element.29.own, f32[8,16,128]{2,1,0:T(8,128)S(1)} %collective-permute-done.8.beside_b, f32[8,16,128]{2,1,0:T(8,128)S(1)} %collective-permute-done.9.beside_a, f32[224,128]{1,0:T(8,128)S(1)} %collective-permute-done.10.band_b, ...), custom_call_target="tpu_custom_call" | custom-call | tf_op jit(solution)/shard_map/eight_sweeps/pallas_call | solution.py:503
  (20 shorter events, 0.1 us)
Async XLA Ops:
  0.6 8.5 %copy-start = (f32[19,8,16,128]{3,2,1,0:T(8,128)S(1)}, f32[19,8,16,128]{3,2,1,0:T(8,128)}, u32[]{:S(2)}) copy-start(f32[19,8,16,128]{3,2,1,0:T(8,128)} %param.6) | copy-start | bytes 3735556
  0.6 8.5 %copy-start.1 = (f32[3,8,16,128]{3,2,1,0:T(8,128)S(1)}, f32[3,8,16,128]{3,2,1,0:T(8,128)}, u32[]{:S(2)}) copy-start(f32[3,8,16,128]{3,2,1,0:T(8,128)} %param.7) | copy-start | bytes 589828
  0.7 8.5 %copy-start.3 = (s32[8,16,128]{2,1,0:T(8,128)S(1)}, s32[8,16,128]{2,1,0:T(8,128)}, u32[]{:S(2)}) copy-start(s32[8,16,128]{2,1,0:T(8,128)} %fluid.5) | copy-start | bytes 196612
  0.7 8.5 %copy-start.2 = (f32[8,16,128]{2,1,0:T(8,128)S(1)}, f32[8,16,128]{2,1,0:T(8,128)}, u32[]{:S(2)}) copy-start(f32[8,16,128]{2,1,0:T(8,128)} %grad.5) | copy-start | bytes 196612
  0.7 13.2 %copy-start.4 = (s32[8,16,128]{2,1,0:T(8,128)S(1)}, s32[8,16,128]{2,1,0:T(8,128)}, u32[]{:S(2)}) copy-start(s32[8,16,128]{2,1,0:T(8,128)} %span.3) | copy-start | bytes 196612
  3.1 12.2 %collective-permute-start = (f32[384,128]{1,0:T(8,128)}, f32[384,128]{1,0:T(8,128)S(1)}, u32[]{:S(2)}, u32[]{:S(2)}) collective-permute-start(f32[384,128]{1,0:T(8,128)} %get-tuple-element.19), channel_id=1, source_target_pairs={{1,2},{2,1},{5,6},{6,5},{9,10},{10,9},{13,14},{14,13},{17,18},{18,... | collective-permute-start | bytes 589832 | tf_op jit(solution)/shard_map/ppermute | solution.py:519
  6.6 8.8 %collective-permute-start.1 = (f32[384,128]{1,0:T(8,128)}, f32[384,128]{1,0:T(8,128)S(1)}, u32[]{:S(2)}, u32[]{:S(2)}) collective-permute-start(f32[384,128]{1,0:T(8,128)} %get-tuple-element.20), channel_id=1, source_target_pairs={{0,1},{2,3},{1,0},{3,2},{4,5},{6,7},{5,4},{7,6},{8,9},{10,11},{9,8... | collective-permute-start | bytes 589832 | tf_op jit(solution)/shard_map/ppermute | solution.py:519
  6.7 7.2 %collective-permute-start.2 = (s32[8,16,128]{2,1,0:T(8,128)}, s32[8,16,128]{2,1,0:T(8,128)S(1)}, u32[]{:S(2)}, u32[]{:S(2)}) collective-permute-start(s32[8,16,128]{2,1,0:T(8,128)} %span.3), channel_id=1, source_target_pairs={{4,8},{12,16},{20,24},{8,4},{16,12},{24,20},{5,9},{13,17},{21,25},... | collective-permute-start | bytes 196616 | tf_op jit(solution)/shard_map/ppermute | solution.py:519
  9.7 12.9 %copy-start.5 = (f32[8,16,128]{2,1,0:T(8,128)S(1)}, f32[8,16,128]{2,1,0:T(8,128)}, u32[]{:S(2)}) copy-start(f32[8,16,128]{2,1,0:T(8,128)} %heat.1) | copy-start | bytes 196612
  9.7 9.2 %collective-permute-start.4 = (f32[304,128]{1,0:T(8,128)S(1)}, f32[304,128]{1,0:T(8,128)S(1)}, u32[]{:S(2)}, u32[]{:S(2)}) collective-permute-start(f32[304,128]{1,0:T(8,128)S(1)} %get-tuple-element.23), channel_id=1, source_target_pairs={{4,8},{12,16},{20,24},{8,4},{16,12},{24,20},{5,9},{13,17},{21,25},... | collective-permute-start | bytes 466952 | tf_op jit(solution)/shard_map/ppermute | solution.py:519
  13.8 5.1 %collective-permute-start.5 = (f32[304,128]{1,0:T(8,128)S(1)}, f32[304,128]{1,0:T(8,128)S(1)}, u32[]{:S(2)}, u32[]{:S(2)}) collective-permute-start(f32[304,128]{1,0:T(8,128)S(1)} %get-tuple-element.24), channel_id=1, source_target_pairs={{0,4},{8,12},{16,20},{24,28},{4,0},{12,8},{20,16},{28,24},{1,5},{9... | collective-permute-start | bytes 466952 | tf_op jit(solution)/shard_map/ppermute | solution.py:519
  13.9 1.4 %collective-permute-start.3 = (s32[8,16,128]{2,1,0:T(8,128)S(1)}, s32[8,16,128]{2,1,0:T(8,128)S(1)}, u32[]{:S(2)}, u32[]{:S(2)}) collective-permute-start(s32[8,16,128]{2,1,0:T(8,128)S(1)} %copy-done.4), channel_id=1, source_target_pairs={{0,4},{8,12},{16,20},{24,28},{4,0},{12,8},{20,16},{28,24},{1,5},{9... | collective-permute-start | bytes 196616 | tf_op jit(solution)/shard_map/ppermute | solution.py:519
  16.2 6.4 %collective-permute-start.6 = (f32[112,128]{1,0:T(8,128)S(1)}, f32[112,128]{1,0:T(8,128)S(1)}, u32[]{:S(2)}, u32[]{:S(2)}) collective-permute-start(f32[112,128]{1,0:T(8,128)S(1)} %get-tuple-element.25), channel_id=1, source_target_pairs={{4,8},{12,16},{20,24},{8,4},{16,12},{24,20},{5,9},{13,17},{21,25},... | collective-permute-start | bytes 172040 | tf_op jit(solution)/shard_map/ppermute | solution.py:519
  18.7 3.9 %collective-permute-start.7 = (f32[112,128]{1,0:T(8,128)S(1)}, f32[112,128]{1,0:T(8,128)S(1)}, u32[]{:S(2)}, u32[]{:S(2)}) collective-permute-start(f32[112,128]{1,0:T(8,128)S(1)} %get-tuple-element.26), channel_id=1, source_target_pairs={{0,4},{8,12},{16,20},{24,28},{4,0},{12,8},{20,16},{28,24},{1,5},{9... | collective-permute-start | bytes 172040 | tf_op jit(solution)/shard_map/ppermute | solution.py:519
  24.4 6.5 %collective-permute-start.8 = (f32[8,16,128]{2,1,0:T(8,128)S(1)}, f32[8,16,128]{2,1,0:T(8,128)S(1)}, u32[]{:S(2)}, u32[]{:S(2)}) collective-permute-start(f32[8,16,128]{2,1,0:T(8,128)S(1)} %get-tuple-element.29.own), channel_id=1, source_target_pairs={{4,8},{12,16},{20,24},{8,4},{16,12},{24,20},{5,9},{13,17},{21,25},... | collective-permute-start | bytes 196616 | tf_op jit(solution)/shard_map/ppermute | solution.py:519
  26.9 3.9 %collective-permute-start.9 = (f32[8,16,128]{2,1,0:T(8,128)S(1)}, f32[8,16,128]{2,1,0:T(8,128)S(1)}, u32[]{:S(2)}, u32[]{:S(2)}) collective-permute-start(f32[8,16,128]{2,1,0:T(8,128)S(1)} %get-tuple-element.29.own), channel_id=1, source_target_pairs={{0,4},{8,12},{16,20},{24,28},{4,0},{12,8},{20,16},{28,24},{1,5},{9... | collective-permute-start | bytes 196616 | tf_op jit(solution)/shard_map/ppermute | solution.py:519
  30.9 6.7 %collective-permute-start.10 = (f32[224,128]{1,0:T(8,128)S(1)}, f32[224,128]{1,0:T(8,128)S(1)}, u32[]{:S(2)}, u32[]{:S(2)}) collective-permute-start(f32[224,128]{1,0:T(8,128)S(1)} %get-tuple-element.32), channel_id=1, source_target_pairs={{1,2},{2,1},{5,6},{6,5},{9,10},{10,9},{13,14},{14,13},{17,18},{18,... | collective-permute-start | bytes 344072 | tf_op jit(solution)/shard_map/ppermute | solution.py:519
  33.3 4.9 %collective-permute-start.11 = (f32[224,128]{1,0:T(8,128)S(1)}, f32[224,128]{1,0:T(8,128)S(1)}, u32[]{:S(2)}, u32[]{:S(2)}) collective-permute-start(f32[224,128]{1,0:T(8,128)S(1)} %get-tuple-element.33), channel_id=1, source_target_pairs={{0,1},{2,3},{1,0},{3,2},{4,5},{6,7},{5,4},{7,6},{8,9},{10,11},{9,8... | collective-permute-start | bytes 344072 | tf_op jit(solution)/shard_map/ppermute | solution.py:519

commit v7 on v5

--- a/solution.py
+++ b/solution.py
@@ -177,13 +177,14 @@
 
 
 def rim_kernel(x_size, y_size, *refs):
-    sources, messages, held, arrived = refs[:4], (refs[5], refs[4]), refs[6:10], refs[10]
-    copies = [pltpu.make_async_copy(a, b, arrived.at[n]) for n, (a, b) in enumerate(zip(sources, held))]
+    sources, (b, a, state, coef, heat, radii), held, arrived = refs[:6], refs[6:12], refs[12:17], refs[17]
+    messages = (a, b)
+    copies = [pltpu.make_async_copy(a, b, arrived.at[n]) for n, (a, b) in enumerate(zip(sources, (*held, heat)))]
     for copy in copies:
         copy.start()
     for copy in copies:
         copy.wait()
-    dual, vel, grad, fluid = held
+    dual, vel, grad, fluid, span = held
     lanes = dual.shape[-1]
     flat = [ref.reshape(ref.shape[0] * y_size, lanes) for ref in (dual, vel, fluid, grad)]
     for after, out in zip(toward_next("blk"), messages):
@@ -194,6 +195,9 @@
             if kind == 2:
                 value = value.astype(jnp.float32) + 1.0
             out[pl.ds(k * x_size, x_size), :] = value
+    extend_own(x_size, y_size, dual, vel, grad, fluid, state, coef)
+    for x in range(x_size):
+        radii[x] = span[x].astype(jnp.float32)
 
 
 def edge_steps(x_size, after, state, coef, near, far, raw, first, second, put):
@@ -255,8 +259,7 @@
 EARLY = (0, 5, 10, 15)
 
 
-def early_kernel(x_size, y_size, dual, vel, grad, fluid, early_b, early_a, state, coef, near, far):
-    extend_own(x_size, y_size, dual, vel, grad, fluid, state, coef)
+def early_kernel(x_size, y_size, state, coef, span, early_b, early_a, near, far):
     rows = range(PAD, PAD + y_size, 8)
     for after, out in zip(toward_next("grp"), (early_a, early_b)):
 
@@ -264,6 +267,8 @@
             out[pl.ds((EARLY[kind] + n) * y_size + at - PAD, 8), :] = value
 
         edge_steps(x_size, after, state, coef, near, far, rows, rows, rows, put)
+        for x in range(x_size):
+            out[pl.ds((EDGES + x) * y_size, y_size), :] = span[x]
 
 
 def late_pieces(y_size):
@@ -277,8 +282,7 @@
     return pieces, -(-offset // 8) * 8
 
 
-def late_kernel(x_size, y_size, dual, vel, grad, fluid, rim_b, rim_a, late_b, late_a, state, coef, near, far):
-    extend_own(x_size, y_size, dual, vel, grad, fluid, state, coef)
+def late_kernel(x_size, y_size, _state, _coef, rim_b, rim_a, late_b, late_a, state, coef, near, far):
     extend_rims(x_size, y_size, (rim_a, rim_b), state, coef)
     pieces, _ = late_pieces(y_size)
     starts = [(PAD - reach, PAD + y_size + reach - 8) for reach in (3, 2, 1)]
@@ -291,12 +295,49 @@
         edge_steps(x_size, after, state, coef, near, far, *starts, put)
 
 
-def steps_kernel(
-    x_size, y_size, dual, vel, grad, fluid, rim_b, rim_a, heat, early_b, early_a, late_b, late_a,
-    sens, state, coef, later, shifts, extra, halos,
+def step_plane(x_size, y_size, number, x, source, target, coef, shifts):
+    planes = x_size + 2
+    for j in range((y_size + 8) // 8):
+        at = FIRST + 8 * j
+        keep, rate, *u, drive = [coef[n * x_size + x, pl.ds(at, 8), :] for n in range(6)]
+        p = pulled_from(reader(planes, source, x, at), range(POPS))
+        shift, equilib = relaxed(p, u)
+        shifts[(number - 1) * x_size + x, pl.ds(at, 8), :] = shift
+        posts = posts_of(p, keep, equilib, rate, drive, range(POPS))
+        for i in range(POPS):
+            target[i * planes + x + 1, pl.ds(at, 8), :] = posts[i]
+
+
+def reader(planes, source, x, at):
+    def read(i):
+        cx, cy, _ = VELOCITIES[i]
+        return source[i * planes + x + 1 + cx, pl.ds(at + cy, 8), :]
+
+    return read
+
+
+def sens_plane(x_size, y_size, x, state, coef, shifts, heat, sens):
+    for j in range(y_size // 8):
+        at = PAD + 8 * j
+        u = [coef[n * x_size + x, pl.ds(at, 8), :] for n in (2, 3, 4)]
+        p = pulled_from(reader(x_size + 2, state, x, at), range(1, POPS))
+        shift = shifts[x, pl.ds(at, 8), :] + shifts[x_size + x, pl.ds(at, 8), :] + relaxed(p, u)[0]
+        sens[x, pl.ds(8 * j, 8), :] = heat[x, pl.ds(8 * j, 8), :] * shift
+
+
+def inner_kernel(x_size, y_size, state, coef, heat, state_1, state_2, shifts, sens):
+    for x in range(1, x_size - 1):
+        step_plane(x_size, y_size, 1, x, state, state_1, coef, shifts)
+    for x in range(2, x_size - 2):
+        step_plane(x_size, y_size, 2, x, state_1, state_2, coef, shifts)
+    for x in range(3, x_size - 3):
+        sens_plane(x_size, y_size, x, state_2, coef, shifts, heat, sens)
+
+
+def outer_kernel(
+    x_size, y_size, coef, heat, early_b, early_a, late_b, late_a, _state, _state_1, _state_2, _shifts, _sens,
+    state, state_1, state_2, shifts, sens, extra, halos,
 ):
-    extend_own(x_size, y_size, dual, vel, grad, fluid, state, coef)
-    extend_rims(x_size, y_size, (rim_a, rim_b), state, coef)
     planes = x_size + 2
     window = y_size + 8
     groups = window // 8
@@ -316,27 +357,9 @@
                     begin, rows, offset = pieces[kind, end]
                     ref[plane, pl.ds(begin, rows), :] = late[pl.ds(offset + n * rows, rows), :]
 
-    def read_from(source, x, at):
-        def read(i):
-            cx, cy, _ = VELOCITIES[i]
-            return source[i * planes + x + 1 + cx, pl.ds(at + cy, 8), :]
-
-        return read
-
-    def step(number, source, target):
-        def plane(x, _):
-            for j in range(groups):
-                at = FIRST + 8 * j
-                keep, rate, *u, drive = [coef[n * x_size + x, pl.ds(at, 8), :] for n in range(6)]
-                p = pulled_from(read_from(source, x, at), range(POPS))
-                shift, equilib = relaxed(p, u)
-                shifts[(number - 1) * x_size + x, pl.ds(at, 8), :] = shift
-                posts = posts_of(p, keep, equilib, rate, drive, range(POPS))
-                for i in range(POPS):
-                    target[i * planes + x + 1, pl.ds(at, 8), :] = posts[i]
-            return 0
-
-        lax.fori_loop(0, x_size, plane, 0, unroll=True)
+    for number, source, target in ((1, state, state_1), (2, state_1, state_2)):
+        for x in (*range(number), *range(x_size - number, x_size)):
+            step_plane(x_size, y_size, number, x, source, target, coef, shifts)
         for side, after in enumerate(afters):
             halo = jnp.where(after, x_size + 1, 0)
             edge = jnp.where(after, x_size, 1)
@@ -360,21 +383,8 @@
                     target[pick(after, i, mirrored(i, 0)) * planes + halo, pl.ds(at, 8), :] = (
                         halos[side * 14 + 5 * number - 5 + n, pl.ds(at, 8), :] + added
                     )
-
-    step(1, state, later)
-    step(2, later, state)
-
-    def last(x, _):
-        for j in range(y_size // 8):
-            at = PAD + 8 * j
-            u = [coef[n * x_size + x, pl.ds(at, 8), :] for n in (2, 3, 4)]
-            p = pulled_from(read_from(state, x, at), range(1, POPS))
-            shift = relaxed(p, u)[0]
-            shift = shifts[x, pl.ds(at, 8), :] + shifts[x_size + x, pl.ds(at, 8), :] + shift
-            sens[x, pl.ds(8 * j, 8), :] = heat[x, pl.ds(8 * j, 8), :] * shift
-        return 0
-
-    lax.fori_loop(0, x_size, last, 0, unroll=True)
+    for x in (*range(3), *range(x_size - 3, x_size)):
+        sens_plane(x_size, y_size, x, state_2, coef, shifts, heat, sens)
 
 
 def adjoint_kernel(x_size, y_size, state, coef, adjoint):
@@ -421,6 +431,7 @@
         for refs, reach, base in (((own, beside_a, beside_b), REACH, 0), ((span, span_a, span_b), REACH - 1, skip)):
             for slot, k, rows, offset in diamond(x_size, reach)[0]:
                 _, plane = slot_plane(x_size, slot, k)
+                plane = plane + EDGES if slot > 0 and base > 0 else plane
                 value = refs[slot][plane, pl.ds(jnp.where(after, y_size - rows, 0), rows), :]
                 out[pl.ds(base + offset, rows), :] = value.astype(jnp.float32)
 
@@ -445,7 +456,7 @@
 
         def plane(x, _, slot=slot, ref=ref, inside=inside):
             place, k = slot_plane(x_size, slot, x)
-            inverse[place], beta[place] = shares(ref[k].astype(jnp.float32), inside)
+            inverse[place], beta[place] = shares(ref[k if slot == 0 else EDGES + k].astype(jnp.float32), inside)
             return 0
 
         lax.fori_loop(0, x_size, plane, 0, unroll=4)
@@ -499,14 +510,15 @@
         source, target = target, source
 
 
-def call(kernel, outs, scratch, args, name, place=pltpu.VMEM, grant=32):
+def call(kernel, outs, scratch, args, name, place=pltpu.VMEM, in_place=()):
     return pl.pallas_call(
         kernel,
         out_shape=[jax.ShapeDtypeStruct(shape, jnp.float32) for shape in outs],
         in_specs=[pl.BlockSpec(memory_space=place)] * len(args),
         out_specs=[pl.BlockSpec(memory_space=pltpu.VMEM)] * len(outs),
         scratch_shapes=[pltpu.VMEM(s, jnp.float32) if isinstance(s, tuple) else s for s in scratch],
-        compiler_params=pltpu.CompilerParams(vmem_limit_bytes=grant * 1024 * 1024),
+        compiler_params=pltpu.CompilerParams(vmem_limit_bytes=32 * 1024 * 1024),
+        input_output_aliases=dict(in_place),
         name=name,
     )(*args)
 
@@ -533,46 +545,64 @@
     coef = (6 * x_size, pitch, lanes)
     edge_scratch = [state, coef, (len(LEVEL), pitch, lanes), (len(RIGHT), pitch, lanes)]
 
-    spans = swapped("grp", filter_span_group, filter_span_group)
-    rims = call(
+    own = (x_size, y_size, lanes)
+    fields = (*fields, filter_span_group, forward_heat_level)
+    *rims, state_0, coefs, heat, span = call(
         functools.partial(rim_kernel, *sizes),
-        [rim, rim],
-        [pltpu.VMEM(f.shape, f.dtype) for f in fields] + [pltpu.SemaphoreType.DMA((len(fields),))],
-        fields,
+        [rim, rim, state, coef, own, own],
+        [pltpu.VMEM(f.shape, f.dtype) for f in fields[:-1]] + [pltpu.SemaphoreType.DMA((len(fields),))],
+        [pltpu.with_memory_space_constraint(f, pltpu.HBM) for f in fields],
         "rim_rows",
         pltpu.HBM,
-        63,
     )
     rims = swapped("blk", *rims)
-    early = (EDGES * y_size, lanes)
+    early = ((EDGES + x_size) * y_size, lanes)
+    near_far = [(len(LEVEL), pitch, lanes), (len(RIGHT), pitch, lanes)]
     earlies = call(
         functools.partial(early_kernel, *sizes),
         [early, early],
-        edge_scratch,
-        fields,
+        near_far,
+        (state_0, coefs, span),
         "edges_early",
     )
     earlies = swapped("grp", *earlies)
     late = (late_pieces(y_size)[1], lanes)
-    lates = call(functools.partial(late_kernel, *sizes), [late, late], edge_scratch, (*fields, *rims), "edges_late")
+    *lates, state_0, coefs = call(
+        functools.partial(late_kernel, *sizes),
+        [late, late, state, coef],
+        near_far,
+        (state_0, coefs, *rims),
+        "edges_late",
+        in_place=((0, 2), (1, 3)),
+    )
     lates = swapped("grp", *lates)
-    sens, state_2, coefs = call(
-        functools.partial(steps_kernel, *sizes),
-        [(x_size, y_size, lanes), state, coef],
-        [state, (2 * x_size, pitch, lanes), (2, pitch, lanes), (28, pitch, lanes)],
-        (*fields, *rims, forward_heat_level, *earlies, *lates),
-        "two_steps_and_sens",
-    )
+    shifts = (2 * x_size, pitch, lanes)
+    inner = call(
+        functools.partial(inner_kernel, *sizes),
+        [state, state, shifts, own],
+        [],
+        (state_0, coefs, heat),
+        "steps_inside",
+    )
+    _, _, state_2, _, sens = call(
+        functools.partial(outer_kernel, *sizes),
+        [state, state, state, shifts, own],
+        [(2, pitch, lanes), (28, pitch, lanes)],
+        (coefs, heat, *earlies, *lates, state_0, *inner),
+        "steps_at_edges",
+        in_place=((6, 0), (7, 1), (8, 2), (9, 3), (10, 4)),
+    )
+    spans = [e.reshape(EDGES + x_size, y_size, lanes) for e in earlies]
     beside = swapped("grp", sens, sens)
     (adjoint,) = call(
         functools.partial(adjoint_kernel, *sizes), [(POPS * x_size, y_size, lanes)], [], (state_2, coefs), "third_step"
     )
     inverse, beta = call(
-        functools.partial(radius_kernel, *sizes), [(3 * x_size, y_size, lanes)] * 2, [], (filter_span_group, *spans), "radius"
+        functools.partial(radius_kernel, *sizes), [(3 * x_size, y_size, lanes)] * 2, [], (span, *spans), "radius"
     )
     band = (diamond(x_size, REACH)[1] + diamond(x_size, REACH - 1)[1], lanes)
     bands = call(
-        functools.partial(band_kernel, *sizes), [band, band], [], (sens, *beside, filter_span_group, *spans), "bands"
+        functools.partial(band_kernel, *sizes), [band, band], [], (sens, *beside, span, *spans), "bands"
     )
     bands = swapped("blk", *bands)
     wide, rows = 3 * x_size, y_size + 2 * REACH

time: 39.1 us -> 36.1 us (0.923)
  starting transfers between devices: 19.9 us -> 15.8 us
  waiting for transfers between devices: 7.62 us -> 11.6 us
  local copies, waits for them, and re-layouts: 1.31 us -> 0 us
  Pallas kernels: 8.94 us -> 7.66 us
    ppermute x12 -> x10, starting transfers between devices: 19.9 us -> 15.8 us  [swapped(): lax.ppermute(message, axis, pairs + [(j, i) for i, j in pairs])]
    ppermute x12 -> x10, waiting for transfers between devices: 7.62 us -> 11.6 us  [swapped(): lax.ppermute(message, axis, pairs + [(j, i) for i, j in pairs])]
    unnamed x12 -> x0, local copies, waits for them, and re-layouts: 1.31 us -> none
    pallas_call x8 -> x9, Pallas kernels: 8.94 us -> 7.66 us  [call(): pl.pallas_call(kernel, out_shape=[jax.ShapeDtypeStruct(shape, jnp.float32...]
  transfers between devices with their start and end apart: 12 -> 10, of which waited for: 4 -> 6; matrix products, arithmetic and copies ran while one was open for 0% -> 0% of each run, Pallas kernels for 12% -> 9%
where the time goes in v7:
time: 36.1 us; the launch traced here: 35.8 us
  starting transfers between devices  15.8 us (44%)
  waiting for transfers between devices  11.6 us (32%)
  Pallas kernels  7.66 us (21%)
  between operations  0.76 us (2%)
    ppermute x10, starting transfers between devices, swapped(): lax.ppermute(message, axis, pairs + [(j, i) for i, j in pairs])  15.8 us
    ppermute x10, waiting for transfers between devices, swapped(): lax.ppermute(message, axis, pairs + [(j, i) for i, j in pairs])  11.6 us
    pallas_call x9, Pallas kernels, call(): pl.pallas_call(kernel, out_shape=[jax.ShapeDtypeStruct(shape, jnp.float32...  7.66 us
  transfers between devices with their start and end apart: 10, of which 6 were waited for; matrix products, arithmetic and copies ran while one was open for 0% of the time, Pallas kernels for 9%

profile of v7, /device:TPU:12, one launch (start us, length us, event | category | flops | bytes accessed | tf_op | source)
XLA Modules:
  0.0 35.8 jit_solution(4131371138500353310)
XLA Ops:
  0.6 1.8 %rim_rows.1 = (f32[384,128]{1,0:T(8,128)S(1)}, f32[384,128]{1,0:T(8,128)S(1)}, f32[190,32,128]{2,1,0:T(8,128)S(1)}, f32[48,32,128]{2,1,0:T(8,128)S(1)}, f32[8,16...) custom-call(f32[152,16,128]{2,1,0:T(8,128)} %bitcast.10, f32[24,16,128]{2,1,0:T(8,128)} %bitcast.11, f32[8,16,128]{2,1,0:T(8,128)} %refs_2_.1, ...), custom_call_target="tpu_custom_call" | custom-call | tf_op jit(solution)/shard_map/rim_rows/pallas_call | solution.py:514
  2.4 3.5 %collective-permute-start = (f32[384,128]{1,0:T(8,128)S(1)}, f32[384,128]{1,0:T(8,128)S(1)}, u32[]{:S(2)}, u32[]{:S(2)}) collective-permute-start(f32[384,128]{1,0:T(8,128)S(1)} %get-tuple-element.26), channel_id=1, source_target_pairs={{1,2},{2,1},{5,6},{6,5},{9,10},{10,9},{13,14},{14,13},{17,18},{18,... | collective-permute-start | bytes 589832 | tf_op jit(solution)/shard_map/ppermute | solution.py:531
  5.9 0.1 collective-permute-start.1
  6.0 0.3 edges_early.1
  6.3 2.5 %collective-permute-start.2 = (f32[432,128]{1,0:T(8,128)S(1)}, f32[432,128]{1,0:T(8,128)S(1)}, u32[]{:S(2)}, u32[]{:S(2)}) collective-permute-start(f32[432,128]{1,0:T(8,128)S(1)} %get-tuple-element.31), channel_id=1, source_target_pairs={{4,8},{12,16},{20,24},{8,4},{16,12},{24,20},{5,9},{13,17},{21,25},... | collective-permute-start | bytes 663560 | tf_op jit(solution)/shard_map/ppermute | solution.py:531
  8.8 1.1 %collective-permute-start.3 = (f32[432,128]{1,0:T(8,128)S(1)}, f32[432,128]{1,0:T(8,128)S(1)}, u32[]{:S(2)}, u32[]{:S(2)}) collective-permute-start(f32[432,128]{1,0:T(8,128)S(1)} %get-tuple-element.32), channel_id=1, source_target_pairs={{0,4},{8,12},{16,20},{24,28},{4,0},{12,8},{20,16},{28,24},{1,5},{9... | collective-permute-start | bytes 663560 | tf_op jit(solution)/shard_map/ppermute | solution.py:531
  9.9 1.1 %collective-permute-done.rim_b = f32[384,128]{1,0:T(8,128)S(1)} collective-permute-done((f32[384,128]{1,0:T(8,128)S(1)}, f32[384,128]{1,0:T(8,128)S(1)}, u32[]{:S(2)}, u32[]{:S(2)}) %collective-permute-start) | collective-permute-done | bytes 196640 | tf_op jit(solution)/shard_map/ppermute | solution.py:531
  11.0 1.4 %collective-permute-done.1.rim_a = f32[384,128]{1,0:T(8,128)S(1)} collective-permute-done((f32[384,128]{1,0:T(8,128)S(1)}, f32[384,128]{1,0:T(8,128)S(1)}, u32[]{:S(2)}, u32[]{:S(2)}) %collective-permute-start.1) | collective-permute-done | bytes 196640 | tf_op jit(solution)/shard_map/ppermute | solution.py:531
  12.4 0.6 %edges_late.1 = (f32[112,128]{1,0:T(8,128)S(1)}, f32[112,128]{1,0:T(8,128)S(1)}, f32[190,32,128]{2,1,0:T(8,128)S(1)}, f32[48,32,128]{2,1,0:T(8,128)S(1)}) custom-call(f32[190,32,128]{2,1,0:T(8,128)S(1)} %get-tuple-element.24._state.state, f32[48,32,128]{2,1,0:T(8,128)S(1)} %get-tuple-element.25._coef.coef, ...), custom_call_target="tpu_custom_call", output_to_operand_aliasing={{2}: (0, {}), {3}: (1, {})} | custom-call | tf_op jit(solution)/shard_map/edges_late/pallas_call | solution.py:514
  13.0 1.9 %collective-permute-start.4 = (f32[112,128]{1,0:T(8,128)S(1)}, f32[112,128]{1,0:T(8,128)S(1)}, u32[]{:S(2)}, u32[]{:S(2)}) collective-permute-start(f32[112,128]{1,0:T(8,128)S(1)} %get-tuple-element.33), channel_id=1, source_target_pairs={{4,8},{12,16},{20,24},{8,4},{16,12},{24,20},{5,9},{13,17},{21,25},... | collective-permute-start | bytes 172040 | tf_op jit(solution)/shard_map/ppermute | solution.py:531
  14.9 1.7 %collective-permute-start.5 = (f32[112,128]{1,0:T(8,128)S(1)}, f32[112,128]{1,0:T(8,128)S(1)}, u32[]{:S(2)}, u32[]{:S(2)}) collective-permute-start(f32[112,128]{1,0:T(8,128)S(1)} %get-tuple-element.34), channel_id=1, source_target_pairs={{0,4},{8,12},{16,20},{24,28},{4,0},{12,8},{20,16},{28,24},{1,5},{9... | collective-permute-start | bytes 172040 | tf_op jit(solution)/shard_map/ppermute | solution.py:531
  16.6 0.7 %steps_inside.1 = (f32[190,32,128]{2,1,0:T(8,128)S(1)}, f32[190,32,128]{2,1,0:T(8,128)S(1)}, f32[16,32,128]{2,1,0:T(8,128)S(1)}, f32[8,16,128]{2,1,0:T(8,128)S(1)}) custom-call(f32[190,32,128]{2,1,0:T(8,128)S(1)} %get-tuple-element.35.state._state, f32[48,32,128]{2,1,0:T(8,128)S(1)} %get-tuple-element.28.coef, f32[8,16,128]{2,1,0:T(8,128)S(1)} %get-tuple-element.29.heat), custom_call_target="tpu_custom_call" | custom-call | tf_op jit(solution)/shard_map/steps_inside/pallas_call | solution.py:514
  17.3 2.1 %collective-permute-done.4.late_b = f32[112,128]{1,0:T(8,128)S(1)} collective-permute-done((f32[112,128]{1,0:T(8,128)S(1)}, f32[112,128]{1,0:T(8,128)S(1)}, u32[]{:S(2)}, u32[]{:S(2)}) %collective-permute-start.4) | collective-permute-done | bytes 57376 | tf_op jit(solution)/shard_map/ppermute | solution.py:531
  19.4 0.8 %steps_at_edges.1 = (f32[190,32,128]{2,1,0:T(8,128)S(1)}, f32[190,32,128]{2,1,0:T(8,128)S(1)}, f32[190,32,128]{2,1,0:T(8,128)S(1)}, f32[16,32,128]{2,1,0:T(8,128)S(1)}, f32[8,16,128]{2,1,0:T(8,128)S(1)}) custom-call(f32[48,32,128]{2,1,0:T(8,128)S(1)} %get-tuple-element.28.coef, ...), custom_call_target="tpu_custom_call", output_to_operand_aliasing={{0}: (6, {}), {1}: (7, {}), {2}: (8, {}), {3}: (9, {}), {4}... | custom-call | tf_op jit(solution)/shard_map/steps_at_edges/pallas_call | solution.py:514
  20.2 1.9 %collective-permute-start.6 = (f32[8,16,128]{2,1,0:T(8,128)S(1)}, f32[8,16,128]{2,1,0:T(8,128)S(1)}, u32[]{:S(2)}, u32[]{:S(2)}) collective-permute-start(f32[8,16,128]{2,1,0:T(8,128)S(1)} %get-tuple-element.41.own), channel_id=1, source_target_pairs={{4,8},{12,16},{20,24},{8,4},{16,12},{24,20},{5,9},{13,17},{21,25},... | collective-permute-start | bytes 196616 | tf_op jit(solution)/shard_map/ppermute | solution.py:531
  22.1 0.8 %collective-permute-start.7 = (f32[8,16,128]{2,1,0:T(8,128)S(1)}, f32[8,16,128]{2,1,0:T(8,128)S(1)}, u32[]{:S(2)}, u32[]{:S(2)}) collective-permute-start(f32[8,16,128]{2,1,0:T(8,128)S(1)} %get-tuple-element.41.own), channel_id=1, source_target_pairs={{0,4},{8,12},{16,20},{24,28},{4,0},{12,8},{20,16},{28,24},{1,5},{9... | collective-permute-start | bytes 196616 | tf_op jit(solution)/shard_map/ppermute | solution.py:531
  22.8 3.8 %collective-permute-done.6.beside_b = f32[8,16,128]{2,1,0:T(8,128)S(1)} collective-permute-done((f32[8,16,128]{2,1,0:T(8,128)S(1)}, f32[8,16,128]{2,1,0:T(8,128)S(1)}, u32[]{:S(2)}, u32[]{:S(2)}) %collective-permute-start.6) | collective-permute-done | bytes 65568 | tf_op jit(solution)/shard_map/ppermute | solution.py:531
  26.7 2.4 %collective-permute-start.8 = (f32[224,128]{1,0:T(8,128)S(1)}, f32[224,128]{1,0:T(8,128)S(1)}, u32[]{:S(2)}, u32[]{:S(2)}) collective-permute-start(f32[224,128]{1,0:T(8,128)S(1)} %get-tuple-element.42), channel_id=1, source_target_pairs={{1,2},{2,1},{5,6},{6,5},{9,10},{10,9},{13,14},{14,13},{17,18},{18,... | collective-permute-start | bytes 344072 | tf_op jit(solution)/shard_map/ppermute | solution.py:531
  29.1 0.1 collective-permute-start.9
  29.2 0.1 radius.1
  29.3 1.4 %third_step.1 = f32[152,16,128]{2,1,0:T(8,128)} custom-call(f32[190,32,128]{2,1,0:T(8,128)S(1)} %get-tuple-element.40.state, f32[48,32,128]{2,1,0:T(8,128)S(1)} %get-tuple-element.28.coef), custom_call_target="tpu_custom_call" | custom-call | tf_op jit(solution)/shard_map/third_step/pallas_call | solution.py:514
  30.7 2.7 %collective-permute-done.8.band_b = f32[224,128]{1,0:T(8,128)S(1)} collective-permute-done((f32[224,128]{1,0:T(8,128)S(1)}, f32[224,128]{1,0:T(8,128)S(1)}, u32[]{:S(2)}, u32[]{:S(2)}) %collective-permute-start.8) | collective-permute-done | bytes 114720 | tf_op jit(solution)/shard_map/ppermute | solution.py:531
  33.4 0.5 %collective-permute-done.9.band_a = f32[224,128]{1,0:T(8,128)S(1)} collective-permute-done((f32[224,128]{1,0:T(8,128)S(1)}, f32[224,128]{1,0:T(8,128)S(1)}, u32[]{:S(2)}, u32[]{:S(2)}) %collective-permute-start.9) | collective-permute-done | bytes 114720 | tf_op jit(solution)/shard_map/ppermute | solution.py:531
  33.9 1.9 %eight_sweeps.1 = f32[8,16,128]{2,1,0:T(8,128)} custom-call(f32[8,16,128]{2,1,0:T(8,128)S(1)} %get-tuple-element.41.own, f32[8,16,128]{2,1,0:T(8,128)S(1)} %collective-permute-done.6.beside_b, f32[8,16,128]{2,1,0:T(8,128)S(1)} %collective-permute-done.7.beside_a, f32[224,128]{1,0:T(8,128)S(1)} %collective-permute-done.8.band_b, ...), custom_call_target="tpu_custom_call" | custom-call | tf_op jit(solution)/shard_map/eight_sweeps/pallas_call | solution.py:514
  (5 shorter events, 0.1 us)
Async XLA Ops:
  2.4 8.5 %collective-permute-start = (f32[384,128]{1,0:T(8,128)S(1)}, f32[384,128]{1,0:T(8,128)S(1)}, u32[]{:S(2)}, u32[]{:S(2)}) collective-permute-start(f32[384,128]{1,0:T(8,128)S(1)} %get-tuple-element.26), channel_id=1, source_target_pairs={{1,2},{2,1},{5,6},{6,5},{9,10},{10,9},{13,14},{14,13},{17,18},{18,... | collective-permute-start | bytes 589832 | tf_op jit(solution)/shard_map/ppermute | solution.py:531
  5.9 6.4 %collective-permute-start.1 = (f32[384,128]{1,0:T(8,128)S(1)}, f32[384,128]{1,0:T(8,128)S(1)}, u32[]{:S(2)}, u32[]{:S(2)}) collective-permute-start(f32[384,128]{1,0:T(8,128)S(1)} %get-tuple-element.27), channel_id=1, source_target_pairs={{0,1},{2,3},{1,0},{3,2},{4,5},{6,7},{5,4},{7,6},{8,9},{10,11},{9,8... | collective-permute-start | bytes 589832 | tf_op jit(solution)/shard_map/ppermute | solution.py:531
  6.3 11.0 %collective-permute-start.2 = (f32[432,128]{1,0:T(8,128)S(1)}, f32[432,128]{1,0:T(8,128)S(1)}, u32[]{:S(2)}, u32[]{:S(2)}) collective-permute-start(f32[432,128]{1,0:T(8,128)S(1)} %get-tuple-element.31), channel_id=1, source_target_pairs={{4,8},{12,16},{20,24},{8,4},{16,12},{24,20},{5,9},{13,17},{21,25},... | collective-permute-start | bytes 663560 | tf_op jit(solution)/shard_map/ppermute | solution.py:531
  8.8 8.5 %collective-permute-start.3 = (f32[432,128]{1,0:T(8,128)S(1)}, f32[432,128]{1,0:T(8,128)S(1)}, u32[]{:S(2)}, u32[]{:S(2)}) collective-permute-start(f32[432,128]{1,0:T(8,128)S(1)} %get-tuple-element.32), channel_id=1, source_target_pairs={{0,4},{8,12},{16,20},{24,28},{4,0},{12,8},{20,16},{28,24},{1,5},{9... | collective-permute-start | bytes 663560 | tf_op jit(solution)/shard_map/ppermute | solution.py:531
  13.0 6.4 %collective-permute-start.4 = (f32[112,128]{1,0:T(8,128)S(1)}, f32[112,128]{1,0:T(8,128)S(1)}, u32[]{:S(2)}, u32[]{:S(2)}) collective-permute-start(f32[112,128]{1,0:T(8,128)S(1)} %get-tuple-element.33), channel_id=1, source_target_pairs={{4,8},{12,16},{20,24},{8,4},{16,12},{24,20},{5,9},{13,17},{21,25},... | collective-permute-start | bytes 172040 | tf_op jit(solution)/shard_map/ppermute | solution.py:531
  14.9 4.5 %collective-permute-start.5 = (f32[112,128]{1,0:T(8,128)S(1)}, f32[112,128]{1,0:T(8,128)S(1)}, u32[]{:S(2)}, u32[]{:S(2)}) collective-permute-start(f32[112,128]{1,0:T(8,128)S(1)} %get-tuple-element.34), channel_id=1, source_target_pairs={{0,4},{8,12},{16,20},{24,28},{4,0},{12,8},{20,16},{28,24},{1,5},{9... | collective-permute-start | bytes 172040 | tf_op jit(solution)/shard_map/ppermute | solution.py:531
  20.2 6.5 %collective-permute-start.6 = (f32[8,16,128]{2,1,0:T(8,128)S(1)}, f32[8,16,128]{2,1,0:T(8,128)S(1)}, u32[]{:S(2)}, u32[]{:S(2)}) collective-permute-start(f32[8,16,128]{2,1,0:T(8,128)S(1)} %get-tuple-element.41.own), channel_id=1, source_target_pairs={{4,8},{12,16},{20,24},{8,4},{16,12},{24,20},{5,9},{13,17},{21,25},... | collective-permute-start | bytes 196616 | tf_op jit(solution)/shard_map/ppermute | solution.py:531
  22.1 4.6 %collective-permute-start.7 = (f32[8,16,128]{2,1,0:T(8,128)S(1)}, f32[8,16,128]{2,1,0:T(8,128)S(1)}, u32[]{:S(2)}, u32[]{:S(2)}) collective-permute-start(f32[8,16,128]{2,1,0:T(8,128)S(1)} %get-tuple-element.41.own), channel_id=1, source_target_pairs={{0,4},{8,12},{16,20},{24,28},{4,0},{12,8},{20,16},{28,24},{1,5},{9... | collective-permute-start | bytes 196616 | tf_op jit(solution)/shard_map/ppermute | solution.py:531
  26.7 6.7 %collective-permute-start.8 = (f32[224,128]{1,0:T(8,128)S(1)}, f32[224,128]{1,0:T(8,128)S(1)}, u32[]{:S(2)}, u32[]{:S(2)}) collective-permute-start(f32[224,128]{1,0:T(8,128)S(1)} %get-tuple-element.42), channel_id=1, source_target_pairs={{1,2},{2,1},{5,6},{6,5},{9,10},{10,9},{13,14},{14,13},{17,18},{18,... | collective-permute-start | bytes 344072 | tf_op jit(solution)/shard_map/ppermute | solution.py:531
  29.1 4.9 %collective-permute-start.9 = (f32[224,128]{1,0:T(8,128)S(1)}, f32[224,128]{1,0:T(8,128)S(1)}, u32[]{:S(2)}, u32[]{:S(2)}) collective-permute-start(f32[224,128]{1,0:T(8,128)S(1)} %get-tuple-element.43), channel_id=1, source_target_pairs={{0,1},{2,3},{1,0},{3,2},{4,5},{6,7},{5,4},{7,6},{8,9},{10,11},{9,8... | collective-permute-start | bytes 344072 | tf_op jit(solution)/shard_map/ppermute | solution.py:531

commit v8 on v7

--- a/solution.py
+++ b/solution.py
@@ -39,7 +39,6 @@
 LEVEL = tuple(i for i in range(POPS) if VELOCITIES[i][0] == 0)
 PAD = 8
 FIRST = 5
-EDGES = 19
 
 
 def rim_entries():
@@ -256,19 +255,30 @@
             put(2, n, at, posts[i])
 
 
-EARLY = (0, 5, 10, 15)
+def early_pieces(y_size):
+    pieces, offset = [], 0
+    for count, margin in ((5, 0), (5, 1), (5, 2), (4, 0)):
+        pieces.append((offset, margin))
+        offset += count * (y_size - 2 * margin)
+    return pieces, offset
 
 
 def early_kernel(x_size, y_size, state, coef, span, early_b, early_a, near, far):
     rows = range(PAD, PAD + y_size, 8)
+    pieces, radii = early_pieces(y_size)
     for after, out in zip(toward_next("grp"), (early_a, early_b)):
 
         def put(kind, n, at, value, out=out):
-            out[pl.ds((EARLY[kind] + n) * y_size + at - PAD, 8), :] = value
+            offset, margin = pieces[kind]
+            begin = max(at, PAD + margin)
+            end = min(at + 8, PAD + y_size - margin)
+            place = offset + n * (y_size - 2 * margin) + begin - PAD - margin
+            out[pl.ds(place, end - begin), :] = value[begin - at : end - at]
 
         edge_steps(x_size, after, state, coef, near, far, rows, rows, rows, put)
-        for x in range(x_size):
-            out[pl.ds((EDGES + x) * y_size, y_size), :] = span[x]
+        for k in range(REACH - 1):
+            plane = jnp.where(after, x_size - 1 - k, k)
+            out[pl.ds(radii + k * y_size, y_size), :] = span[plane]
 
 
 def late_pieces(y_size):
@@ -351,8 +361,10 @@
                 if kind == 0:
                     ref, plane = state, pick(after, RIGHT[n], mirrored(RIGHT[n], 0)) * planes + halo
                 else:
-                    ref, plane = halos, side * 14 + EARLY[kind] - 5 + n
-                ref[plane, pl.ds(PAD, y_size), :] = early[pl.ds((EARLY[kind] + n) * y_size, y_size), :]
+                    ref, plane = halos, side * 14 + 5 * kind - 5 + n
+                offset, margin = early_pieces(y_size)[0][kind]
+                rows = y_size - 2 * margin
+                ref[plane, pl.ds(PAD + margin, rows), :] = early[pl.ds(offset + n * rows, rows), :]
                 for end in (0, 1):
                     begin, rows, offset = pieces[kind, end]
                     ref[plane, pl.ds(begin, rows), :] = late[pl.ds(offset + n * rows, rows), :]
@@ -408,14 +420,20 @@
     lax.fori_loop(0, x_size, plane, 0, unroll=True)
 
 
-def diamond(x_size, reach):
-    pieces, offset = [], 0
-    for slot in range(3):
+def diamond(x_size, reach, slots, base=0):
+    pieces, offset = [], base
+    for slot in slots:
         for k in range(x_size if slot == 0 else min(x_size, reach - 1)):
             rows = reach if slot == 0 else reach - 1 - k
             pieces.append((slot, k, rows, offset))
             offset += rows
-    return pieces, -(-offset // 8) * 8
+    return pieces, offset
+
+
+def bands_of(x_size, slots):
+    sens, offset = diamond(x_size, REACH, slots)
+    radii, offset = diamond(x_size, REACH - 1, slots, offset)
+    return sens, radii, -(-offset // 8) * 8
 
 
 def slot_plane(x_size, slot, k):
@@ -425,15 +443,24 @@
     return jnp.where(after, 2 * x_size + k, x_size - 1 - k), jnp.where(after, k, x_size - 1 - k)
 
 
-def band_kernel(x_size, y_size, own, beside_b, beside_a, span, span_b, span_a, band_b, band_a):
-    pieces, skip = diamond(x_size, REACH)
+def own_band_kernel(x_size, y_size, own, span, band_b, band_a):
+    sens, radii, _ = bands_of(x_size, (0,))
     for after, out in zip(toward_next("blk"), (band_a, band_b)):
-        for refs, reach, base in (((own, beside_a, beside_b), REACH, 0), ((span, span_a, span_b), REACH - 1, skip)):
-            for slot, k, rows, offset in diamond(x_size, reach)[0]:
-                _, plane = slot_plane(x_size, slot, k)
-                plane = plane + EDGES if slot > 0 and base > 0 else plane
-                value = refs[slot][plane, pl.ds(jnp.where(after, y_size - rows, 0), rows), :]
-                out[pl.ds(base + offset, rows), :] = value.astype(jnp.float32)
+        for ref, pieces in ((own, sens), (span, radii)):
+            for _, k, rows, offset in pieces:
+                out[pl.ds(offset, rows), :] = ref[k, pl.ds(jnp.where(after, y_size - rows, 0), rows), :]
+
+
+def band_kernel(x_size, y_size, beside_b, beside_a, early_b, early_a, band_b, band_a):
+    sens, radii, _ = bands_of(x_size, (1, 2))
+    for after, out in zip(toward_next("blk"), (band_a, band_b)):
+        for slot, k, rows, offset in sens:
+            _, plane = slot_plane(x_size, slot, k)
+            start = jnp.where(after, y_size - rows, 0)
+            out[pl.ds(offset, rows), :] = (beside_a, beside_b)[slot - 1][plane, pl.ds(start, rows), :]
+        for slot, k, rows, offset in radii:
+            start = early_pieces(y_size)[1] + k * y_size + jnp.where(after, y_size - rows, 0)
+            out[pl.ds(offset, rows), :] = (early_a, early_b)[slot - 1][pl.ds(start, rows), :]
 
 
 def shares(span, inside):
@@ -454,16 +481,14 @@
     for slot, ref in enumerate((span, span_a, span_b)):
         inside = slot_inside(slot)
 
-        def plane(x, _, slot=slot, ref=ref, inside=inside):
-            place, k = slot_plane(x_size, slot, x)
-            inverse[place], beta[place] = shares(ref[k if slot == 0 else EDGES + k].astype(jnp.float32), inside)
-            return 0
-
-        lax.fori_loop(0, x_size, plane, 0, unroll=4)
+        for x in range(x_size if slot == 0 else min(x_size, REACH - 1)):
+            place, _ = slot_plane(x_size, slot, x)
+            classes = ref[x] if slot == 0 else ref[pl.ds(early_pieces(y_size)[1] + x * y_size, y_size), :]
+            inverse[place], beta[place] = shares(classes, inside)
 
 
 def filter_kernel(
-    x_size, y_size, own, beside_b, beside_a, band_b, band_a, inverse, own_beta, filtered, first, second, given, beta
+    x_size, y_size, own, beside_b, beside_a, own_b, own_a, band_b, band_a, inverse, own_beta, filtered, first, second, given, beta
 ):
     rows = y_size + 2 * REACH
     for x in range(x_size):
@@ -473,38 +498,40 @@
             first[place, pl.ds(PAD + REACH, y_size), :] = s
             given[place, pl.ds(REACH, y_size), :] = s * inverse[place]
             beta[place, pl.ds(REACH, y_size), :] = own_beta[place]
-    pieces, skip = diamond(x_size, REACH)
-    radii = {(slot, k): (rows, skip + offset) for slot, k, rows, offset in diamond(x_size, REACH - 1)[0]}
     me, size = lax.axis_index("blk"), lax.axis_size("blk")
-    for after, ref in zip(toward_next("blk"), (band_a, band_b)):
+    for after, refs in zip(toward_next("blk"), ((own_a, band_a), (own_b, band_b))):
         there = jnp.where(after, me < size - 1, me > 0)
-        for slot, k, count, offset in pieces:
-            place, _ = slot_plane(x_size, slot, k)
-            at = jnp.where(after, REACH + y_size, REACH - count)
-            s = ref[pl.ds(offset, count), :]
-            first[place, pl.ds(PAD + at, count), :] = s
-            if (slot, k) in radii:
-                count, offset = radii[slot, k]
+        for ref, slots in zip(refs, ((0,), (1, 2))):
+            pieces, radii, _ = bands_of(x_size, slots)
+            radii = {(slot, k): (count, offset) for slot, k, count, offset in radii}
+            for slot, k, count, offset in pieces:
+                place, _ = slot_plane(x_size, slot, k)
                 at = jnp.where(after, REACH + y_size, REACH - count)
-                inside = jnp.logical_and(there, slot_inside(slot))
-                share, beta[place, pl.ds(at, count), :] = shares(ref[pl.ds(offset, count), :], inside)
-                given[place, pl.ds(at, count), :] = first[place, pl.ds(PAD + at, count), :] * share
+                first[place, pl.ds(PAD + at, count), :] = ref[pl.ds(offset, count), :]
+                if (slot, k) in radii:
+                    count, offset = radii[slot, k]
+                    at = jnp.where(after, REACH + y_size, REACH - count)
+                    inside = jnp.logical_and(there, slot_inside(slot))
+                    share, beta[place, pl.ds(at, count), :] = shares(ref[pl.ds(offset, count), :], inside)
+                    given[place, pl.ds(at, count), :] = first[place, pl.ds(PAD + at, count), :] * share
     source, target = first, second
     for number in range(1, SWEEPS + 1):
         final = number == SWEEPS
         margin = SWEEPS - number
 
-        for j in range(1, 1 + y_size // 8) if final else range(rows // 8):
-            at = PAD + 8 * j
+        groups = -(-(y_size + 2 * margin) // 8)
+        start = min(REACH - margin, rows - 8 * groups)
+        for row in range(start, start + 8 * groups, 8):
+            at = PAD + row
             begin, end = x_size - margin, 2 * x_size + margin
             column = {x: source[x, pl.ds(at, 8), :] for x in range(begin - 1, end + 1)}
             for x in range(begin, end):
                 beside = column[x + 1] + column[x - 1]
                 beside = beside + source[x, pl.ds(at + 1, 8), :] + source[x, pl.ds(at - 1, 8), :]
                 beside = beside + lane_pull(column[x], 1) + lane_pull(column[x], -1)
-                value = given[x, pl.ds(8 * j, 8), :] + beta[x, pl.ds(8 * j, 8), :] * beside
+                value = given[x, pl.ds(row, 8), :] + beta[x, pl.ds(row, 8), :] * beside
                 if final:
-                    filtered[x - x_size, pl.ds(8 * j - REACH, 8), :] = value
+                    filtered[x - x_size, pl.ds(row - REACH, 8), :] = value
                 else:
                     target[x, pl.ds(at, 8), :] = value
         source, target = target, source
@@ -556,7 +583,7 @@
         pltpu.HBM,
     )
     rims = swapped("blk", *rims)
-    early = ((EDGES + x_size) * y_size, lanes)
+    early = (early_pieces(y_size)[1] + (REACH - 1) * y_size, lanes)
     near_far = [(len(LEVEL), pitch, lanes), (len(RIGHT), pitch, lanes)]
     earlies = call(
         functools.partial(early_kernel, *sizes),
@@ -592,25 +619,27 @@
         "steps_at_edges",
         in_place=((6, 0), (7, 1), (8, 2), (9, 3), (10, 4)),
     )
-    spans = [e.reshape(EDGES + x_size, y_size, lanes) for e in earlies]
+    spans = earlies
     beside = swapped("grp", sens, sens)
+    band = (bands_of(x_size, (0,))[2], lanes)
+    own_bands = call(functools.partial(own_band_kernel, *sizes), [band, band], [], (sens, span), "own_bands")
+    own_bands = swapped("blk", *own_bands)
+    band = (bands_of(x_size, (1, 2))[2], lanes)
+    bands = call(functools.partial(band_kernel, *sizes), [band, band], [], (*beside, *spans), "bands")
+    bands = swapped("blk", *bands)
+    own_bands, state_2 = lax.optimization_barrier((own_bands, state_2))
     (adjoint,) = call(
         functools.partial(adjoint_kernel, *sizes), [(POPS * x_size, y_size, lanes)], [], (state_2, coefs), "third_step"
     )
     inverse, beta = call(
         functools.partial(radius_kernel, *sizes), [(3 * x_size, y_size, lanes)] * 2, [], (span, *spans), "radius"
     )
-    band = (diamond(x_size, REACH)[1] + diamond(x_size, REACH - 1)[1], lanes)
-    bands = call(
-        functools.partial(band_kernel, *sizes), [band, band], [], (sens, *beside, span, *spans), "bands"
-    )
-    bands = swapped("blk", *bands)
     wide, rows = 3 * x_size, y_size + 2 * REACH
     (filtered,) = call(
         functools.partial(filter_kernel, *sizes),
         [(x_size, y_size, lanes)],
         [(wide, rows + 2 * PAD, lanes)] * 2 + [(wide, rows, lanes)] * 2,
-        (sens, *beside, *bands, inverse, beta),
+        (sens, *beside, *own_bands, *bands, inverse, beta),
         "eight_sweeps",
     )
     return adjoint.reshape(dual_populace.shape), filtered

time: 36.1 us -> 36.3 us (level)
  the two profiles are of different devices: /device:TPU:12 before, /device:TPU:0 now
where the time goes in v8:
time: 36.3 us; the launch traced here: 36 us
  starting transfers between devices  26.1 us (72%)
  Pallas kernels  7.66 us (21%)
  waiting for transfers between devices  1.52 us (4%)
  between operations  0.78 us (2%)
    ppermute x12, starting transfers between devices, swapped(): lax.ppermute(message, axis, pairs + [(j, i) for i, j in pairs])  26.1 us
    pallas_call x10, Pallas kernels, call(): pl.pallas_call(kernel, out_shape=[jax.ShapeDtypeStruct(shape, jnp.float32...  7.66 us
    ppermute x12, waiting for transfers between devices, swapped(): lax.ppermute(message, axis, pairs + [(j, i) for i, j in pairs])  1.52 us
  transfers between devices with their start and end apart: 12, of which 3 were waited for; matrix products, arithmetic and copies ran while one was open for 0% of the time, Pallas kernels for 9%

profile of v8, /device:TPU:0, one launch (start us, length us, event | category | flops | bytes accessed | tf_op | source)
XLA Modules:
  0.0 36.0 jit_solution(16941653599293827262)
XLA Ops:
  0.6 1.8 %rim_rows.1 = (f32[384,128]{1,0:T(8,128)S(1)}, f32[384,128]{1,0:T(8,128)S(1)}, f32[190,32,128]{2,1,0:T(8,128)S(1)}, f32[48,32,128]{2,1,0:T(8,128)S(1)}, f32[8,16...) custom-call(f32[152,16,128]{2,1,0:T(8,128)} %bitcast.4, f32[24,16,128]{2,1,0:T(8,128)} %bitcast.5, f32[8,16,128]{2,1,0:T(8,128)} %refs_2_.1, ...), custom_call_target="tpu_custom_call" | custom-call | tf_op jit(solution)/shard_map/rim_rows/pallas_call | solution.py:541
  2.4 0.7 %collective-permute-start = (f32[384,128]{1,0:T(8,128)S(1)}, f32[384,128]{1,0:T(8,128)S(1)}, u32[]{:S(2)}, u32[]{:S(2)}) collective-permute-start(f32[384,128]{1,0:T(8,128)S(1)} %get-tuple-element.31), channel_id=1, source_target_pairs={{1,2},{2,1},{5,6},{6,5},{9,10},{10,9},{13,14},{14,13},{17,18},{18,... | collective-permute-start | bytes 589832 | tf_op jit(solution)/shard_map/ppermute | solution.py:558
  3.1 5.9 %collective-permute-start.1 = (f32[384,128]{1,0:T(8,128)S(1)}, f32[384,128]{1,0:T(8,128)S(1)}, u32[]{:S(2)}, u32[]{:S(2)}) collective-permute-start(f32[384,128]{1,0:T(8,128)S(1)} %get-tuple-element.32), channel_id=1, source_target_pairs={{0,1},{2,3},{1,0},{3,2},{4,5},{6,7},{5,4},{7,6},{8,9},{10,11},{9,8... | collective-permute-start | bytes 589832 | tf_op jit(solution)/shard_map/ppermute | solution.py:558
  9.0 0.3 edges_early.1
  9.3 0.7 %collective-permute-start.2 = (f32[386,128]{1,0:T(8,128)S(1)}, f32[386,128]{1,0:T(8,128)S(1)}, u32[]{:S(2)}, u32[]{:S(2)}) collective-permute-start(f32[386,128]{1,0:T(8,128)S(1)} %get-tuple-element.36), channel_id=1, source_target_pairs={{4,8},{12,16},{20,24},{8,4},{16,12},{24,20},{5,9},{13,17},{21,25},... | collective-permute-start | bytes 592904 | tf_op jit(solution)/shard_map/ppermute | solution.py:558
  10.0 2.9 %collective-permute-start.3 = (f32[386,128]{1,0:T(8,128)S(1)}, f32[386,128]{1,0:T(8,128)S(1)}, u32[]{:S(2)}, u32[]{:S(2)}) collective-permute-start(f32[386,128]{1,0:T(8,128)S(1)} %get-tuple-element.37), channel_id=1, source_target_pairs={{0,4},{8,12},{16,20},{24,28},{4,0},{12,8},{20,16},{28,24},{1,5},{9... | collective-permute-start | bytes 592904 | tf_op jit(solution)/shard_map/ppermute | solution.py:558
  12.9 0.0 collective-permute-done.rim_b
  12.9 0.8 %collective-permute-done.1.rim_a = f32[384,128]{1,0:T(8,128)S(1)} collective-permute-done((f32[384,128]{1,0:T(8,128)S(1)}, f32[384,128]{1,0:T(8,128)S(1)}, u32[]{:S(2)}, u32[]{:S(2)}) %collective-permute-start.1) | collective-permute-done | bytes 196640 | tf_op jit(solution)/shard_map/ppermute | solution.py:558
  13.6 0.6 %edges_late.1 = (f32[112,128]{1,0:T(8,128)S(1)}, f32[112,128]{1,0:T(8,128)S(1)}, f32[190,32,128]{2,1,0:T(8,128)S(1)}, f32[48,32,128]{2,1,0:T(8,128)S(1)}) custom-call(f32[190,32,128]{2,1,0:T(8,128)S(1)} %get-tuple-element.29._state.state, f32[48,32,128]{2,1,0:T(8,128)S(1)} %get-tuple-element.30._coef.coef, ...), custom_call_target="tpu_custom_call", output_to_operand_aliasing={{2}: (0, {}), {3}: (1, {})} | custom-call | tf_op jit(solution)/shard_map/edges_late/pallas_call | solution.py:541
  14.3 0.7 %collective-permute-start.4 = (f32[112,128]{1,0:T(8,128)S(1)}, f32[112,128]{1,0:T(8,128)S(1)}, u32[]{:S(2)}, u32[]{:S(2)}) collective-permute-start(f32[112,128]{1,0:T(8,128)S(1)} %get-tuple-element.38), channel_id=1, source_target_pairs={{4,8},{12,16},{20,24},{8,4},{16,12},{24,20},{5,9},{13,17},{21,25},... | collective-permute-start | bytes 172040 | tf_op jit(solution)/shard_map/ppermute | solution.py:558
  14.9 2.9 %collective-permute-start.5 = (f32[112,128]{1,0:T(8,128)S(1)}, f32[112,128]{1,0:T(8,128)S(1)}, u32[]{:S(2)}, u32[]{:S(2)}) collective-permute-start(f32[112,128]{1,0:T(8,128)S(1)} %get-tuple-element.39), channel_id=1, source_target_pairs={{0,4},{8,12},{16,20},{24,28},{4,0},{12,8},{20,16},{28,24},{1,5},{9... | collective-permute-start | bytes 172040 | tf_op jit(solution)/shard_map/ppermute | solution.py:558
  17.8 0.7 %steps_inside.1 = (f32[190,32,128]{2,1,0:T(8,128)S(1)}, f32[190,32,128]{2,1,0:T(8,128)S(1)}, f32[16,32,128]{2,1,0:T(8,128)S(1)}, f32[8,16,128]{2,1,0:T(8,128)S(1)}) custom-call(f32[190,32,128]{2,1,0:T(8,128)S(1)} %get-tuple-element.40.state._state, f32[48,32,128]{2,1,0:T(8,128)S(1)} %get-tuple-element.33.coef, f32[8,16,128]{2,1,0:T(8,128)S(1)} %get-tuple-element.34.heat), custom_call_target="tpu_custom_call" | custom-call | tf_op jit(solution)/shard_map/steps_inside/pallas_call | solution.py:541
  18.6 0.1 collective-permute-done.5.late_a
  18.7 0.8 %steps_at_edges.1 = (f32[190,32,128]{2,1,0:T(8,128)S(1)}, f32[190,32,128]{2,1,0:T(8,128)S(1)}, f32[190,32,128]{2,1,0:T(8,128)S(1)}, f32[16,32,128]{2,1,0:T(8,128)S(1)}, f32[8,16,128]{2,1,0:T(8,128)S(1)}) custom-call(f32[48,32,128]{2,1,0:T(8,128)S(1)} %get-tuple-element.33.coef, ...), custom_call_target="tpu_custom_call", output_to_operand_aliasing={{0}: (6, {}), {1}: (7, {}), {2}: (8, {}), {3}: (9, {}), {4}... | custom-call | tf_op jit(solution)/shard_map/steps_at_edges/pallas_call | solution.py:541
  19.6 0.7 %collective-permute-start.8 = (f32[8,16,128]{2,1,0:T(8,128)S(1)}, f32[8,16,128]{2,1,0:T(8,128)S(1)}, u32[]{:S(2)}, u32[]{:S(2)}) collective-permute-start(f32[8,16,128]{2,1,0:T(8,128)S(1)} %get-tuple-element.45.own), channel_id=1, source_target_pairs={{4,8},{12,16},{20,24},{8,4},{16,12},{24,20},{5,9},{13,17},{21,25},... | collective-permute-start | bytes 196616 | tf_op jit(solution)/shard_map/ppermute | solution.py:558
  20.2 3.9 %collective-permute-start.9 = (f32[8,16,128]{2,1,0:T(8,128)S(1)}, f32[8,16,128]{2,1,0:T(8,128)S(1)}, u32[]{:S(2)}, u32[]{:S(2)}) collective-permute-start(f32[8,16,128]{2,1,0:T(8,128)S(1)} %get-tuple-element.45.own), channel_id=1, source_target_pairs={{0,4},{8,12},{16,20},{24,28},{4,0},{12,8},{20,16},{28,24},{1,5},{9... | collective-permute-start | bytes 196616 | tf_op jit(solution)/shard_map/ppermute | solution.py:558
  24.2 0.7 %collective-permute-start.6 = (f32[120,128]{1,0:T(8,128)S(1)}, f32[120,128]{1,0:T(8,128)S(1)}, u32[]{:S(2)}, u32[]{:S(2)}) collective-permute-start(f32[120,128]{1,0:T(8,128)S(1)} %get-tuple-element.46), channel_id=1, source_target_pairs={{1,2},{2,1},{5,6},{6,5},{9,10},{10,9},{13,14},{14,13},{17,18},{18,... | collective-permute-start | bytes 184328 | tf_op jit(solution)/shard_map/ppermute | solution.py:558
  24.9 3.5 %collective-permute-start.7 = (f32[120,128]{1,0:T(8,128)S(1)}, f32[120,128]{1,0:T(8,128)S(1)}, u32[]{:S(2)}, u32[]{:S(2)}) collective-permute-start(f32[120,128]{1,0:T(8,128)S(1)} %get-tuple-element.47), channel_id=1, source_target_pairs={{0,1},{2,3},{1,0},{3,2},{4,5},{6,7},{5,4},{7,6},{8,9},{10,11},{9,8... | collective-permute-start | bytes 184328 | tf_op jit(solution)/shard_map/ppermute | solution.py:558
  28.4 0.7 %collective-permute-start.10 = (f32[104,128]{1,0:T(8,128)S(1)}, f32[104,128]{1,0:T(8,128)S(1)}, u32[]{:S(2)}, u32[]{:S(2)}) collective-permute-start(f32[104,128]{1,0:T(8,128)S(1)} %get-tuple-element.52), channel_id=1, source_target_pairs={{1,2},{2,1},{5,6},{6,5},{9,10},{10,9},{13,14},{14,13},{17,18},{18,... | collective-permute-start | bytes 159752 | tf_op jit(solution)/shard_map/ppermute | solution.py:558
  29.1 2.9 %collective-permute-start.11 = (f32[104,128]{1,0:T(8,128)S(1)}, f32[104,128]{1,0:T(8,128)S(1)}, u32[]{:S(2)}, u32[]{:S(2)}) collective-permute-start(f32[104,128]{1,0:T(8,128)S(1)} %get-tuple-element.53), channel_id=1, source_target_pairs={{0,1},{2,3},{1,0},{3,2},{4,5},{6,7},{5,4},{7,6},{8,9},{10,11},{9,8... | collective-permute-start | bytes 159752 | tf_op jit(solution)/shard_map/ppermute | solution.py:558
  32.0 0.1 radius.1
  32.1 1.4 %third_step.1 = f32[152,16,128]{2,1,0:T(8,128)} custom-call(f32[190,32,128]{2,1,0:T(8,128)S(1)} %get-tuple-element.49.state, f32[48,32,128]{2,1,0:T(8,128)S(1)} %get-tuple-element.33.coef), custom_call_target="tpu_custom_call" | custom-call | tf_op jit(solution)/shard_map/third_step/pallas_call | solution.py:541
  33.5 0.6 %collective-permute-done.11.band_a = f32[104,128]{1,0:T(8,128)S(1)} collective-permute-done((f32[104,128]{1,0:T(8,128)S(1)}, f32[104,128]{1,0:T(8,128)S(1)}, u32[]{:S(2)}, u32[]{:S(2)}) %collective-permute-start.11) | collective-permute-done | bytes 53280 | tf_op jit(solution)/shard_map/ppermute | solution.py:558
  34.1 1.9 %eight_sweeps.1 = f32[8,16,128]{2,1,0:T(8,128)} custom-call(f32[8,16,128]{2,1,0:T(8,128)S(1)} %get-tuple-element.45.own, f32[8,16,128]{2,1,0:T(8,128)S(1)} %collective-permute-done.8.beside_b, f32[8,16,128]{2,1,0:T(8,128)S(1)} %collective-permute-done.9.beside_a, f32[120,128]{1,0:T(8,128)S(1)} %collective-permute-done.6.own_b, ...), custom_call_target="tpu_custom_call" | custom-call | tf_op jit(solution)/shard_map/eight_sweeps/pallas_call | solution.py:541
  (10 shorter events, 0.1 us)
Async XLA Ops:
  2.4 10.4 %collective-permute-start = (f32[384,128]{1,0:T(8,128)S(1)}, f32[384,128]{1,0:T(8,128)S(1)}, u32[]{:S(2)}, u32[]{:S(2)}) collective-permute-start(f32[384,128]{1,0:T(8,128)S(1)} %get-tuple-element.31), channel_id=1, source_target_pairs={{1,2},{2,1},{5,6},{6,5},{9,10},{10,9},{13,14},{14,13},{17,18},{18,... | collective-permute-start | bytes 589832 | tf_op jit(solution)/shard_map/ppermute | solution.py:558
  3.1 10.5 %collective-permute-start.1 = (f32[384,128]{1,0:T(8,128)S(1)}, f32[384,128]{1,0:T(8,128)S(1)}, u32[]{:S(2)}, u32[]{:S(2)}) collective-permute-start(f32[384,128]{1,0:T(8,128)S(1)} %get-tuple-element.32), channel_id=1, source_target_pairs={{0,1},{2,3},{1,0},{3,2},{4,5},{6,7},{5,4},{7,6},{8,9},{10,11},{9,8... | collective-permute-start | bytes 589832 | tf_op jit(solution)/shard_map/ppermute | solution.py:558
  9.3 9.3 %collective-permute-start.2 = (f32[386,128]{1,0:T(8,128)S(1)}, f32[386,128]{1,0:T(8,128)S(1)}, u32[]{:S(2)}, u32[]{:S(2)}) collective-permute-start(f32[386,128]{1,0:T(8,128)S(1)} %get-tuple-element.36), channel_id=1, source_target_pairs={{4,8},{12,16},{20,24},{8,4},{16,12},{24,20},{5,9},{13,17},{21,25},... | collective-permute-start | bytes 592904 | tf_op jit(solution)/shard_map/ppermute | solution.py:558
  10.0 8.7 %collective-permute-start.3 = (f32[386,128]{1,0:T(8,128)S(1)}, f32[386,128]{1,0:T(8,128)S(1)}, u32[]{:S(2)}, u32[]{:S(2)}) collective-permute-start(f32[386,128]{1,0:T(8,128)S(1)} %get-tuple-element.37), channel_id=1, source_target_pairs={{0,4},{8,12},{16,20},{24,28},{4,0},{12,8},{20,16},{28,24},{1,5},{9... | collective-permute-start | bytes 592904 | tf_op jit(solution)/shard_map/ppermute | solution.py:558
  14.3 4.4 %collective-permute-start.4 = (f32[112,128]{1,0:T(8,128)S(1)}, f32[112,128]{1,0:T(8,128)S(1)}, u32[]{:S(2)}, u32[]{:S(2)}) collective-permute-start(f32[112,128]{1,0:T(8,128)S(1)} %get-tuple-element.38), channel_id=1, source_target_pairs={{4,8},{12,16},{20,24},{8,4},{16,12},{24,20},{5,9},{13,17},{21,25},... | collective-permute-start | bytes 172040 | tf_op jit(solution)/shard_map/ppermute | solution.py:558
  14.9 3.8 %collective-permute-start.5 = (f32[112,128]{1,0:T(8,128)S(1)}, f32[112,128]{1,0:T(8,128)S(1)}, u32[]{:S(2)}, u32[]{:S(2)}) collective-permute-start(f32[112,128]{1,0:T(8,128)S(1)} %get-tuple-element.39), channel_id=1, source_target_pairs={{0,4},{8,12},{16,20},{24,28},{4,0},{12,8},{20,16},{28,24},{1,5},{9... | collective-permute-start | bytes 172040 | tf_op jit(solution)/shard_map/ppermute | solution.py:558
  19.6 8.8 %collective-permute-start.8 = (f32[8,16,128]{2,1,0:T(8,128)S(1)}, f32[8,16,128]{2,1,0:T(8,128)S(1)}, u32[]{:S(2)}, u32[]{:S(2)}) collective-permute-start(f32[8,16,128]{2,1,0:T(8,128)S(1)} %get-tuple-element.45.own), channel_id=1, source_target_pairs={{4,8},{12,16},{20,24},{8,4},{16,12},{24,20},{5,9},{13,17},{21,25},... | collective-permute-start | bytes 196616 | tf_op jit(solution)/shard_map/ppermute | solution.py:558
  20.2 8.1 %collective-permute-start.9 = (f32[8,16,128]{2,1,0:T(8,128)S(1)}, f32[8,16,128]{2,1,0:T(8,128)S(1)}, u32[]{:S(2)}, u32[]{:S(2)}) collective-permute-start(f32[8,16,128]{2,1,0:T(8,128)S(1)} %get-tuple-element.45.own), channel_id=1, source_target_pairs={{0,4},{8,12},{16,20},{24,28},{4,0},{12,8},{20,16},{28,24},{1,5},{9... | collective-permute-start | bytes 196616 | tf_op jit(solution)/shard_map/ppermute | solution.py:558
  24.2 7.9 %collective-permute-start.6 = (f32[120,128]{1,0:T(8,128)S(1)}, f32[120,128]{1,0:T(8,128)S(1)}, u32[]{:S(2)}, u32[]{:S(2)}) collective-permute-start(f32[120,128]{1,0:T(8,128)S(1)} %get-tuple-element.46), channel_id=1, source_target_pairs={{1,2},{2,1},{5,6},{6,5},{9,10},{10,9},{13,14},{14,13},{17,18},{18,... | collective-permute-start | bytes 184328 | tf_op jit(solution)/shard_map/ppermute | solution.py:558
  24.9 7.2 %collective-permute-start.7 = (f32[120,128]{1,0:T(8,128)S(1)}, f32[120,128]{1,0:T(8,128)S(1)}, u32[]{:S(2)}, u32[]{:S(2)}) collective-permute-start(f32[120,128]{1,0:T(8,128)S(1)} %get-tuple-element.47), channel_id=1, source_target_pairs={{0,1},{2,3},{1,0},{3,2},{4,5},{6,7},{5,4},{7,6},{8,9},{10,11},{9,8... | collective-permute-start | bytes 184328 | tf_op jit(solution)/shard_map/ppermute | solution.py:558
  28.4 5.1 %collective-permute-start.10 = (f32[104,128]{1,0:T(8,128)S(1)}, f32[104,128]{1,0:T(8,128)S(1)}, u32[]{:S(2)}, u32[]{:S(2)}) collective-permute-start(f32[104,128]{1,0:T(8,128)S(1)} %get-tuple-element.52), channel_id=1, source_target_pairs={{1,2},{2,1},{5,6},{6,5},{9,10},{10,9},{13,14},{14,13},{17,18},{18,... | collective-permute-start | bytes 159752 | tf_op jit(solution)/shard_map/ppermute | solution.py:558
  29.1 5.1 %collective-permute-start.11 = (f32[104,128]{1,0:T(8,128)S(1)}, f32[104,128]{1,0:T(8,128)S(1)}, u32[]{:S(2)}, u32[]{:S(2)}) collective-permute-start(f32[104,128]{1,0:T(8,128)S(1)} %get-tuple-element.53), channel_id=1, source_target_pairs={{0,1},{2,3},{1,0},{3,2},{4,5},{6,7},{5,4},{7,6},{8,9},{10,11},{9,8... | collective-permute-start | bytes 159752 | tf_op jit(solution)/shard_map/ppermute | solution.py:558

commit v9 on v7

--- a/solution.py
+++ b/solution.py
@@ -39,7 +39,6 @@
 LEVEL = tuple(i for i in range(POPS) if VELOCITIES[i][0] == 0)
 PAD = 8
 FIRST = 5
-EDGES = 19
 
 
 def rim_entries():
@@ -256,19 +255,30 @@
             put(2, n, at, posts[i])
 
 
-EARLY = (0, 5, 10, 15)
+def early_pieces(y_size):
+    pieces, offset = [], 0
+    for count, margin in ((5, 0), (5, 1), (5, 2), (4, 0)):
+        pieces.append((offset, margin))
+        offset += count * (y_size - 2 * margin)
+    return pieces, offset
 
 
 def early_kernel(x_size, y_size, state, coef, span, early_b, early_a, near, far):
     rows = range(PAD, PAD + y_size, 8)
+    pieces, radii = early_pieces(y_size)
     for after, out in zip(toward_next("grp"), (early_a, early_b)):
 
         def put(kind, n, at, value, out=out):
-            out[pl.ds((EARLY[kind] + n) * y_size + at - PAD, 8), :] = value
+            offset, margin = pieces[kind]
+            begin = max(at, PAD + margin)
+            end = min(at + 8, PAD + y_size - margin)
+            place = offset + n * (y_size - 2 * margin) + begin - PAD - margin
+            out[pl.ds(place, end - begin), :] = value[begin - at : end - at]
 
         edge_steps(x_size, after, state, coef, near, far, rows, rows, rows, put)
-        for x in range(x_size):
-            out[pl.ds((EDGES + x) * y_size, y_size), :] = span[x]
+        for k in range(REACH - 1):
+            plane = jnp.where(after, x_size - 1 - k, k)
+            out[pl.ds(radii + k * y_size, y_size), :] = span[plane]
 
 
 def late_pieces(y_size):
@@ -351,8 +361,10 @@
                 if kind == 0:
                     ref, plane = state, pick(after, RIGHT[n], mirrored(RIGHT[n], 0)) * planes + halo
                 else:
-                    ref, plane = halos, side * 14 + EARLY[kind] - 5 + n
-                ref[plane, pl.ds(PAD, y_size), :] = early[pl.ds((EARLY[kind] + n) * y_size, y_size), :]
+                    ref, plane = halos, side * 14 + 5 * kind - 5 + n
+                offset, margin = early_pieces(y_size)[0][kind]
+                rows = y_size - 2 * margin
+                ref[plane, pl.ds(PAD + margin, rows), :] = early[pl.ds(offset + n * rows, rows), :]
                 for end in (0, 1):
                     begin, rows, offset = pieces[kind, end]
                     ref[plane, pl.ds(begin, rows), :] = late[pl.ds(offset + n * rows, rows), :]
@@ -425,15 +437,18 @@
     return jnp.where(after, 2 * x_size + k, x_size - 1 - k), jnp.where(after, k, x_size - 1 - k)
 
 
-def band_kernel(x_size, y_size, own, beside_b, beside_a, span, span_b, span_a, band_b, band_a):
+def band_kernel(x_size, y_size, own, beside_a, beside_b, span, span_b, span_a, band_b, band_a):
     pieces, skip = diamond(x_size, REACH)
     for after, out in zip(toward_next("blk"), (band_a, band_b)):
         for refs, reach, base in (((own, beside_a, beside_b), REACH, 0), ((span, span_a, span_b), REACH - 1, skip)):
             for slot, k, rows, offset in diamond(x_size, reach)[0]:
                 _, plane = slot_plane(x_size, slot, k)
-                plane = plane + EDGES if slot > 0 and base > 0 else plane
-                value = refs[slot][plane, pl.ds(jnp.where(after, y_size - rows, 0), rows), :]
-                out[pl.ds(base + offset, rows), :] = value.astype(jnp.float32)
+                start = jnp.where(after, y_size - rows, 0)
+                if slot > 0 and base > 0:
+                    value = refs[slot][pl.ds(early_pieces(y_size)[1] + k * y_size + start, rows), :]
+                else:
+                    value = refs[slot][plane, pl.ds(start, rows), :]
+                out[pl.ds(base + offset, rows), :] = value
 
 
 def shares(span, inside):
@@ -450,29 +465,51 @@
     return jnp.where(after, me < size - 1, me > 0)
 
 
-def radius_kernel(x_size, y_size, span, span_b, span_a, inverse, beta):
-    for slot, ref in enumerate((span, span_a, span_b)):
+def sweep(x_size, number, row, source, given, beta, put):
+    margin = SWEEPS - number
+    begin, end = x_size - margin, 2 * x_size + margin
+    column = {x: source(x, row) for x in range(begin - 1, end + 1)}
+    for x in range(begin, end):
+        beside = column[x + 1] + column[x - 1]
+        beside = beside + source(x, row + 1) + source(x, row - 1)
+        beside = beside + lane_pull(column[x], 1) + lane_pull(column[x], -1)
+        place = pl.ds(REACH + row, 8)
+        put(x, row, given[x, place, :] + beta[x, place, :] * beside)
+
+
+def level_access(x_size, levels, number):
+    def read(x, row):
+        return levels[number * 3 * x_size + x, pl.ds(PAD + REACH + row, 8), :]
+
+    def write(x, row, value):
+        levels[number * 3 * x_size + x, pl.ds(PAD + REACH + row, 8), :] = value
+
+    return read, write
+
+
+def inner_sweeps_kernel(
+    x_size, y_size, beside_b, beside_a, own, span, span_b, span_a, levels, given, beta
+):
+    for slot, (classes, sens) in enumerate(((span, own), (span_a, beside_a), (span_b, beside_b))):
         inside = slot_inside(slot)
-
-        def plane(x, _, slot=slot, ref=ref, inside=inside):
-            place, k = slot_plane(x_size, slot, x)
-            inverse[place], beta[place] = shares(ref[k if slot == 0 else EDGES + k].astype(jnp.float32), inside)
-            return 0
-
-        lax.fori_loop(0, x_size, plane, 0, unroll=4)
-
-
-def filter_kernel(
-    x_size, y_size, own, beside_b, beside_a, band_b, band_a, inverse, own_beta, filtered, first, second, given, beta
+        for k in range(x_size):
+            place, plane = slot_plane(x_size, slot, k)
+            s = sens[plane]
+            levels[place, pl.ds(PAD + REACH, y_size), :] = s
+            if slot == 0 or k < REACH - 1:
+                c = classes[k] if slot == 0 else classes[pl.ds(early_pieces(y_size)[1] + k * y_size, y_size), :]
+                share, beta[place, pl.ds(REACH, y_size), :] = shares(c, inside)
+                given[place, pl.ds(REACH, y_size), :] = s * share
+    for number in range(1, SWEEPS):
+        source, _ = level_access(x_size, levels, number - 1)
+        _, put = level_access(x_size, levels, number)
+        for row in range(number, y_size - number, 8):
+            sweep(x_size, number, row, source, given, beta, put)
+
+
+def outer_sweeps_kernel(
+    x_size, y_size, band_b, band_a, _levels, _given, _beta, filtered, levels, given, beta
 ):
-    rows = y_size + 2 * REACH
-    for x in range(x_size):
-        for slot, ref in enumerate((own, beside_a, beside_b)):
-            place, plane = slot_plane(x_size, slot, x)
-            s = ref[plane]
-            first[place, pl.ds(PAD + REACH, y_size), :] = s
-            given[place, pl.ds(REACH, y_size), :] = s * inverse[place]
-            beta[place, pl.ds(REACH, y_size), :] = own_beta[place]
     pieces, skip = diamond(x_size, REACH)
     radii = {(slot, k): (rows, skip + offset) for slot, k, rows, offset in diamond(x_size, REACH - 1)[0]}
     me, size = lax.axis_index("blk"), lax.axis_size("blk")
@@ -481,33 +518,23 @@
         for slot, k, count, offset in pieces:
             place, _ = slot_plane(x_size, slot, k)
             at = jnp.where(after, REACH + y_size, REACH - count)
-            s = ref[pl.ds(offset, count), :]
-            first[place, pl.ds(PAD + at, count), :] = s
+            levels[place, pl.ds(PAD + at, count), :] = ref[pl.ds(offset, count), :]
             if (slot, k) in radii:
-                count, offset = radii[slot, k]
-                at = jnp.where(after, REACH + y_size, REACH - count)
+                rows, base = radii[slot, k]
+                at = jnp.where(after, REACH + y_size, REACH - rows)
                 inside = jnp.logical_and(there, slot_inside(slot))
-                share, beta[place, pl.ds(at, count), :] = shares(ref[pl.ds(offset, count), :], inside)
-                given[place, pl.ds(at, count), :] = first[place, pl.ds(PAD + at, count), :] * share
-    source, target = first, second
+                first = offset + jnp.where(after, 0, count - rows)
+                share, beta[place, pl.ds(at, rows), :] = shares(ref[pl.ds(base, rows), :], inside)
+                given[place, pl.ds(at, rows), :] = ref[pl.ds(first, rows), :] * share
+
+    def put_out(x, row, value):
+        filtered[x - x_size, pl.ds(row, 8), :] = value
+
     for number in range(1, SWEEPS + 1):
-        final = number == SWEEPS
-        margin = SWEEPS - number
-
-        for j in range(1, 1 + y_size // 8) if final else range(rows // 8):
-            at = PAD + 8 * j
-            begin, end = x_size - margin, 2 * x_size + margin
-            column = {x: source[x, pl.ds(at, 8), :] for x in range(begin - 1, end + 1)}
-            for x in range(begin, end):
-                beside = column[x + 1] + column[x - 1]
-                beside = beside + source[x, pl.ds(at + 1, 8), :] + source[x, pl.ds(at - 1, 8), :]
-                beside = beside + lane_pull(column[x], 1) + lane_pull(column[x], -1)
-                value = given[x, pl.ds(8 * j, 8), :] + beta[x, pl.ds(8 * j, 8), :] * beside
-                if final:
-                    filtered[x - x_size, pl.ds(8 * j - REACH, 8), :] = value
-                else:
-                    target[x, pl.ds(at, 8), :] = value
-        source, target = target, source
+        source, _ = level_access(x_size, levels, number - 1)
+        put = level_access(x_size, levels, number)[1] if number < SWEEPS else put_out
+        for row in (number - SWEEPS, y_size - number):
+            sweep(x_size, number, row, source, given, beta, put)
 
 
 def call(kernel, outs, scratch, args, name, place=pltpu.VMEM, in_place=()):
@@ -535,6 +562,7 @@
 def on_device(dual_populace, forward_motion_vector, forward_heat_level, objective_heat_gradient, liquid_indicator,
               filter_span_group):
     _, x_size, y_size, lanes = dual_populace.shape
+    assert x_size >= REACH and y_size == 2 * REACH
     planes, pitch = x_size + 2, y_size + 2 * PAD
     sizes = (x_size, y_size)
     dual = dual_populace.reshape(POPS * x_size, y_size, lanes)
@@ -556,7 +584,7 @@
         pltpu.HBM,
     )
     rims = swapped("blk", *rims)
-    early = ((EDGES + x_size) * y_size, lanes)
+    early = (early_pieces(y_size)[1] + (REACH - 1) * y_size, lanes)
     near_far = [(len(LEVEL), pitch, lanes), (len(RIGHT), pitch, lanes)]
     earlies = call(
         functools.partial(early_kernel, *sizes),
@@ -592,26 +620,28 @@
         "steps_at_edges",
         in_place=((6, 0), (7, 1), (8, 2), (9, 3), (10, 4)),
     )
-    spans = [e.reshape(EDGES + x_size, y_size, lanes) for e in earlies]
+    spans = earlies
     beside = swapped("grp", sens, sens)
     (adjoint,) = call(
         functools.partial(adjoint_kernel, *sizes), [(POPS * x_size, y_size, lanes)], [], (state_2, coefs), "third_step"
     )
-    inverse, beta = call(
-        functools.partial(radius_kernel, *sizes), [(3 * x_size, y_size, lanes)] * 2, [], (span, *spans), "radius"
-    )
     band = (diamond(x_size, REACH)[1] + diamond(x_size, REACH - 1)[1], lanes)
     bands = call(
-        functools.partial(band_kernel, *sizes), [band, band], [], (sens, *beside, span, *spans), "bands"
+        functools.partial(band_kernel, *sizes), [band, band], [], (sens, *beside[::-1], span, *spans), "bands"
     )
     bands = swapped("blk", *bands)
     wide, rows = 3 * x_size, y_size + 2 * REACH
-    (filtered,) = call(
-        functools.partial(filter_kernel, *sizes),
-        [(x_size, y_size, lanes)],
-        [(wide, rows + 2 * PAD, lanes)] * 2 + [(wide, rows, lanes)] * 2,
-        (sens, *beside, *bands, inverse, beta),
-        "eight_sweeps",
+    smooth = [(SWEEPS * wide, rows + 2 * PAD, lanes), (wide, rows, lanes), (wide, rows, lanes)]
+    inner = call(
+        functools.partial(inner_sweeps_kernel, *sizes), smooth, [], (*beside, sens, span, *spans), "sweeps_inside"
+    )
+    filtered, *_ = call(
+        functools.partial(outer_sweeps_kernel, *sizes),
+        [own, *smooth],
+        [],
+        (*bands, *inner),
+        "sweeps_at_ends",
+        in_place=((2, 1), (3, 2), (4, 3)),
     )
     return adjoint.reshape(dual_populace.shape), filtered
 

time: 36.1 us -> 35.8 us (level)
  waiting for transfers between devices: 11.6 us -> 10.8 us
  Pallas kernels: 7.66 us -> 8.18 us
    ppermute x10, waiting for transfers between devices: 11.6 us -> 10.8 us  [swapped(): lax.ppermute(message, axis, pairs + [(j, i) for i, j in pairs])]
    pallas_call x9, Pallas kernels: 7.66 us -> 8.18 us  [call(): pl.pallas_call(kernel, out_shape=[jax.ShapeDtypeStruct(shape, jnp.float32...]
  transfers between devices with their start and end apart: 10 -> 10, of which waited for: 6 -> 6; matrix products, arithmetic and copies ran while one was open for 0% -> 0% of each run, Pallas kernels for 9% -> 11%
where the time goes in v9:
time: 35.8 us; the launch traced here: 35.6 us
  starting transfers between devices  15.8 us (44%)
  waiting for transfers between devices  10.8 us (30%)
  Pallas kernels  8.18 us (23%)
  between operations  0.76 us (2%)
    ppermute x10, starting transfers between devices, swapped(): lax.ppermute(message, axis, pairs + [(j, i) for i, j in pairs])  15.8 us
    ppermute x10, waiting for transfers between devices, swapped(): lax.ppermute(message, axis, pairs + [(j, i) for i, j in pairs])  10.8 us
    pallas_call x9, Pallas kernels, call(): pl.pallas_call(kernel, out_shape=[jax.ShapeDtypeStruct(shape, jnp.float32...  8.18 us
  transfers between devices with their start and end apart: 10, of which 6 were waited for; matrix products, arithmetic and copies ran while one was open for 0% of the time, Pallas kernels for 11%

profile of v9, /device:TPU:12, one launch (start us, length us, event | category | flops | bytes accessed | tf_op | source)
XLA Modules:
  0.0 35.6 jit_solution(9905412498934602597)
XLA Ops:
  0.6 1.8 %rim_rows.1 = (f32[384,128]{1,0:T(8,128)S(1)}, f32[384,128]{1,0:T(8,128)S(1)}, f32[190,32,128]{2,1,0:T(8,128)S(1)}, f32[48,32,128]{2,1,0:T(8,128)S(1)}, f32[8,16...) custom-call(f32[152,16,128]{2,1,0:T(8,128)} %bitcast.4, f32[24,16,128]{2,1,0:T(8,128)} %bitcast.5, f32[8,16,128]{2,1,0:T(8,128)} %refs_2_.1, ...), custom_call_target="tpu_custom_call" | custom-call | tf_op jit(solution)/shard_map/rim_rows/pallas_call | solution.py:541
  2.4 3.5 %collective-permute-start = (f32[384,128]{1,0:T(8,128)S(1)}, f32[384,128]{1,0:T(8,128)S(1)}, u32[]{:S(2)}, u32[]{:S(2)}) collective-permute-start(f32[384,128]{1,0:T(8,128)S(1)} %get-tuple-element.28), channel_id=1, source_target_pairs={{1,2},{2,1},{5,6},{6,5},{9,10},{10,9},{13,14},{14,13},{17,18},{18,... | collective-permute-start | bytes 589832 | tf_op jit(solution)/shard_map/ppermute | solution.py:558
  5.9 0.1 collective-permute-start.1
  6.0 0.3 edges_early.1
  6.3 2.5 %collective-permute-start.2 = (f32[386,128]{1,0:T(8,128)S(1)}, f32[386,128]{1,0:T(8,128)S(1)}, u32[]{:S(2)}, u32[]{:S(2)}) collective-permute-start(f32[386,128]{1,0:T(8,128)S(1)} %get-tuple-element.33), channel_id=1, source_target_pairs={{4,8},{12,16},{20,24},{8,4},{16,12},{24,20},{5,9},{13,17},{21,25},... | collective-permute-start | bytes 592904 | tf_op jit(solution)/shard_map/ppermute | solution.py:558
  8.8 1.1 %collective-permute-start.3 = (f32[386,128]{1,0:T(8,128)S(1)}, f32[386,128]{1,0:T(8,128)S(1)}, u32[]{:S(2)}, u32[]{:S(2)}) collective-permute-start(f32[386,128]{1,0:T(8,128)S(1)} %get-tuple-element.34), channel_id=1, source_target_pairs={{0,4},{8,12},{16,20},{24,28},{4,0},{12,8},{20,16},{28,24},{1,5},{9... | collective-permute-start | bytes 592904 | tf_op jit(solution)/shard_map/ppermute | solution.py:558
  9.9 1.1 %collective-permute-done.rim_b = f32[384,128]{1,0:T(8,128)S(1)} collective-permute-done((f32[384,128]{1,0:T(8,128)S(1)}, f32[384,128]{1,0:T(8,128)S(1)}, u32[]{:S(2)}, u32[]{:S(2)}) %collective-permute-start) | collective-permute-done | bytes 196640 | tf_op jit(solution)/shard_map/ppermute | solution.py:558
  11.0 1.4 %collective-permute-done.1.rim_a = f32[384,128]{1,0:T(8,128)S(1)} collective-permute-done((f32[384,128]{1,0:T(8,128)S(1)}, f32[384,128]{1,0:T(8,128)S(1)}, u32[]{:S(2)}, u32[]{:S(2)}) %collective-permute-start.1) | collective-permute-done | bytes 196640 | tf_op jit(solution)/shard_map/ppermute | solution.py:558
  12.4 0.6 %edges_late.1 = (f32[112,128]{1,0:T(8,128)S(1)}, f32[112,128]{1,0:T(8,128)S(1)}, f32[190,32,128]{2,1,0:T(8,128)S(1)}, f32[48,32,128]{2,1,0:T(8,128)S(1)}) custom-call(f32[190,32,128]{2,1,0:T(8,128)S(1)} %get-tuple-element.26._state.state, f32[48,32,128]{2,1,0:T(8,128)S(1)} %get-tuple-element.27._coef.coef, ...), custom_call_target="tpu_custom_call", output_to_operand_aliasing={{2}: (0, {}), {3}: (1, {})} | custom-call | tf_op jit(solution)/shard_map/edges_late/pallas_call | solution.py:541
  13.0 1.9 %collective-permute-start.4 = (f32[112,128]{1,0:T(8,128)S(1)}, f32[112,128]{1,0:T(8,128)S(1)}, u32[]{:S(2)}, u32[]{:S(2)}) collective-permute-start(f32[112,128]{1,0:T(8,128)S(1)} %get-tuple-element.35), channel_id=1, source_target_pairs={{4,8},{12,16},{20,24},{8,4},{16,12},{24,20},{5,9},{13,17},{21,25},... | collective-permute-start | bytes 172040 | tf_op jit(solution)/shard_map/ppermute | solution.py:558
  14.9 1.7 %collective-permute-start.5 = (f32[112,128]{1,0:T(8,128)S(1)}, f32[112,128]{1,0:T(8,128)S(1)}, u32[]{:S(2)}, u32[]{:S(2)}) collective-permute-start(f32[112,128]{1,0:T(8,128)S(1)} %get-tuple-element.36), channel_id=1, source_target_pairs={{0,4},{8,12},{16,20},{24,28},{4,0},{12,8},{20,16},{28,24},{1,5},{9... | collective-permute-start | bytes 172040 | tf_op jit(solution)/shard_map/ppermute | solution.py:558
  16.6 0.7 %steps_inside.1 = (f32[190,32,128]{2,1,0:T(8,128)S(1)}, f32[190,32,128]{2,1,0:T(8,128)S(1)}, f32[16,32,128]{2,1,0:T(8,128)S(1)}, f32[8,16,128]{2,1,0:T(8,128)S(1)}) custom-call(f32[190,32,128]{2,1,0:T(8,128)S(1)} %get-tuple-element.37.state._state, f32[48,32,128]{2,1,0:T(8,128)S(1)} %get-tuple-element.30.coef, f32[8,16,128]{2,1,0:T(8,128)S(1)} %get-tuple-element.31.heat), custom_call_target="tpu_custom_call" | custom-call | tf_op jit(solution)/shard_map/steps_inside/pallas_call | solution.py:541
  17.3 2.0 %collective-permute-done.4.late_b = f32[112,128]{1,0:T(8,128)S(1)} collective-permute-done((f32[112,128]{1,0:T(8,128)S(1)}, f32[112,128]{1,0:T(8,128)S(1)}, u32[]{:S(2)}, u32[]{:S(2)}) %collective-permute-start.4) | collective-permute-done | bytes 57376 | tf_op jit(solution)/shard_map/ppermute | solution.py:558
  19.4 0.8 %steps_at_edges.1 = (f32[190,32,128]{2,1,0:T(8,128)S(1)}, f32[190,32,128]{2,1,0:T(8,128)S(1)}, f32[190,32,128]{2,1,0:T(8,128)S(1)}, f32[16,32,128]{2,1,0:T(8,128)S(1)}, f32[8,16,128]{2,1,0:T(8,128)S(1)}) custom-call(f32[48,32,128]{2,1,0:T(8,128)S(1)} %get-tuple-element.30.coef, ...), custom_call_target="tpu_custom_call", output_to_operand_aliasing={{0}: (6, {}), {1}: (7, {}), {2}: (8, {}), {3}: (9, {}), {4}... | custom-call | tf_op jit(solution)/shard_map/steps_at_edges/pallas_call | solution.py:541
  20.2 1.9 %collective-permute-start.7 = (f32[8,16,128]{2,1,0:T(8,128)S(1)}, f32[8,16,128]{2,1,0:T(8,128)S(1)}, u32[]{:S(2)}, u32[]{:S(2)}) collective-permute-start(f32[8,16,128]{2,1,0:T(8,128)S(1)} %get-tuple-element.43.own), channel_id=1, source_target_pairs={{4,8},{12,16},{20,24},{8,4},{16,12},{24,20},{5,9},{13,17},{21,25},... | collective-permute-start | bytes 196616 | tf_op jit(solution)/shard_map/ppermute | solution.py:558
  22.1 0.8 %collective-permute-start.6 = (f32[8,16,128]{2,1,0:T(8,128)S(1)}, f32[8,16,128]{2,1,0:T(8,128)S(1)}, u32[]{:S(2)}, u32[]{:S(2)}) collective-permute-start(f32[8,16,128]{2,1,0:T(8,128)S(1)} %get-tuple-element.43.own), channel_id=1, source_target_pairs={{0,4},{8,12},{16,20},{24,28},{4,0},{12,8},{20,16},{28,24},{1,5},{9... | collective-permute-start | bytes 196616 | tf_op jit(solution)/shard_map/ppermute | solution.py:558
  22.9 3.8 %collective-permute-done.7.beside_b = f32[8,16,128]{2,1,0:T(8,128)S(1)} collective-permute-done((f32[8,16,128]{2,1,0:T(8,128)S(1)}, f32[8,16,128]{2,1,0:T(8,128)S(1)}, u32[]{:S(2)}, u32[]{:S(2)}) %collective-permute-start.7) | collective-permute-done | bytes 65568 | tf_op jit(solution)/shard_map/ppermute | solution.py:558
  26.7 2.4 %collective-permute-start.8 = (f32[224,128]{1,0:T(8,128)S(1)}, f32[224,128]{1,0:T(8,128)S(1)}, u32[]{:S(2)}, u32[]{:S(2)}) collective-permute-start(f32[224,128]{1,0:T(8,128)S(1)} %get-tuple-element.44), channel_id=1, source_target_pairs={{1,2},{2,1},{5,6},{6,5},{9,10},{10,9},{13,14},{14,13},{17,18},{18,... | collective-permute-start | bytes 344072 | tf_op jit(solution)/shard_map/ppermute | solution.py:558
  29.1 0.1 collective-permute-start.9
  29.2 1.4 %third_step.1 = f32[152,16,128]{2,1,0:T(8,128)} custom-call(f32[190,32,128]{2,1,0:T(8,128)S(1)} %get-tuple-element.42.state, f32[48,32,128]{2,1,0:T(8,128)S(1)} %get-tuple-element.30.coef), custom_call_target="tpu_custom_call" | custom-call | tf_op jit(solution)/shard_map/third_step/pallas_call | solution.py:541
  30.6 0.8 %sweeps_inside.1 = (f32[192,48,128]{2,1,0:T(8,128)S(1)}, f32[24,32,128]{2,1,0:T(8,128)S(1)}, f32[24,32,128]{2,1,0:T(8,128)S(1)}) custom-call(f32[8,16,128]{2,1,0:T(8,128)S(1)} %collective-permute-done.7.beside_b, f32[8,16,128]{2,1,0:T(8,128)S(1)} %collective-permute-done.6.beside_a, f32[8,16,128]{2,1,0:T(8,128)S(1)} %get-tuple-element.43.own, ...), custom_call_target="tpu_custom_call" | custom-call | tf_op jit(solution)/shard_map/sweeps_inside/pallas_call | solution.py:541
  31.4 2.0 %collective-permute-done.8.band_b = f32[224,128]{1,0:T(8,128)S(1)} collective-permute-done((f32[224,128]{1,0:T(8,128)S(1)}, f32[224,128]{1,0:T(8,128)S(1)}, u32[]{:S(2)}, u32[]{:S(2)}) %collective-permute-start.8) | collective-permute-done | bytes 114720 | tf_op jit(solution)/shard_map/ppermute | solution.py:558
  33.4 0.5 %collective-permute-done.9.band_a = f32[224,128]{1,0:T(8,128)S(1)} collective-permute-done((f32[224,128]{1,0:T(8,128)S(1)}, f32[224,128]{1,0:T(8,128)S(1)}, u32[]{:S(2)}, u32[]{:S(2)}) %collective-permute-start.9) | collective-permute-done | bytes 114720 | tf_op jit(solution)/shard_map/ppermute | solution.py:558
  34.0 1.6 %sweeps_at_ends.1 = (f32[8,16,128]{2,1,0:T(8,128)}, f32[192,48,128]{2,1,0:T(8,128)S(1)}, f32[24,32,128]{2,1,0:T(8,128)S(1)}, f32[24,32,128]{2,1,0:T(8,128)S(1)}) custom-call(f32[224,128]{1,0:T(8,128)S(1)} %collective-permute-done.8.band_b, f32[224,128]{1,0:T(8,128)S(1)} %collective-permute-done.9.band_a, ...), custom_call_target="tpu_custom_call", output_to_operand_aliasing={{1}: (2, {}), {2}: (3, {}), {3}: (4, {})} | custom-call | tf_op jit(solution)/shard_map/sweeps_at_ends/pallas_call | solution.py:541
  (5 shorter events, 0.1 us)
Async XLA Ops:
  2.4 8.5 %collective-permute-start = (f32[384,128]{1,0:T(8,128)S(1)}, f32[384,128]{1,0:T(8,128)S(1)}, u32[]{:S(2)}, u32[]{:S(2)}) collective-permute-start(f32[384,128]{1,0:T(8,128)S(1)} %get-tuple-element.28), channel_id=1, source_target_pairs={{1,2},{2,1},{5,6},{6,5},{9,10},{10,9},{13,14},{14,13},{17,18},{18,... | collective-permute-start | bytes 589832 | tf_op jit(solution)/shard_map/ppermute | solution.py:558
  5.9 6.4 %collective-permute-start.1 = (f32[384,128]{1,0:T(8,128)S(1)}, f32[384,128]{1,0:T(8,128)S(1)}, u32[]{:S(2)}, u32[]{:S(2)}) collective-permute-start(f32[384,128]{1,0:T(8,128)S(1)} %get-tuple-element.29), channel_id=1, source_target_pairs={{0,1},{2,3},{1,0},{3,2},{4,5},{6,7},{5,4},{7,6},{8,9},{10,11},{9,8... | collective-permute-start | bytes 589832 | tf_op jit(solution)/shard_map/ppermute | solution.py:558
  6.3 11.0 %collective-permute-start.2 = (f32[386,128]{1,0:T(8,128)S(1)}, f32[386,128]{1,0:T(8,128)S(1)}, u32[]{:S(2)}, u32[]{:S(2)}) collective-permute-start(f32[386,128]{1,0:T(8,128)S(1)} %get-tuple-element.33), channel_id=1, source_target_pairs={{4,8},{12,16},{20,24},{8,4},{16,12},{24,20},{5,9},{13,17},{21,25},... | collective-permute-start | bytes 592904 | tf_op jit(solution)/shard_map/ppermute | solution.py:558
  8.8 8.5 %collective-permute-start.3 = (f32[386,128]{1,0:T(8,128)S(1)}, f32[386,128]{1,0:T(8,128)S(1)}, u32[]{:S(2)}, u32[]{:S(2)}) collective-permute-start(f32[386,128]{1,0:T(8,128)S(1)} %get-tuple-element.34), channel_id=1, source_target_pairs={{0,4},{8,12},{16,20},{24,28},{4,0},{12,8},{20,16},{28,24},{1,5},{9... | collective-permute-start | bytes 592904 | tf_op jit(solution)/shard_map/ppermute | solution.py:558
  13.0 6.4 %collective-permute-start.4 = (f32[112,128]{1,0:T(8,128)S(1)}, f32[112,128]{1,0:T(8,128)S(1)}, u32[]{:S(2)}, u32[]{:S(2)}) collective-permute-start(f32[112,128]{1,0:T(8,128)S(1)} %get-tuple-element.35), channel_id=1, source_target_pairs={{4,8},{12,16},{20,24},{8,4},{16,12},{24,20},{5,9},{13,17},{21,25},... | collective-permute-start | bytes 172040 | tf_op jit(solution)/shard_map/ppermute | solution.py:558
  14.9 4.5 %collective-permute-start.5 = (f32[112,128]{1,0:T(8,128)S(1)}, f32[112,128]{1,0:T(8,128)S(1)}, u32[]{:S(2)}, u32[]{:S(2)}) collective-permute-start(f32[112,128]{1,0:T(8,128)S(1)} %get-tuple-element.36), channel_id=1, source_target_pairs={{0,4},{8,12},{16,20},{24,28},{4,0},{12,8},{20,16},{28,24},{1,5},{9... | collective-permute-start | bytes 172040 | tf_op jit(solution)/shard_map/ppermute | solution.py:558
  20.2 6.5 %collective-permute-start.7 = (f32[8,16,128]{2,1,0:T(8,128)S(1)}, f32[8,16,128]{2,1,0:T(8,128)S(1)}, u32[]{:S(2)}, u32[]{:S(2)}) collective-permute-start(f32[8,16,128]{2,1,0:T(8,128)S(1)} %get-tuple-element.43.own), channel_id=1, source_target_pairs={{4,8},{12,16},{20,24},{8,4},{16,12},{24,20},{5,9},{13,17},{21,25},... | collective-permute-start | bytes 196616 | tf_op jit(solution)/shard_map/ppermute | solution.py:558
  22.1 4.6 %collective-permute-start.6 = (f32[8,16,128]{2,1,0:T(8,128)S(1)}, f32[8,16,128]{2,1,0:T(8,128)S(1)}, u32[]{:S(2)}, u32[]{:S(2)}) collective-permute-start(f32[8,16,128]{2,1,0:T(8,128)S(1)} %get-tuple-element.43.own), channel_id=1, source_target_pairs={{0,4},{8,12},{16,20},{24,28},{4,0},{12,8},{20,16},{28,24},{1,5},{9... | collective-permute-start | bytes 196616 | tf_op jit(solution)/shard_map/ppermute | solution.py:558
  26.7 6.7 %collective-permute-start.8 = (f32[224,128]{1,0:T(8,128)S(1)}, f32[224,128]{1,0:T(8,128)S(1)}, u32[]{:S(2)}, u32[]{:S(2)}) collective-permute-start(f32[224,128]{1,0:T(8,128)S(1)} %get-tuple-element.44), channel_id=1, source_target_pairs={{1,2},{2,1},{5,6},{6,5},{9,10},{10,9},{13,14},{14,13},{17,18},{18,... | collective-permute-start | bytes 344072 | tf_op jit(solution)/shard_map/ppermute | solution.py:558
  29.1 4.9 %collective-permute-start.9 = (f32[224,128]{1,0:T(8,128)S(1)}, f32[224,128]{1,0:T(8,128)S(1)}, u32[]{:S(2)}, u32[]{:S(2)}) collective-permute-start(f32[224,128]{1,0:T(8,128)S(1)} %get-tuple-element.45), channel_id=1, source_target_pairs={{0,1},{2,3},{1,0},{3,2},{4,5},{6,7},{5,4},{7,6},{8,9},{10,11},{9,8... | collective-permute-start | bytes 344072 | tf_op jit(solution)/shard_map/ppermute | solution.py:558
